TPU v7x, 512 devices: a whole 4x8x8 slice. The times are simulated.
512 devices in a mesh: member: 8 (over z), space: 64 (over y, x, core).
Axes of the slice: x: 4, y: 8, z: 8, core: 2. Of those that a mesh axis runs over, the one named last changes fastest.
Arguments:
- ensemble: float32 [512, 256, 1024], P('member', 'space'), may hold values from -6 to 6
- speed_row: float32 [256, 1024], P('space'), may hold values from -0.3 to 0.3
- speed_col: float32 [256, 1024], P('space'), may hold values from -0.3 to 0.3
- obs_cell: int32 [64, 8, 1, 2, 128], P('space', 'member'), may hold values from 0 to 511
- obs_value: float32 [64, 8, 1, 2, 128], P('space', 'member'), may hold values from -6 to 6
- obs_var: float32 [64, 8, 1, 2, 128], P('space', 'member'), may hold values from 0.5 to 4
- obs_count: int32 [64, 8, 1, 2], P('space', 'member'), may hold values from 0 to 128
- loc_slots: int32 [64, 8, 1, 12], P('space', 'member'), may hold values from 0 to 17, as said below
Outputs:
- analysis_ensemble: float32 [512, 256, 1024], P('member', 'space')
Inputs may be any that keep to these rules, and one draw needn't show every extreme that they name: `loc_slots`: each patch and cycle lists 12 different neighbour slots. `obs_cell`: a cell of the tile's own patch, counted row by row. `obs_count`: the live observations of a tile are its first ones.
All inputs are finite; a program needn't handle non-finite values.
Results may differ from a plain program's by a relative error of at most 0.0003.
Values sent between devices are 32-bit elements; how exact they have to be, the bound alone decides.
No kernel may reach another device: no remote copies, remote signals or barrier semaphores. Data moves between devices by JAX's collectives and lax.ppermute only.
A program may use at most 64 MiB of HBM per device.

v0:
```python
import functools

import jax
import jax.numpy as jnp
from jax import lax
from jax.experimental import pallas as pl
from jax.experimental.pallas import tpu as pltpu
from jax.sharding import PartitionSpec as P

K = 0.2
HI = lax.Precision.HIGHEST
SUB = 8
NT = (((1,), (1,)), ((), ()))


def split3(x):
    a = x.astype(jnp.bfloat16)
    rest = x - a.astype(jnp.float32)
    b = rest.astype(jnp.bfloat16)
    c = (rest - b.astype(jnp.float32)).astype(jnp.bfloat16)
    return a, b, c


def eye(n):
    rows = lax.broadcasted_iota(jnp.int32, (n, n), 0)
    cols = lax.broadcasted_iota(jnp.int32, (n, n), 1)
    return jnp.where(rows == cols, 1.0, 0.0).astype(jnp.float32)


def advect_kernel(planes, before, after, speed_row, speed_col, out, coef):
    rows, members, width = planes.shape
    blocks = out.shape[0]
    cols = out.shape[3]
    groups = members // SUB
    top, bottom = before[2 * groups], after[2 * groups]
    for r in range(rows + 2):
        if r == 0:
            u, v = top[0:1], top[1:2]
        elif r == rows + 1:
            u, v = bottom[0:1], bottom[1:2]
        else:
            u, v = speed_row[r - 1 : r], speed_col[r - 1 : r]
        for n, c in enumerate((K + 0.5 * u, K - 0.5 * u, K + 0.5 * v, K - 0.5 * v)):
            coef[r, n] = jnp.broadcast_to(c, (SUB, width))

    def step(field, first):
        new = []
        for n in range(1, len(field) - 1):
            r = first + n - 1
            x = field[n]
            new.append(
                (1.0 - 4.0 * K) * x
                + coef[r, 0] * field[n - 1]
                + coef[r, 1] * field[n + 1]
                + coef[r, 2] * pltpu.roll(x, 1, 1)
                + coef[r, 3] * pltpu.roll(x, width - 1, 1)
            )
        return new

    def body(g, carry):
        at = pl.ds(pl.multiple_of(g * SUB, SUB), SUB)
        field = [before[g], before[groups + g]]
        field += [planes[i, at, :] for i in range(rows)]
        field += [after[g], after[groups + g]]
        field = step(step(field, 0), 1)
        for i in range(rows):
            for b in range(blocks):
                out[b, i, at, :] = field[i][:, b * cols : (b + 1) * cols]
        return carry

    lax.fori_loop(0, groups, body, 0)


def patch_matrix(state):
    parts, rows, members, cols = state.shape
    return jnp.concatenate(
        [state[:, i].reshape(parts * members, cols) for i in range(rows)], axis=1
    )


def tile_kernel(count, state, cell, value, variance, tiles, centre):
    parts, rows, members, cols = state.shape
    total = parts * members
    cells = rows * cols
    per_patch, obs = cell.shape
    x = patch_matrix(state)
    mean = jnp.sum(x, axis=0, keepdims=True) * (1.0 / total)
    for i in range(rows):
        centre[i : i + 1, :] = mean[:, i * cols : (i + 1) * cols]
    anomaly = jnp.concatenate([x - mean, jnp.broadcast_to(mean, (SUB, cells))], axis=0)
    parts3 = split3(anomaly)
    row = lax.broadcasted_iota(jnp.int32, (cells, obs), 0)
    lane = lax.broadcasted_iota(jnp.int32, (1, obs), 1)
    below = lax.broadcasted_iota(jnp.int32, (SUB, obs), 0)
    for t in range(per_patch):
        pick = jnp.where(row == cell[t : t + 1, :], 1.0, 0.0).astype(jnp.bfloat16)
        y = sum(jnp.dot(p, pick, preferred_element_type=jnp.float32) for p in parts3[::-1])
        live = lane < count[t]
        weight = jnp.where(live, 1.0 / variance[t : t + 1, :], 0.0)
        scale = jnp.sqrt(weight * (1.0 / (total - 1.0)))
        tiles[t, 0:total, :] = y[:total] * scale
        innovation = (value[t : t + 1, :] - y[total:]) * scale
        tiles[t, total : total + SUB, :] = jnp.where(below == 0, innovation, 0.0)


def spd_inverse(s):
    n = s.shape[0]
    unit = eye(n)
    size = jnp.sum(s * s)
    bound = jnp.minimum(jnp.sqrt(size), jnp.max(jnp.sum(jnp.abs(s), axis=0)))
    bound = jnp.maximum(bound, 1.0) * 1.0001
    scale = 2.0 / (1.0 + bound)
    x = scale * unit
    e = unit - scale * s
    rho = (bound - 1.0) / (bound + 1.0)

    def more(carry):
        return carry[2] > 1e-3

    def square(carry):
        x, e, rho = carry
        both = jnp.dot(jnp.concatenate([x, e], axis=0), e, precision=HI)
        square_rho = rho * rho
        scale = 2.0 / (2.0 - square_rho)
        x = scale * (x + both[:n])
        e = scale * both[n:] + (1.0 - scale) * unit
        return x, e, square_rho / (2.0 - square_rho)

    x, e, rho = lax.while_loop(more, square, (x, e, rho))
    for _ in range(2):
        e = unit - jnp.dot(s, x, precision=HI)
        x = x + jnp.dot(x, e, precision=HI)
    return x


def update_kernel(per_patch, slots, state, centre, *refs):
    near = refs[:9]
    out, z, inv = refs[9:]
    parts, rows, members, cols = state.shape
    total = parts * members
    half = total // 2
    mask = jnp.int32(0)
    for n in range(slots.shape[0]):
        mask = mask | lax.shift_left(jnp.int32(1), slots[n])
    place = jnp.int32(0)
    for q in range(9 * per_patch):
        o, t = q // per_patch, q % per_patch
        r, s = o // 3 - 1, o % 3 - 1
        taper = 1.0 / (1.0 + r * r + s * s)
        chosen = lax.shift_right_logical(mask, q) & 1

        @pl.when(chosen == 1)
        def _():
            obs = near[o].shape[2]
            z[:, pl.ds(pl.multiple_of(place * obs, obs), obs)] = near[o][t] * (taper**0.5)

        place = place + chosen
    gram = lax.dot_general(z[...], z[0:total, :], NT, precision=HI)
    drive = gram[total : total + SUB]
    s11 = gram[:half, :half] + eye(half)
    s12 = gram[:half, half:]
    s22 = gram[half:total, half:] + eye(half)
    inv11 = spd_inverse(s11)
    w = jnp.dot(inv11, s12, precision=HI)
    schur = s22 - lax.dot_general(s12, w, (((0,), (0,)), ((), ())), precision=HI)
    inv22 = spd_inverse(0.5 * (schur + schur.T))
    low = jnp.dot(w, inv22, precision=HI)
    inv[0:half, 0:half] = inv11 + lax.dot_general(low, w, NT, precision=HI)
    inv[0:half, half:] = -low
    inv[half:, 0:half] = -low.T
    inv[half:, half:] = inv22
    shift = jnp.dot(drive, inv[...], precision=HI)[0:1]
    mean = jnp.concatenate([centre[i : i + 1, :] for i in range(rows)], axis=1)
    anomaly = patch_matrix(state) - mean
    result = jnp.dot(0.5 * inv[...] + shift, anomaly, precision=HI)
    result = result + (mean + 0.5 * anomaly)
    for p in range(parts):
        for i in range(rows):
            out[p, i] = result[p * members : (p + 1) * members, i * cols : (i + 1) * cols]


VMEM = pl.BlockSpec(memory_space=pltpu.VMEM)
SMEM = pl.BlockSpec(memory_space=pltpu.SMEM)
PARAMS = pltpu.CompilerParams(vmem_limit_bytes=48 * 1024 * 1024)


def f32(*shape):
    return jax.ShapeDtypeStruct(shape, jnp.float32)


def shifted(x, axis, by):
    n = lax.axis_size(axis)
    return lax.ppermute(x, axis, [(i, (i + by) % n) for i in range(n)])


def swap(x):
    return lax.all_to_all(x, "member", split_axis=0, concat_axis=0, tiled=True)


def on_device(ensemble, speed_row, speed_col, obs_cell, obs_value, obs_var, obs_count, loc_slots):
    members, rows, width = ensemble.shape
    parts = lax.axis_size("member")
    cols = width // parts
    groups = members // SUB
    per_patch, obs = obs_cell.shape[3:]
    total = parts * members

    planes = ensemble.transpose(1, 0, 2)

    def edge(first, row):
        speeds = jnp.concatenate(
            [speed_row[row : row + 1], speed_col[row : row + 1], jnp.zeros((SUB - 2, width), jnp.float32)]
        )
        body = planes[first : first + 2].reshape(2 * groups, SUB, width)
        return jnp.concatenate([body, speeds[None]])

    before = shifted(edge(rows - 2, rows - 1), "space", 1)
    after = shifted(edge(0, 0), "space", -1)
    state = pl.pallas_call(
        advect_kernel,
        out_shape=f32(parts, rows, members, cols),
        in_specs=[VMEM] * 5,
        out_specs=VMEM,
        scratch_shapes=[pltpu.VMEM((rows + 2, 4, SUB, width), jnp.float32)],
        compiler_params=PARAMS,
        name="advect",
    )(planes, before, after, speed_row, speed_col)
    state = swap(state)
    tiles, centre = pl.pallas_call(
        tile_kernel,
        out_shape=(f32(per_patch, total + SUB, obs), f32(rows, cols)),
        in_specs=[SMEM] + [VMEM] * 4,
        out_specs=(VMEM, VMEM),
        compiler_params=PARAMS,
        name="tiles",
    )(obs_count[0, 0, 0], state, obs_cell[0, 0, 0], obs_value[0, 0, 0], obs_var[0, 0, 0])
    left = shifted(tiles, "member", 1)
    right = shifted(tiles, "member", -1)
    line = (left, tiles, right)
    near = [shifted(x, "space", 1) for x in line] + list(line) + [shifted(x, "space", -1) for x in line]
    slots = loc_slots[0, 0, 0]
    state = pl.pallas_call(
        functools.partial(update_kernel, per_patch),
        out_shape=f32(parts, rows, members, cols),
        in_specs=[SMEM] + [VMEM] * 11,
        out_specs=VMEM,
        scratch_shapes=[
            pltpu.VMEM((total + SUB, slots.shape[0] * obs), jnp.float32),
            pltpu.VMEM((total, total), jnp.float32),
        ],
        compiler_params=PARAMS,
        name="update",
    )(slots, state, centre, *near)
    state = swap(state)
    return state.transpose(2, 1, 0, 3).reshape(members, rows, width)


def solution(mesh):
    return jax.shard_map(
        on_device,
        mesh=mesh,
        in_specs=(
            P("member", "space", None),
            P("space", None),
            P("space", None),
            P("space", "member", None, None, None),
            P("space", "member", None, None, None),
            P("space", "member", None, None, None),
            P("space", "member", None, None),
            P("space", "member", None, None),
        ),
        out_specs=P("member", "space", None),
        check_vma=False,
    )
```

profile of v0, /device:TPU:63, one launch (start us, length us, event | category | flops | bytes accessed | tf_op | source)
XLA Modules:
  0.0 152.5 jit_solution(2961772819590364883)
XLA Ops:
  0.0 1.8 %copy.16 = f32[64,4,1024]{2,0,1:T(8,128)S(1)} copy(f32[64,4,1024]{2,1,0:T(4,128)} %param.8) | data formatting | bytes 2097152 | tf_op args[0]
  2.7 7.2 %collective-permute-start = (f32[17,8,1024]{2,1,0:T(8,128)S(1)}, f32[17,8,1024]{2,1,0:T(8,128)S(1)}, u32[]{:S(2)}, u32[]{:S(2)}) collective-permute-start(f32[17,8,1024]{2,1,0:T(8,128)S(1)} %pad_maximum_fusion), channel_id=1, source_target_pairs={{0,1},{1,2},{2,3},{3,4},{4,5},{5,6},{6,7},{7,8},{8,9},{9,10},{10,1... | collective-permute-start | bytes 1671176 | tf_op jit(solution)/shard_map/ppermute | solution.py:193
  10.0 1.9 %collective-permute-start.1 = (f32[17,8,1024]{2,1,0:T(8,128)S(1)}, f32[17,8,1024]{2,1,0:T(8,128)S(1)}, u32[]{:S(2)}, u32[]{:S(2)}) collective-permute-start(f32[17,8,1024]{2,1,0:T(8,128)S(1)} %pad_maximum_fusion.1), channel_id=1, source_target_pairs={{0,63},{1,0},{2,1},{3,2},{4,3},{5,4},{6,5},{7,6},{8,7},{9,8},{10,9... | collective-permute-start | bytes 1671176 | tf_op jit(solution)/shard_map/ppermute | solution.py:193
  11.9 4.5 %collective-permute-done.before = f32[17,8,1024]{2,1,0:T(8,128)S(1)} collective-permute-done((f32[17,8,1024]{2,1,0:T(8,128)S(1)}, f32[17,8,1024]{2,1,0:T(8,128)S(1)}, u32[]{:S(2)}, u32[]{:S(2)}) %collective-permute-start) | collective-permute-done | bytes 557088 | tf_op jit(solution)/shard_map/ppermute | solution.py:193
  16.4 7.8 %collective-permute-done.1.after = f32[17,8,1024]{2,1,0:T(8,128)S(1)} collective-permute-done((f32[17,8,1024]{2,1,0:T(8,128)S(1)}, f32[17,8,1024]{2,1,0:T(8,128)S(1)}, u32[]{:S(2)}, u32[]{:S(2)}) %collective-permute-start.1) | collective-permute-done | bytes 557088 | tf_op jit(solution)/shard_map/ppermute | solution.py:193
  24.2 2.1 %advect.1 = f32[8,4,64,128]{3,2,1,0:T(8,128)S(1)} custom-call(f32[4,64,1024]{2,1,0:T(8,128)S(1)} %bitcast.18, f32[17,8,1024]{2,1,0:T(8,128)S(1)} %collective-permute-done.before, f32[17,8,1024]{2,1,0:T(8,128)S(1)} %collective-permute-done.1.after, f32[4,1024]{1,0:T(4,128)S(1)} %copy-done.1, f32[4,1024]{1,0:T(4,128)S(1)} %copy-done.2), custom_call_target="tpu_custom_call" | custom-call | tf_op jit(solution)/shard_map/advect/pallas_call | solution.py:219
  26.3 31.4 %all_to_all.10.state = f32[8,4,64,128]{3,2,1,0:T(8,128)S(1)} all-to-all(f32[8,4,64,128]{3,2,1,0:T(8,128)S(1)} %advect.1), channel_id=1, replica_groups=mesh['member'=8,'space'=64] {'member'}, dimensions={0} | all-to-all | bytes 2097152 | tf_op jit(solution)/shard_map/all_to_all | solution.py:197
  57.7 0.7 copy-done.3
  58.4 1.6 %tiles.1 = (f32[2,520,128]{2,1,0:T(8,128)S(1)}, f32[4,128]{1,0:T(4,128)S(1)}) custom-call(s32[2]{0:T(128)S(1)} %bitcast.22, f32[8,4,64,128]{3,2,1,0:T(8,128)S(1)} %all_to_all.10.state, s32[2,128]{1,0:T(2,128)S(1)} %bitcast.19, f32[2,128]{1,0:T(2,128)S(1)} %bitcast.20, f32[2,128]{1,0:T(2,128)S(1)} %bitcast.21), custom_call_target="tpu_custom_call" | custom-call | tf_op jit(solution)/shard_map/tiles/pallas_call | solution.py:229
  60.1 1.9 %collective-permute-start.5 = (f32[2,520,128]{2,1,0:T(8,128)S(1)}, f32[2,520,128]{2,1,0:T(8,128)S(1)}, u32[]{:S(2)}, u32[]{:S(2)}) collective-permute-start(f32[2,520,128]{2,1,0:T(8,128)S(1)} %get-tuple-element.8.refs_4_), channel_id=1, source_target_pairs={{0,448},{64,0},{128,64},{192,128},{256,192},{320,256},{384,320},{4... | collective-permute-start | bytes 1597448 | tf_op jit(solution)/shard_map/ppermute | solution.py:193
  62.0 3.4 %collective-permute-start.2 = (f32[2,520,128]{2,1,0:T(8,128)S(1)}, f32[2,520,128]{2,1,0:T(8,128)S(1)}, u32[]{:S(2)}, u32[]{:S(2)}) collective-permute-start(f32[2,520,128]{2,1,0:T(8,128)S(1)} %get-tuple-element.8.refs_4_), channel_id=1, source_target_pairs={{0,64},{64,128},{128,192},{192,256},{256,320},{320,384},{384,448},... | collective-permute-start | bytes 1597448 | tf_op jit(solution)/shard_map/ppermute | solution.py:193
  65.4 1.9 %collective-permute-start.8 = (f32[2,520,128]{2,1,0:T(8,128)S(1)}, f32[2,520,128]{2,1,0:T(8,128)S(1)}, u32[]{:S(2)}, u32[]{:S(2)}) collective-permute-start(f32[2,520,128]{2,1,0:T(8,128)S(1)} %get-tuple-element.8.refs_4_), channel_id=1, source_target_pairs={{0,63},{1,0},{2,1},{3,2},{4,3},{5,4},{6,5},{7,6},{8,7},{9,8},{10,9... | collective-permute-start | bytes 1597448 | tf_op jit(solution)/shard_map/ppermute | solution.py:193
  67.3 7.0 %collective-permute-start.4 = (f32[2,520,128]{2,1,0:T(8,128)S(1)}, f32[2,520,128]{2,1,0:T(8,128)S(1)}, u32[]{:S(2)}, u32[]{:S(2)}) collective-permute-start(f32[2,520,128]{2,1,0:T(8,128)S(1)} %get-tuple-element.8.refs_4_), channel_id=1, source_target_pairs={{0,1},{1,2},{2,3},{3,4},{4,5},{5,6},{6,7},{7,8},{8,9},{9,10},{10,1... | collective-permute-start | bytes 1597448 | tf_op jit(solution)/shard_map/ppermute | solution.py:193
  74.6 1.9 %collective-permute-start.9 = (f32[2,520,128]{2,1,0:T(8,128)S(1)}, f32[2,520,128]{2,1,0:T(8,128)S(1)}, u32[]{:S(2)}, u32[]{:S(2)}) collective-permute-start(f32[2,520,128]{2,1,0:T(8,128)S(1)} %collective-permute-done.5.refs_5_), channel_id=1, source_target_pairs={{0,63},{1,0},{2,1},{3,2},{4,3},{5,4},{6,5},{7,6},{8,7},{9,8},{10,9... | collective-permute-start | bytes 1597448 | tf_op jit(solution)/shard_map/ppermute | solution.py:193
  76.5 7.0 %collective-permute-start.6 = (f32[2,520,128]{2,1,0:T(8,128)S(1)}, f32[2,520,128]{2,1,0:T(8,128)S(1)}, u32[]{:S(2)}, u32[]{:S(2)}) collective-permute-start(f32[2,520,128]{2,1,0:T(8,128)S(1)} %collective-permute-done.5.refs_5_), channel_id=1, source_target_pairs={{0,1},{1,2},{2,3},{3,4},{4,5},{5,6},{6,7},{7,8},{8,9},{9,10},{10,1... | collective-permute-start | bytes 1597448 | tf_op jit(solution)/shard_map/ppermute | solution.py:193
  83.5 1.9 %collective-permute-start.7 = (f32[2,520,128]{2,1,0:T(8,128)S(1)}, f32[2,520,128]{2,1,0:T(8,128)S(1)}, u32[]{:S(2)}, u32[]{:S(2)}) collective-permute-start(f32[2,520,128]{2,1,0:T(8,128)S(1)} %collective-permute-done.2.refs_3_), channel_id=1, source_target_pairs={{0,63},{1,0},{2,1},{3,2},{4,3},{5,4},{6,5},{7,6},{8,7},{9,8},{10,9... | collective-permute-start | bytes 1597448 | tf_op jit(solution)/shard_map/ppermute | solution.py:193
  85.4 7.0 %collective-permute-start.3 = (f32[2,520,128]{2,1,0:T(8,128)S(1)}, f32[2,520,128]{2,1,0:T(8,128)S(1)}, u32[]{:S(2)}, u32[]{:S(2)}) collective-permute-start(f32[2,520,128]{2,1,0:T(8,128)S(1)} %collective-permute-done.2.refs_3_), channel_id=1, source_target_pairs={{0,1},{1,2},{2,3},{3,4},{4,5},{5,6},{6,7},{7,8},{8,9},{9,10},{10,1... | collective-permute-start | bytes 1597448 | tf_op jit(solution)/shard_map/ppermute | solution.py:193
  92.4 5.0 %collective-permute-done.7.refs_6_ = f32[2,520,128]{2,1,0:T(8,128)S(1)} collective-permute-done((f32[2,520,128]{2,1,0:T(8,128)S(1)}, f32[2,520,128]{2,1,0:T(8,128)S(1)}, u32[]{:S(2)}, u32[]{:S(2)}) %collective-permute-start.7) | collective-permute-done | bytes 532512 | tf_op jit(solution)/shard_map/ppermute | solution.py:193
  97.4 1.2 collective-permute-done.3.refs_0_
  98.6 0.7 copy-done.7
  99.2 22.8 %update.1 = f32[8,4,64,128]{3,2,1,0:T(8,128)S(1)} custom-call(s32[12]{0:T(128)S(1)} %bitcast.23, f32[8,4,64,128]{3,2,1,0:T(8,128)} %copy-done, f32[4,128]{1,0:T(4,128)S(1)} %get-tuple-element.7.centre, f32[2,520,128]{2,1,0:T(8,128)S(1)} %collective-permute-done.3.refs_0_, f32[2,520,128]{2,1,0:T(8,128)S(1)} %collective-permute-done.4.refs_1_, ...), custom_call_target="tpu_custom_call" | custom-call | tf_op jit(solution)/shard_map/update/pallas_call | solution.py:242
  122.0 28.5 %all_to_all.11 = f32[8,4,64,128]{3,2,1,0:T(8,128)S(1)} all-to-all(f32[8,4,64,128]{3,2,1,0:T(8,128)S(1)} %update.1), channel_id=1, replica_groups=mesh['member'=8,'space'=64] {'member'}, dimensions={0} | all-to-all | bytes 2097152 | tf_op jit(solution)/shard_map/all_to_all | solution.py:197
  150.5 0.6 copy.13
  151.1 1.3 reshape.12
  (27 shorter events, 1.2 us)
Async XLA Ops:
  1.8 0.7 copy-start.1
  1.9 0.7 copy-start.2
  2.7 13.7 %collective-permute-start = (f32[17,8,1024]{2,1,0:T(8,128)S(1)}, f32[17,8,1024]{2,1,0:T(8,128)S(1)}, u32[]{:S(2)}, u32[]{:S(2)}) collective-permute-start(f32[17,8,1024]{2,1,0:T(8,128)S(1)} %pad_maximum_fusion), channel_id=1, source_target_pairs={{0,1},{1,2},{2,3},{3,4},{4,5},{5,6},{6,7},{7,8},{8,9},{9,10},{10,1... | collective-permute-start | bytes 1671176 | tf_op jit(solution)/shard_map/ppermute | solution.py:193
  10.0 14.2 %collective-permute-start.1 = (f32[17,8,1024]{2,1,0:T(8,128)S(1)}, f32[17,8,1024]{2,1,0:T(8,128)S(1)}, u32[]{:S(2)}, u32[]{:S(2)}) collective-permute-start(f32[17,8,1024]{2,1,0:T(8,128)S(1)} %pad_maximum_fusion.1), channel_id=1, source_target_pairs={{0,63},{1,0},{2,1},{3,2},{4,3},{5,4},{6,5},{7,6},{8,7},{9,8},{10,9... | collective-permute-start | bytes 1671176 | tf_op jit(solution)/shard_map/ppermute | solution.py:193
  26.3 31.5 %copy-start.4 = (f32[1,1,1,2,128]{4,3,2,1,0:T(2,128)S(1)}, f32[1,1,1,2,128]{4,3,2,1,0:T(2,128)}, u32[]{:S(2)}) copy-start(f32[1,1,1,2,128]{4,3,2,1,0:T(2,128)} %param.12) | copy-start | bytes 3076
  26.3 31.5 %copy-start.5 = (f32[1,1,1,2,128]{4,3,2,1,0:T(2,128)S(1)}, f32[1,1,1,2,128]{4,3,2,1,0:T(2,128)}, u32[]{:S(2)}) copy-start(f32[1,1,1,2,128]{4,3,2,1,0:T(2,128)} %param.13) | copy-start | bytes 3076
  57.7 40.9 %copy-start = (f32[8,4,64,128]{3,2,1,0:T(8,128)}, f32[8,4,64,128]{3,2,1,0:T(8,128)S(1)}, u32[]{:S(2)}) copy-start(f32[8,4,64,128]{3,2,1,0:T(8,128)S(1)} %all_to_all.10.state) | copy-start | bytes 3145732
  57.7 0.7 copy-start.3
  57.7 0.7 copy-start.6
  60.1 14.5 %collective-permute-start.5 = (f32[2,520,128]{2,1,0:T(8,128)S(1)}, f32[2,520,128]{2,1,0:T(8,128)S(1)}, u32[]{:S(2)}, u32[]{:S(2)}) collective-permute-start(f32[2,520,128]{2,1,0:T(8,128)S(1)} %get-tuple-element.8.refs_4_), channel_id=1, source_target_pairs={{0,448},{64,0},{128,64},{192,128},{256,192},{320,256},{384,320},{4... | collective-permute-start | bytes 1597448 | tf_op jit(solution)/shard_map/ppermute | solution.py:193
  62.0 21.4 %collective-permute-start.2 = (f32[2,520,128]{2,1,0:T(8,128)S(1)}, f32[2,520,128]{2,1,0:T(8,128)S(1)}, u32[]{:S(2)}, u32[]{:S(2)}) collective-permute-start(f32[2,520,128]{2,1,0:T(8,128)S(1)} %get-tuple-element.8.refs_4_), channel_id=1, source_target_pairs={{0,64},{64,128},{128,192},{192,256},{256,320},{320,384},{384,448},... | collective-permute-start | bytes 1597448 | tf_op jit(solution)/shard_map/ppermute | solution.py:193
  65.4 20.0 %collective-permute-start.8 = (f32[2,520,128]{2,1,0:T(8,128)S(1)}, f32[2,520,128]{2,1,0:T(8,128)S(1)}, u32[]{:S(2)}, u32[]{:S(2)}) collective-permute-start(f32[2,520,128]{2,1,0:T(8,128)S(1)} %get-tuple-element.8.refs_4_), channel_id=1, source_target_pairs={{0,63},{1,0},{2,1},{3,2},{4,3},{5,4},{6,5},{7,6},{8,7},{9,8},{10,9... | collective-permute-start | bytes 1597448 | tf_op jit(solution)/shard_map/ppermute | solution.py:193
  67.3 25.1 %collective-permute-start.4 = (f32[2,520,128]{2,1,0:T(8,128)S(1)}, f32[2,520,128]{2,1,0:T(8,128)S(1)}, u32[]{:S(2)}, u32[]{:S(2)}) collective-permute-start(f32[2,520,128]{2,1,0:T(8,128)S(1)} %get-tuple-element.8.refs_4_), channel_id=1, source_target_pairs={{0,1},{1,2},{2,3},{3,4},{4,5},{5,6},{6,7},{7,8},{8,9},{9,10},{10,1... | collective-permute-start | bytes 1597448 | tf_op jit(solution)/shard_map/ppermute | solution.py:193
  74.6 17.8 %collective-permute-start.9 = (f32[2,520,128]{2,1,0:T(8,128)S(1)}, f32[2,520,128]{2,1,0:T(8,128)S(1)}, u32[]{:S(2)}, u32[]{:S(2)}) collective-permute-start(f32[2,520,128]{2,1,0:T(8,128)S(1)} %collective-permute-done.5.refs_5_), channel_id=1, source_target_pairs={{0,63},{1,0},{2,1},{3,2},{4,3},{5,4},{6,5},{7,6},{8,7},{9,8},{10,9... | collective-permute-start | bytes 1597448 | tf_op jit(solution)/shard_map/ppermute | solution.py:193
  76.5 15.9 %collective-permute-start.6 = (f32[2,520,128]{2,1,0:T(8,128)S(1)}, f32[2,520,128]{2,1,0:T(8,128)S(1)}, u32[]{:S(2)}, u32[]{:S(2)}) collective-permute-start(f32[2,520,128]{2,1,0:T(8,128)S(1)} %collective-permute-done.5.refs_5_), channel_id=1, source_target_pairs={{0,1},{1,2},{2,3},{3,4},{4,5},{5,6},{6,7},{7,8},{8,9},{9,10},{10,1... | collective-permute-start | bytes 1597448 | tf_op jit(solution)/shard_map/ppermute | solution.py:193
  83.5 13.9 %collective-permute-start.7 = (f32[2,520,128]{2,1,0:T(8,128)S(1)}, f32[2,520,128]{2,1,0:T(8,128)S(1)}, u32[]{:S(2)}, u32[]{:S(2)}) collective-permute-start(f32[2,520,128]{2,1,0:T(8,128)S(1)} %collective-permute-done.2.refs_3_), channel_id=1, source_target_pairs={{0,63},{1,0},{2,1},{3,2},{4,3},{5,4},{6,5},{7,6},{8,7},{9,8},{10,9... | collective-permute-start | bytes 1597448 | tf_op jit(solution)/shard_map/ppermute | solution.py:193
  85.4 13.2 %collective-permute-start.3 = (f32[2,520,128]{2,1,0:T(8,128)S(1)}, f32[2,520,128]{2,1,0:T(8,128)S(1)}, u32[]{:S(2)}, u32[]{:S(2)}) collective-permute-start(f32[2,520,128]{2,1,0:T(8,128)S(1)} %collective-permute-done.2.refs_3_), channel_id=1, source_target_pairs={{0,1},{1,2},{2,3},{3,4},{4,5},{5,6},{6,7},{7,8},{8,9},{9,10},{10,1... | collective-permute-start | bytes 1597448 | tf_op jit(solution)/shard_map/ppermute | solution.py:193
  98.6 0.7 copy-start.7
where the time goes:
time: 153 us; the launch traced here: 152 us
  blocking collectives  59.9 us (39%)
  starting transfers between devices  41.1 us (27%)
  Pallas kernels  26.5 us (17%)
  waiting for transfers between devices  18.7 us (12%)
  local copies, waits for them, and re-layouts  5.84 us (4%)
    all_to_all x2, blocking collectives, swap(): return lax.all_to_all(x, 'member', split_axis=0, concat_axis=0, tiled=True)  59.9 us
    ppermute x10, starting transfers between devices, shifted(): return lax.ppermute(x, axis, [(i, (i + by) % n) for i in range(n)])  41.1 us
    pallas_call x1, Pallas kernels, on_device(): pl.pallas_call(functools.partial(update_kernel, per_patch), out_shape=f32...  22.8 us
    ppermute x10, waiting for transfers between devices, shifted(): return lax.ppermute(x, axis, [(i, (i + by) % n) for i in range(n)])  18.7 us
    unnamed x17, local copies, waits for them, and re-layouts  3.73 us
  transfers between devices with their start and end apart: 10, of which 5 were waited for; matrix products, arithmetic and copies ran while one was open for 0% of the time, Pallas kernels for 0%

commit v1 on v0

--- a/solution.py
+++ b/solution.py
@@ -27,12 +27,44 @@
     return jnp.where(rows == cols, 1.0, 0.0).astype(jnp.float32)
 
 
-def advect_kernel(planes, before, after, speed_row, speed_col, out, coef):
+def parity(axis):
+    return lax.rem(lax.axis_index(axis), 2)
+
+
+def edge_kernel(ensemble, speed_row, speed_col, across, within):
+    members, rows, width = ensemble.shape
+    groups = members // SUB
+    odd = parity("space") == 1
+
+    def put(at, low, high):
+        across[at] = jnp.where(odd, high, low)
+        within[at] = jnp.where(odd, low, high)
+
+    for g in range(groups):
+        for n in range(2):
+            low = ensemble[g * SUB : (g + 1) * SUB, n, :]
+            high = ensemble[g * SUB : (g + 1) * SUB, rows - 2 + n, :]
+            put(n * groups + g, low, high)
+    across[2 * groups] = jnp.zeros((SUB, width), jnp.float32)
+    within[2 * groups] = jnp.zeros((SUB, width), jnp.float32)
+    for n, speed in enumerate((speed_row, speed_col)):
+        put((2 * groups, slice(n, n + 1)), speed[0:1], speed[rows - 1 : rows])
+
+
+def advect_kernel(planes, across, within, speed_row, speed_col, out, coef):
     rows, members, width = planes.shape
     blocks = out.shape[0]
     cols = out.shape[3]
     groups = members // SUB
-    top, bottom = before[2 * groups], after[2 * groups]
+    odd = parity("space") == 1
+
+    def before(at):
+        return jnp.where(odd, within[at], across[at])
+
+    def after(at):
+        return jnp.where(odd, across[at], within[at])
+
+    top, bottom = before(2 * groups), after(2 * groups)
     for r in range(rows + 2):
         if r == 0:
             u, v = top[0:1], top[1:2]
@@ -59,9 +91,9 @@
 
     def body(g, carry):
         at = pl.ds(pl.multiple_of(g * SUB, SUB), SUB)
-        field = [before[g], before[groups + g]]
+        field = [before(g), before(groups + g)]
         field += [planes[i, at, :] for i in range(rows)]
-        field += [after[g], after[groups + g]]
+        field += [after(g), after(groups + g)]
         field = step(step(field, 0), 1)
         for i in range(rows):
             for b in range(blocks):
@@ -133,26 +165,31 @@
     return x
 
 
-def update_kernel(per_patch, slots, state, centre, *refs):
-    near = refs[:9]
-    out, z, inv = refs[9:]
+def update_kernel(per_patch, slots, state, centre, lines, corners, out, z, inv):
     parts, rows, members, cols = state.shape
     total = parts * members
     half = total // 2
+    odd_row, odd_col = parity("space"), parity("member")
     mask = jnp.int32(0)
     for n in range(slots.shape[0]):
-        mask = mask | lax.shift_left(jnp.int32(1), slots[n])
+        o, t = lax.div(slots[n], per_patch), lax.rem(slots[n], per_patch)
+        r, s = lax.div(o, 3), lax.rem(o, 3)
+        r = r + odd_row * (2 - 2 * r)
+        s = s + odd_col * (2 - 2 * s)
+        mask = mask | lax.shift_left(jnp.int32(1), (r * 3 + s) * per_patch + t)
     place = jnp.int32(0)
     for q in range(9 * per_patch):
         o, t = q // per_patch, q % per_patch
         r, s = o // 3 - 1, o % 3 - 1
         taper = 1.0 / (1.0 + r * r + s * s)
         chosen = lax.shift_right_logical(mask, q) & 1
+        ref = corners[r, s][0] if r and s else lines[r, s]
+        row = t + (corners[r, s][1] if r and s else 0)
 
         @pl.when(chosen == 1)
         def _():
-            obs = near[o].shape[2]
-            z[:, pl.ds(pl.multiple_of(place * obs, obs), obs)] = near[o][t] * (taper**0.5)
+            obs = ref.shape[2]
+            z[:, pl.ds(pl.multiple_of(place * obs, obs), obs)] = ref[row] * (taper**0.5)
 
         place = place + chosen
     gram = lax.dot_general(z[...], z[0:total, :], NT, precision=HI)
@@ -179,18 +216,30 @@
             out[p, i] = result[p * members : (p + 1) * members, i * cols : (i + 1) * cols]
 
 
+def update(per_patch, slots, state, centre, own, odd_z, even_z, across, within, within_c, across_c, *rest):
+    lines = {(0, 0): own, (0, 1): even_z, (0, -1): odd_z, (-1, 0): across, (1, 0): within}
+    corners = {
+        (-1, 1): (across_c, 0),
+        (-1, -1): (across_c, per_patch),
+        (1, 1): (within_c, 0),
+        (1, -1): (within_c, per_patch),
+    }
+    update_kernel(per_patch, slots, state, centre, lines, corners, *rest)
+
+
 VMEM = pl.BlockSpec(memory_space=pltpu.VMEM)
 SMEM = pl.BlockSpec(memory_space=pltpu.SMEM)
-PARAMS = pltpu.CompilerParams(vmem_limit_bytes=48 * 1024 * 1024)
+PARAMS = pltpu.CompilerParams(vmem_limit_bytes=28 * 1024 * 1024)
 
 
 def f32(*shape):
     return jax.ShapeDtypeStruct(shape, jnp.float32)
 
 
-def shifted(x, axis, by):
+def paired(x, axis, first):
     n = lax.axis_size(axis)
-    return lax.ppermute(x, axis, [(i, (i + by) % n) for i in range(n)])
+    pairs = [(i, (i + 1) % n) for i in range(first, n, 2)]
+    return lax.ppermute(x, axis, pairs + [(j, i) for i, j in pairs])
 
 
 def swap(x):
@@ -206,16 +255,16 @@
     total = parts * members
 
     planes = ensemble.transpose(1, 0, 2)
-
-    def edge(first, row):
-        speeds = jnp.concatenate(
-            [speed_row[row : row + 1], speed_col[row : row + 1], jnp.zeros((SUB - 2, width), jnp.float32)]
-        )
-        body = planes[first : first + 2].reshape(2 * groups, SUB, width)
-        return jnp.concatenate([body, speeds[None]])
-
-    before = shifted(edge(rows - 2, rows - 1), "space", 1)
-    after = shifted(edge(0, 0), "space", -1)
+    across, within = pl.pallas_call(
+        edge_kernel,
+        out_shape=(f32(2 * groups + 1, SUB, width), f32(2 * groups + 1, SUB, width)),
+        in_specs=[VMEM] * 3,
+        out_specs=(VMEM, VMEM),
+        compiler_params=PARAMS,
+        name="edges",
+    )(ensemble, speed_row, speed_col)
+    across = paired(across, "space", 1)
+    within = paired(within, "space", 0)
     state = pl.pallas_call(
         advect_kernel,
         out_shape=f32(parts, rows, members, cols),
@@ -224,7 +273,7 @@
         scratch_shapes=[pltpu.VMEM((rows + 2, 4, SUB, width), jnp.float32)],
         compiler_params=PARAMS,
         name="advect",
-    )(planes, before, after, speed_row, speed_col)
+    )(planes, across, within, speed_row, speed_col)
     state = swap(state)
     tiles, centre = pl.pallas_call(
         tile_kernel,
@@ -234,15 +283,19 @@
         compiler_params=PARAMS,
         name="tiles",
     )(obs_count[0, 0, 0], state, obs_cell[0, 0, 0], obs_value[0, 0, 0], obs_var[0, 0, 0])
-    left = shifted(tiles, "member", 1)
-    right = shifted(tiles, "member", -1)
-    line = (left, tiles, right)
-    near = [shifted(x, "space", 1) for x in line] + list(line) + [shifted(x, "space", -1) for x in line]
+    within = paired(tiles, "space", 0)
+    across = paired(tiles, "space", 1)
+    even_z = paired(tiles, "member", 0)
+    odd_z = paired(tiles, "member", 1)
+    within, across, even_z, odd_z = lax.optimization_barrier((within, across, even_z, odd_z))
+    both_z = jnp.concatenate([even_z, odd_z])
+    within_c = paired(both_z, "space", 0)
+    across_c = paired(both_z, "space", 1)
     slots = loc_slots[0, 0, 0]
     state = pl.pallas_call(
-        functools.partial(update_kernel, per_patch),
+        functools.partial(update, per_patch),
         out_shape=f32(parts, rows, members, cols),
-        in_specs=[SMEM] + [VMEM] * 11,
+        in_specs=[SMEM] + [VMEM] * 9,
         out_specs=VMEM,
         scratch_shapes=[
             pltpu.VMEM((total + SUB, slots.shape[0] * obs), jnp.float32),
@@ -250,7 +303,7 @@
         ],
         compiler_params=PARAMS,
         name="update",
-    )(slots, state, centre, *near)
+    )(slots, state, centre, tiles, odd_z, even_z, across, within, within_c, across_c)
     state = swap(state)
     return state.transpose(2, 1, 0, 3).reshape(members, rows, width)
 

time: 153 us -> 151 us (0.987)
  the two profiles are of different devices: /device:TPU:63 before, /device:TPU:55 now
where the time goes in v1:
time: 151 us; the launch traced here: 150 us
  blocking collectives  70.7 us (47%)
  waiting for transfers between devices  30.1 us (20%)
  Pallas kernels  26.2 us (17%)
  starting transfers between devices  18 us (12%)
  local copies, waits for them, and re-layouts  5.31 us (4%)
    all_to_all x2, blocking collectives, swap(): return lax.all_to_all(x, 'member', split_axis=0, concat_axis=0, tiled=True)  70.7 us
    ppermute x8, waiting for transfers between devices, paired(): return lax.ppermute(x, axis, pairs + [(j, i) for i, j in pairs])  30.1 us
    pallas_call x1, Pallas kernels, on_device(): pl.pallas_call(functools.partial(update, per_patch), out_shape=f32(parts,...  22.3 us
    ppermute x8, starting transfers between devices, paired(): return lax.ppermute(x, axis, pairs + [(j, i) for i, j in pairs])  18 us
    unnamed x24, local copies, waits for them, and re-layouts  3.35 us
  transfers between devices with their start and end apart: 8, of which 4 were waited for; matrix products, arithmetic and copies ran while one was open for 0% of the time, Pallas kernels for 0%

profile of v1, /device:TPU:55, one launch (start us, length us, event | category | flops | bytes accessed | tf_op | source)
XLA Modules:
  0.0 150.5 jit_solution(3484311941738711222)
XLA Ops:
  0.0 1.2 copy-done
  1.2 0.7 copy-done.2
  1.9 0.7 copy-done.4
  2.7 0.2 edges.1
  2.9 2.9 %collective-permute-start = (f32[17,8,1024]{2,1,0:T(8,128)S(1)}, f32[17,8,1024]{2,1,0:T(8,128)S(1)}, u32[]{:S(2)}, u32[]{:S(2)}) collective-permute-start(f32[17,8,1024]{2,1,0:T(8,128)S(1)} %get-tuple-element.13), channel_id=1, source_target_pairs={{1,2},{3,4},{5,6},{7,8},{9,10},{11,12},{13,14},{15,16},{17,18},{19... | collective-permute-start | bytes 1671176 | tf_op jit(solution)/shard_map/ppermute | solution.py:242
  5.8 2.0 %collective-permute-start.1 = (f32[17,8,1024]{2,1,0:T(8,128)S(1)}, f32[17,8,1024]{2,1,0:T(8,128)S(1)}, u32[]{:S(2)}, u32[]{:S(2)}) collective-permute-start(f32[17,8,1024]{2,1,0:T(8,128)S(1)} %get-tuple-element.14), channel_id=1, source_target_pairs={{0,1},{2,3},{4,5},{6,7},{8,9},{10,11},{12,13},{14,15},{16,17},{18,... | collective-permute-start | bytes 1671176 | tf_op jit(solution)/shard_map/ppermute | solution.py:242
  7.8 0.6 copy.16
  8.5 7.6 %collective-permute-done.across = f32[17,8,1024]{2,1,0:T(8,128)S(1)} collective-permute-done((f32[17,8,1024]{2,1,0:T(8,128)S(1)}, f32[17,8,1024]{2,1,0:T(8,128)S(1)}, u32[]{:S(2)}, u32[]{:S(2)}) %collective-permute-start) | collective-permute-done | bytes 557088 | tf_op jit(solution)/shard_map/ppermute | solution.py:242
  16.0 2.1 %advect.1 = f32[8,4,64,128]{3,2,1,0:T(8,128)S(1)} custom-call(f32[4,64,1024]{2,1,0:T(8,128)S(1)} %bitcast.11, f32[17,8,1024]{2,1,0:T(8,128)S(1)} %collective-permute-done.across, f32[17,8,1024]{2,1,0:T(8,128)S(1)} %collective-permute-done.1.within, f32[4,1024]{1,0:T(4,128)S(1)} %copy-done.3, f32[4,1024]{1,0:T(4,128)S(1)} %copy-done.5), custom_call_target="tpu_custom_call" | custom-call | tf_op jit(solution)/shard_map/advect/pallas_call | solution.py:268
  18.2 38.3 %all_to_all.10.state = f32[8,4,64,128]{3,2,1,0:T(8,128)S(1)} all-to-all(f32[8,4,64,128]{3,2,1,0:T(8,128)S(1)} %advect.1), channel_id=1, replica_groups=mesh['member'=8,'space'=64] {'member'}, dimensions={0} | all-to-all | bytes 2097152 | tf_op jit(solution)/shard_map/all_to_all | solution.py:246
  56.5 1.6 %tiles.1 = (f32[2,520,128]{2,1,0:T(8,128)S(1)}, f32[4,128]{1,0:T(4,128)S(1)}) custom-call(s32[2]{0:T(128)S(1)} %bitcast.15, f32[8,4,64,128]{3,2,1,0:T(8,128)S(1)} %all_to_all.10.state, s32[2,128]{1,0:T(2,128)S(1)} %bitcast.12, f32[2,128]{1,0:T(2,128)S(1)} %bitcast.13, f32[2,128]{1,0:T(2,128)S(1)} %bitcast.14), custom_call_target="tpu_custom_call" | custom-call | tf_op jit(solution)/shard_map/tiles/pallas_call | solution.py:278
  58.1 1.9 %collective-permute-start.5 = (f32[2,520,128]{2,1,0:T(8,128)S(1)}, f32[2,520,128]{2,1,0:T(8,128)S(1)}, u32[]{:S(2)}, u32[]{:S(2)}) collective-permute-start(f32[2,520,128]{2,1,0:T(8,128)S(1)} %get-tuple-element.16.own), channel_id=1, source_target_pairs={{64,128},{192,256},{320,384},{448,0},{128,64},{256,192},{384,320},... | collective-permute-start | bytes 1597448 | tf_op jit(solution)/shard_map/ppermute | solution.py:242
  60.0 2.2 %collective-permute-start.4 = (f32[2,520,128]{2,1,0:T(8,128)S(1)}, f32[2,520,128]{2,1,0:T(8,128)S(1)}, u32[]{:S(2)}, u32[]{:S(2)}) collective-permute-start(f32[2,520,128]{2,1,0:T(8,128)S(1)} %get-tuple-element.16.own), channel_id=1, source_target_pairs={{0,64},{128,192},{256,320},{384,448},{64,0},{192,128},{320,256},{4... | collective-permute-start | bytes 1597448 | tf_op jit(solution)/shard_map/ppermute | solution.py:242
  62.2 2.2 %collective-permute-start.3 = (f32[2,520,128]{2,1,0:T(8,128)S(1)}, f32[2,520,128]{2,1,0:T(8,128)S(1)}, u32[]{:S(2)}, u32[]{:S(2)}) collective-permute-start(f32[2,520,128]{2,1,0:T(8,128)S(1)} %get-tuple-element.16.own), channel_id=1, source_target_pairs={{1,2},{3,4},{5,6},{7,8},{9,10},{11,12},{13,14},{15,16},{17,18},{19... | collective-permute-start | bytes 1597448 | tf_op jit(solution)/shard_map/ppermute | solution.py:242
  64.4 1.9 %collective-permute-start.2 = (f32[2,520,128]{2,1,0:T(8,128)S(1)}, f32[2,520,128]{2,1,0:T(8,128)S(1)}, u32[]{:S(2)}, u32[]{:S(2)}) collective-permute-start(f32[2,520,128]{2,1,0:T(8,128)S(1)} %get-tuple-element.16.own), channel_id=1, source_target_pairs={{0,1},{2,3},{4,5},{6,7},{8,9},{10,11},{12,13},{14,15},{16,17},{18,... | collective-permute-start | bytes 1597448 | tf_op jit(solution)/shard_map/ppermute | solution.py:242
  66.4 8.3 %collective-permute-done.5.odd_z = f32[2,520,128]{2,1,0:T(8,128)S(1)} collective-permute-done((f32[2,520,128]{2,1,0:T(8,128)S(1)}, f32[2,520,128]{2,1,0:T(8,128)S(1)}, u32[]{:S(2)}, u32[]{:S(2)}) %collective-permute-start.5) | collective-permute-done | bytes 532512 | tf_op jit(solution)/shard_map/ppermute | solution.py:242
  74.7 0.7 collective-permute-done.4.even_z
  75.5 1.9 %collective-permute-start.7 = (f32[4,520,128]{2,1,0:T(8,128)S(1)}, f32[4,520,128]{2,1,0:T(8,128)S(1)}, u32[]{:S(2)}, u32[]{:S(2)}) collective-permute-start(f32[4,520,128]{2,1,0:T(8,128)S(1)} %constant_dynamic-update-slice_fusion), channel_id=1, source_target_pairs={{1,2},{3,4},{5,6},{7,8},{9,10},{11,12},{13,14},{15,16},{17,18},{19... | collective-permute-start | bytes 3194888 | tf_op jit(solution)/shard_map/ppermute | solution.py:242
  77.4 3.0 %collective-permute-start.6 = (f32[4,520,128]{2,1,0:T(8,128)S(1)}, f32[4,520,128]{2,1,0:T(8,128)S(1)}, u32[]{:S(2)}, u32[]{:S(2)}) collective-permute-start(f32[4,520,128]{2,1,0:T(8,128)S(1)} %constant_dynamic-update-slice_fusion), channel_id=1, source_target_pairs={{0,1},{2,3},{4,5},{6,7},{8,9},{10,11},{12,13},{14,15},{16,17},{18,... | collective-permute-start | bytes 3194888 | tf_op jit(solution)/shard_map/ppermute | solution.py:242
  80.4 13.5 %collective-permute-done.7.across_c = f32[4,520,128]{2,1,0:T(8,128)S(1)} collective-permute-done((f32[4,520,128]{2,1,0:T(8,128)S(1)}, f32[4,520,128]{2,1,0:T(8,128)S(1)}, u32[]{:S(2)}, u32[]{:S(2)}) %collective-permute-start.7) | collective-permute-done | bytes 1064992 | tf_op jit(solution)/shard_map/ppermute | solution.py:242
  93.9 22.3 %update.1 = f32[8,4,64,128]{3,2,1,0:T(8,128)S(1)} custom-call(s32[12]{0:T(128)S(1)} %bitcast.16, f32[8,4,64,128]{3,2,1,0:T(8,128)S(1)} %all_to_all.10.state, f32[4,128]{1,0:T(4,128)S(1)} %get-tuple-element.15.centre, f32[2,520,128]{2,1,0:T(8,128)S(1)} %get-tuple-element.16.own, f32[2,520,128]{2,1,0:T(8,128)S(1)} %collective-permute-done.5.odd_z, ...), custom_call_target="tpu_custom_call" | custom-call | tf_op jit(solution)/shard_map/update/pallas_call | solution.py:295
  116.1 32.4 %all_to_all.11 = f32[8,4,64,128]{3,2,1,0:T(8,128)S(1)} all-to-all(f32[8,4,64,128]{3,2,1,0:T(8,128)S(1)} %update.1), channel_id=1, replica_groups=mesh['member'=8,'space'=64] {'member'}, dimensions={0} | all-to-all | bytes 2097152 | tf_op jit(solution)/shard_map/all_to_all | solution.py:246
  148.6 0.6 copy.13
  149.2 1.3 reshape.4
  (25 shorter events, 0.1 us)
Async XLA Ops:
  0.0 1.2 copy-start
  1.2 0.7 copy-start.2
  1.9 0.7 copy-start.4
  2.7 5.2 %copy-start.1 = (f32[64,4,1024]{2,1,0:T(4,128)S(1)}, f32[64,4,1024]{2,1,0:T(4,128)}, u32[]{:S(2)}) copy-start(f32[64,4,1024]{2,1,0:T(4,128)} %ensemble.1) | copy-start | bytes 3145732
  2.9 13.1 %copy-start.3 = (f32[4,1024]{1,0:T(4,128)S(1)}, f32[4,1024]{1,0:T(4,128)}, u32[]{:S(2)}) copy-start(f32[4,1024]{1,0:T(4,128)} %speed_row.3) | copy-start | bytes 49156
  2.9 13.1 %copy-start.5 = (f32[4,1024]{1,0:T(4,128)S(1)}, f32[4,1024]{1,0:T(4,128)}, u32[]{:S(2)}) copy-start(f32[4,1024]{1,0:T(4,128)} %speed_col.3) | copy-start | bytes 49156
  2.9 13.1 %collective-permute-start = (f32[17,8,1024]{2,1,0:T(8,128)S(1)}, f32[17,8,1024]{2,1,0:T(8,128)S(1)}, u32[]{:S(2)}, u32[]{:S(2)}) collective-permute-start(f32[17,8,1024]{2,1,0:T(8,128)S(1)} %get-tuple-element.13), channel_id=1, source_target_pairs={{1,2},{3,4},{5,6},{7,8},{9,10},{11,12},{13,14},{15,16},{17,18},{19... | collective-permute-start | bytes 1671176 | tf_op jit(solution)/shard_map/ppermute | solution.py:242
  5.8 10.2 %collective-permute-start.1 = (f32[17,8,1024]{2,1,0:T(8,128)S(1)}, f32[17,8,1024]{2,1,0:T(8,128)S(1)}, u32[]{:S(2)}, u32[]{:S(2)}) collective-permute-start(f32[17,8,1024]{2,1,0:T(8,128)S(1)} %get-tuple-element.14), channel_id=1, source_target_pairs={{0,1},{2,3},{4,5},{6,7},{8,9},{10,11},{12,13},{14,15},{16,17},{18,... | collective-permute-start | bytes 1671176 | tf_op jit(solution)/shard_map/ppermute | solution.py:242
  18.1 38.3 %copy-start.6 = (s32[1,1,1,2,128]{4,3,2,1,0:T(2,128)S(1)}, s32[1,1,1,2,128]{4,3,2,1,0:T(2,128)}, u32[]{:S(2)}) copy-start(s32[1,1,1,2,128]{4,3,2,1,0:T(2,128)} %param.11) | copy-start | bytes 3076
  18.1 38.3 %copy-start.7 = (f32[1,1,1,2,128]{4,3,2,1,0:T(2,128)S(1)}, f32[1,1,1,2,128]{4,3,2,1,0:T(2,128)}, u32[]{:S(2)}) copy-start(f32[1,1,1,2,128]{4,3,2,1,0:T(2,128)} %param.12) | copy-start | bytes 3076
  18.1 38.3 %copy-start.8 = (f32[1,1,1,2,128]{4,3,2,1,0:T(2,128)S(1)}, f32[1,1,1,2,128]{4,3,2,1,0:T(2,128)}, u32[]{:S(2)}) copy-start(f32[1,1,1,2,128]{4,3,2,1,0:T(2,128)} %param.13) | copy-start | bytes 3076
  18.2 38.3 %copy-start.9 = (s32[1,1,1,2]{3,2,1,0:T(1,128)S(1)}, s32[1,1,1,2]{3,2,1,0:T(1,128)}, u32[]{:S(2)}) copy-start(s32[1,1,1,2]{3,2,1,0:T(1,128)} %param.14) | copy-start | bytes 28
  58.1 35.8 %copy-start.10 = (s32[1,1,1,12]{3,2,1,0:T(1,128)S(1)}, s32[1,1,1,12]{3,2,1,0:T(1,128)}, u32[]{:S(2)}) copy-start(s32[1,1,1,12]{3,2,1,0:T(1,128)} %param.15) | copy-start | bytes 148
  58.1 16.5 %collective-permute-start.5 = (f32[2,520,128]{2,1,0:T(8,128)S(1)}, f32[2,520,128]{2,1,0:T(8,128)S(1)}, u32[]{:S(2)}, u32[]{:S(2)}) collective-permute-start(f32[2,520,128]{2,1,0:T(8,128)S(1)} %get-tuple-element.16.own), channel_id=1, source_target_pairs={{64,128},{192,256},{320,384},{448,0},{128,64},{256,192},{384,320},... | collective-permute-start | bytes 1597448 | tf_op jit(solution)/shard_map/ppermute | solution.py:242
  60.0 15.3 %collective-permute-start.4 = (f32[2,520,128]{2,1,0:T(8,128)S(1)}, f32[2,520,128]{2,1,0:T(8,128)S(1)}, u32[]{:S(2)}, u32[]{:S(2)}) collective-permute-start(f32[2,520,128]{2,1,0:T(8,128)S(1)} %get-tuple-element.16.own), channel_id=1, source_target_pairs={{0,64},{128,192},{256,320},{384,448},{64,0},{192,128},{320,256},{4... | collective-permute-start | bytes 1597448 | tf_op jit(solution)/shard_map/ppermute | solution.py:242
  62.2 13.2 %collective-permute-start.3 = (f32[2,520,128]{2,1,0:T(8,128)S(1)}, f32[2,520,128]{2,1,0:T(8,128)S(1)}, u32[]{:S(2)}, u32[]{:S(2)}) collective-permute-start(f32[2,520,128]{2,1,0:T(8,128)S(1)} %get-tuple-element.16.own), channel_id=1, source_target_pairs={{1,2},{3,4},{5,6},{7,8},{9,10},{11,12},{13,14},{15,16},{17,18},{19... | collective-permute-start | bytes 1597448 | tf_op jit(solution)/shard_map/ppermute | solution.py:242
  64.4 10.9 %collective-permute-start.2 = (f32[2,520,128]{2,1,0:T(8,128)S(1)}, f32[2,520,128]{2,1,0:T(8,128)S(1)}, u32[]{:S(2)}, u32[]{:S(2)}) collective-permute-start(f32[2,520,128]{2,1,0:T(8,128)S(1)} %get-tuple-element.16.own), channel_id=1, source_target_pairs={{0,1},{2,3},{4,5},{6,7},{8,9},{10,11},{12,13},{14,15},{16,17},{18,... | collective-permute-start | bytes 1597448 | tf_op jit(solution)/shard_map/ppermute | solution.py:242
  75.5 18.4 %collective-permute-start.7 = (f32[4,520,128]{2,1,0:T(8,128)S(1)}, f32[4,520,128]{2,1,0:T(8,128)S(1)}, u32[]{:S(2)}, u32[]{:S(2)}) collective-permute-start(f32[4,520,128]{2,1,0:T(8,128)S(1)} %constant_dynamic-update-slice_fusion), channel_id=1, source_target_pairs={{1,2},{3,4},{5,6},{7,8},{9,10},{11,12},{13,14},{15,16},{17,18},{19... | collective-permute-start | bytes 3194888 | tf_op jit(solution)/shard_map/ppermute | solution.py:242
  77.4 16.5 %collective-permute-start.6 = (f32[4,520,128]{2,1,0:T(8,128)S(1)}, f32[4,520,128]{2,1,0:T(8,128)S(1)}, u32[]{:S(2)}, u32[]{:S(2)}) collective-permute-start(f32[4,520,128]{2,1,0:T(8,128)S(1)} %constant_dynamic-update-slice_fusion), channel_id=1, source_target_pairs={{0,1},{2,3},{4,5},{6,7},{8,9},{10,11},{12,13},{14,15},{16,17},{18,... | collective-permute-start | bytes 3194888 | tf_op jit(solution)/shard_map/ppermute | solution.py:242

commit v2 on v1

--- a/solution.py
+++ b/solution.py
@@ -21,6 +21,27 @@
     return a, b, c
 
 
+def split2(x):
+    a = x.astype(jnp.bfloat16)
+    return a, (x - a.astype(jnp.float32)).astype(jnp.bfloat16)
+
+
+def product(a, b, dims=(((1,), (0,)), ((), ()))):
+    (a, a_low), (b, b_low) = a, b
+    dot = functools.partial(
+        lax.dot_general, dimension_numbers=dims, preferred_element_type=jnp.float32
+    )
+    return dot(a, b) + (dot(a, b_low) + dot(a_low, b))
+
+
+def product3(a, b):
+    return product(split2(a), split2(b))
+
+
+def full(a, b):
+    return jnp.dot(a, b, precision=HI)
+
+
 def eye(n):
     rows = lax.broadcasted_iota(jnp.int32, (n, n), 0)
     cols = lax.broadcasted_iota(jnp.int32, (n, n), 1)
@@ -31,7 +52,17 @@
     return lax.rem(lax.axis_index(axis), 2)
 
 
-def edge_kernel(ensemble, speed_row, speed_col, across, within):
+def edge_kernel(ensemble_far, row_far, col_far, across, within, ensemble, speed_row, speed_col, done):
+    copies = [
+        pltpu.make_async_copy(far, near, done.at[n])
+        for n, (far, near) in enumerate(
+            ((ensemble_far, ensemble), (row_far, speed_row), (col_far, speed_col))
+        )
+    ]
+    for copy in copies:
+        copy.start()
+    for copy in copies:
+        copy.wait()
     members, rows, width = ensemble.shape
     groups = members // SUB
     odd = parity("space") == 1
@@ -146,23 +177,33 @@
     e = unit - scale * s
     rho = (bound - 1.0) / (bound + 1.0)
 
-    def more(carry):
-        return carry[2] > 1e-3
-
-    def square(carry):
+    def square(multiply, carry):
         x, e, rho = carry
-        both = jnp.dot(jnp.concatenate([x, e], axis=0), e, precision=HI)
+        both = multiply(jnp.concatenate([x, e], axis=0), e)
         square_rho = rho * rho
         scale = 2.0 / (2.0 - square_rho)
         x = scale * (x + both[:n])
         e = scale * both[n:] + (1.0 - scale) * unit
         return x, e, square_rho / (2.0 - square_rho)
 
-    x, e, rho = lax.while_loop(more, square, (x, e, rho))
-    for _ in range(2):
-        e = unit - jnp.dot(s, x, precision=HI)
-        x = x + jnp.dot(x, e, precision=HI)
-    return x
+    def quick(carry):
+        return (carry[2] > 1e-3) & (bound < 1000.0)
+
+    def careful(carry):
+        return carry[2] > 1e-3
+
+    carry = lax.while_loop(quick, functools.partial(square, product3), (x, e, rho))
+    x = lax.while_loop(careful, functools.partial(square, full), carry)[0]
+
+    def unsettled(carry):
+        return (carry[1] > 1e-5) & (carry[2] < 8)
+
+    def newton(carry):
+        x, _, count = carry
+        e = unit - full(s, x)
+        return x + product3(x, e), jnp.sum(e * e), count + 1
+
+    return lax.while_loop(unsettled, newton, (x, jnp.float32(1.0), jnp.int32(0)))[0]
 
 
 def update_kernel(per_patch, slots, state, centre, lines, corners, out, z, inv):
@@ -192,11 +233,15 @@
             z[:, pl.ds(pl.multiple_of(place * obs, obs), obs)] = ref[row] * (taper**0.5)
 
         place = place + chosen
-    gram = lax.dot_general(z[...], z[0:total, :], NT, precision=HI)
-    drive = gram[total : total + SUB]
-    s11 = gram[:half, :half] + eye(half)
-    s12 = gram[:half, half:]
-    s22 = gram[half:total, half:] + eye(half)
+    z1, z2 = split2(z[0:half, :]), split2(z[half:total, :])
+    zd = split2(z[total:, :])
+    top = [jnp.concatenate([p, q], axis=0) for p, q in zip(z1, zd)]
+    gram1 = product(top, z1, NT)
+    gram2 = product(top, z2, NT)
+    drive = jnp.concatenate([gram1[half:], gram2[half:]], axis=1)
+    s11 = gram1[:half] + eye(half)
+    s12 = gram2[:half]
+    s22 = product(z2, z2, NT) + eye(half)
     inv11 = spd_inverse(s11)
     w = jnp.dot(inv11, s12, precision=HI)
     schur = s22 - lax.dot_general(s12, w, (((0,), (0,)), ((), ())), precision=HI)
@@ -209,7 +254,7 @@
     shift = jnp.dot(drive, inv[...], precision=HI)[0:1]
     mean = jnp.concatenate([centre[i : i + 1, :] for i in range(rows)], axis=1)
     anomaly = patch_matrix(state) - mean
-    result = jnp.dot(0.5 * inv[...] + shift, anomaly, precision=HI)
+    result = product3(0.5 * inv[...] + shift, anomaly)
     result = result + (mean + 0.5 * anomaly)
     for p in range(parts):
         for i in range(rows):
@@ -258,9 +303,15 @@
     across, within = pl.pallas_call(
         edge_kernel,
         out_shape=(f32(2 * groups + 1, SUB, width), f32(2 * groups + 1, SUB, width)),
-        in_specs=[VMEM] * 3,
+        in_specs=[pl.BlockSpec(memory_space=pltpu.HBM)] * 3,
         out_specs=(VMEM, VMEM),
-        compiler_params=PARAMS,
+        scratch_shapes=[
+            pltpu.VMEM(ensemble.shape, jnp.float32),
+            pltpu.VMEM(speed_row.shape, jnp.float32),
+            pltpu.VMEM(speed_col.shape, jnp.float32),
+            pltpu.SemaphoreType.DMA((3,)),
+        ],
+        compiler_params=pltpu.CompilerParams(vmem_limit_bytes=62 * 1024 * 1024),
         name="edges",
     )(ensemble, speed_row, speed_col)
     across = paired(across, "space", 1)

time: 151 us -> 142 us (0.940)
  Pallas kernels: 26.2 us -> 20 us
  local copies, waits for them, and re-layouts: 5.31 us -> 2.65 us
    pallas_call x1, Pallas kernels: 22.3 us -> 13.7 us  [on_device(): pl.pallas_call(functools.partial(update, per_patch), out_shape=f32(parts,...]
    unnamed x24 -> x18, local copies, waits for them, and re-layouts: 3.35 us -> 0.7 us
    pallas_call x1, Pallas kernels: 0.23 us -> 2.56 us  [on_device(): pl.pallas_call(edge_kernel, out_shape=(f32(2 * groups + 1, SUB, width), f...]
where the time goes in v2:
time: 142 us
  blocking collectives  70.7 us (50%)
  waiting for transfers between devices  30.3 us (21%)
  Pallas kernels  20 us (14%)
  starting transfers between devices  17.9 us (13%)
  local copies, waits for them, and re-layouts  2.65 us (2%)
    all_to_all x2, blocking collectives, swap(): return lax.all_to_all(x, 'member', split_axis=0, concat_axis=0, tiled=True)  70.7 us
    ppermute x8, waiting for transfers between devices, paired(): return lax.ppermute(x, axis, pairs + [(j, i) for i, j in pairs])  30.3 us
    ppermute x8, starting transfers between devices, paired(): return lax.ppermute(x, axis, pairs + [(j, i) for i, j in pairs])  17.9 us
    pallas_call x1, Pallas kernels, on_device(): pl.pallas_call(functools.partial(update, per_patch), out_shape=f32(parts,...  13.7 us
  transfers between devices with their start and end apart: 8, of which 4 were waited for; matrix products, arithmetic and copies ran while one was open for 0% of the time, Pallas kernels for 0%

profile of v2, /device:TPU:55, one launch (start us, length us, event | category | flops | bytes accessed | tf_op | source)
XLA Modules:
  0.0 141.7 jit_solution(13322931340387340356)
XLA Ops:
  0.0 2.6 %edges.1 = (f32[17,8,1024]{2,1,0:T(8,128)}, f32[17,8,1024]{2,1,0:T(8,128)}) custom-call(f32[64,4,1024]{2,1,0:T(4,128)} %ensemble_far.1, f32[4,1024]{1,0:T(4,128)} %speed_row.1, f32[4,1024]{1,0:T(4,128)} %speed_col.1), custom_call_target="tpu_custom_call" | custom-call | tf_op jit(solution)/shard_map/edges/pallas_call | solution.py:303
  2.6 0.0 copy-start.1
  2.6 2.8 %collective-permute-start = (f32[17,8,1024]{2,1,0:T(8,128)}, f32[17,8,1024]{2,1,0:T(8,128)S(1)}, u32[]{:S(2)}, u32[]{:S(2)}) collective-permute-start(f32[17,8,1024]{2,1,0:T(8,128)} %get-tuple-element.13), channel_id=1, source_target_pairs={{1,2},{3,4},{5,6},{7,8},{9,10},{11,12},{13,14},{15,16},{17,18},{19... | collective-permute-start | bytes 1671176 | tf_op jit(solution)/shard_map/ppermute | solution.py:287
  5.4 2.0 %collective-permute-start.1 = (f32[17,8,1024]{2,1,0:T(8,128)}, f32[17,8,1024]{2,1,0:T(8,128)S(1)}, u32[]{:S(2)}, u32[]{:S(2)}) collective-permute-start(f32[17,8,1024]{2,1,0:T(8,128)} %get-tuple-element.14), channel_id=1, source_target_pairs={{0,1},{2,3},{4,5},{6,7},{8,9},{10,11},{12,13},{14,15},{16,17},{18,... | collective-permute-start | bytes 1671176 | tf_op jit(solution)/shard_map/ppermute | solution.py:287
  7.4 0.6 copy.16
  8.0 7.8 %collective-permute-done.across = f32[17,8,1024]{2,1,0:T(8,128)S(1)} collective-permute-done((f32[17,8,1024]{2,1,0:T(8,128)}, f32[17,8,1024]{2,1,0:T(8,128)S(1)}, u32[]{:S(2)}, u32[]{:S(2)}) %collective-permute-start) | collective-permute-done | bytes 557088 | tf_op jit(solution)/shard_map/ppermute | solution.py:287
  15.8 2.1 %advect.1 = f32[8,4,64,128]{3,2,1,0:T(8,128)S(1)} custom-call(f32[4,64,1024]{2,1,0:T(8,128)S(1)} %bitcast.11, f32[17,8,1024]{2,1,0:T(8,128)S(1)} %collective-permute-done.across, f32[17,8,1024]{2,1,0:T(8,128)S(1)} %collective-permute-done.1.within, f32[4,1024]{1,0:T(4,128)S(1)} %copy-done, f32[4,1024]{1,0:T(4,128)S(1)} %copy-done.1), custom_call_target="tpu_custom_call" | custom-call | tf_op jit(solution)/shard_map/advect/pallas_call | solution.py:319
  17.9 0.0 copy-start.2
  17.9 0.0 copy-start.5
  17.9 38.3 %all_to_all.10.state = f32[8,4,64,128]{3,2,1,0:T(8,128)S(1)} all-to-all(f32[8,4,64,128]{3,2,1,0:T(8,128)S(1)} %advect.1), channel_id=1, replica_groups=mesh['member'=8,'space'=64] {'member'}, dimensions={0} | all-to-all | bytes 2097152 | tf_op jit(solution)/shard_map/all_to_all | solution.py:291
  56.2 1.6 %tiles.1 = (f32[2,520,128]{2,1,0:T(8,128)S(1)}, f32[4,128]{1,0:T(4,128)S(1)}) custom-call(s32[2]{0:T(128)S(1)} %bitcast.15, f32[8,4,64,128]{3,2,1,0:T(8,128)S(1)} %all_to_all.10.state, s32[2,128]{1,0:T(2,128)S(1)} %bitcast.12, f32[2,128]{1,0:T(2,128)S(1)} %bitcast.13, f32[2,128]{1,0:T(2,128)S(1)} %bitcast.14), custom_call_target="tpu_custom_call" | custom-call | tf_op jit(solution)/shard_map/tiles/pallas_call | solution.py:329
  57.9 1.9 %collective-permute-start.5 = (f32[2,520,128]{2,1,0:T(8,128)S(1)}, f32[2,520,128]{2,1,0:T(8,128)S(1)}, u32[]{:S(2)}, u32[]{:S(2)}) collective-permute-start(f32[2,520,128]{2,1,0:T(8,128)S(1)} %get-tuple-element.16.own), channel_id=1, source_target_pairs={{64,128},{192,256},{320,384},{448,0},{128,64},{256,192},{384,320},... | collective-permute-start | bytes 1597448 | tf_op jit(solution)/shard_map/ppermute | solution.py:287
  59.8 2.2 %collective-permute-start.4 = (f32[2,520,128]{2,1,0:T(8,128)S(1)}, f32[2,520,128]{2,1,0:T(8,128)S(1)}, u32[]{:S(2)}, u32[]{:S(2)}) collective-permute-start(f32[2,520,128]{2,1,0:T(8,128)S(1)} %get-tuple-element.16.own), channel_id=1, source_target_pairs={{0,64},{128,192},{256,320},{384,448},{64,0},{192,128},{320,256},{4... | collective-permute-start | bytes 1597448 | tf_op jit(solution)/shard_map/ppermute | solution.py:287
  62.0 2.2 %collective-permute-start.3 = (f32[2,520,128]{2,1,0:T(8,128)S(1)}, f32[2,520,128]{2,1,0:T(8,128)S(1)}, u32[]{:S(2)}, u32[]{:S(2)}) collective-permute-start(f32[2,520,128]{2,1,0:T(8,128)S(1)} %get-tuple-element.16.own), channel_id=1, source_target_pairs={{1,2},{3,4},{5,6},{7,8},{9,10},{11,12},{13,14},{15,16},{17,18},{19... | collective-permute-start | bytes 1597448 | tf_op jit(solution)/shard_map/ppermute | solution.py:287
  64.2 1.9 %collective-permute-start.2 = (f32[2,520,128]{2,1,0:T(8,128)S(1)}, f32[2,520,128]{2,1,0:T(8,128)S(1)}, u32[]{:S(2)}, u32[]{:S(2)}) collective-permute-start(f32[2,520,128]{2,1,0:T(8,128)S(1)} %get-tuple-element.16.own), channel_id=1, source_target_pairs={{0,1},{2,3},{4,5},{6,7},{8,9},{10,11},{12,13},{14,15},{16,17},{18,... | collective-permute-start | bytes 1597448 | tf_op jit(solution)/shard_map/ppermute | solution.py:287
  66.1 8.3 %collective-permute-done.5.odd_z = f32[2,520,128]{2,1,0:T(8,128)S(1)} collective-permute-done((f32[2,520,128]{2,1,0:T(8,128)S(1)}, f32[2,520,128]{2,1,0:T(8,128)S(1)}, u32[]{:S(2)}, u32[]{:S(2)}) %collective-permute-start.5) | collective-permute-done | bytes 532512 | tf_op jit(solution)/shard_map/ppermute | solution.py:287
  74.4 0.7 collective-permute-done.4.even_z
  75.2 1.9 %collective-permute-start.7 = (f32[4,520,128]{2,1,0:T(8,128)S(1)}, f32[4,520,128]{2,1,0:T(8,128)S(1)}, u32[]{:S(2)}, u32[]{:S(2)}) collective-permute-start(f32[4,520,128]{2,1,0:T(8,128)S(1)} %constant_dynamic-update-slice_fusion), channel_id=1, source_target_pairs={{1,2},{3,4},{5,6},{7,8},{9,10},{11,12},{13,14},{15,16},{17,18},{19... | collective-permute-start | bytes 3194888 | tf_op jit(solution)/shard_map/ppermute | solution.py:287
  77.2 3.0 %collective-permute-start.6 = (f32[4,520,128]{2,1,0:T(8,128)S(1)}, f32[4,520,128]{2,1,0:T(8,128)S(1)}, u32[]{:S(2)}, u32[]{:S(2)}) collective-permute-start(f32[4,520,128]{2,1,0:T(8,128)S(1)} %constant_dynamic-update-slice_fusion), channel_id=1, source_target_pairs={{0,1},{2,3},{4,5},{6,7},{8,9},{10,11},{12,13},{14,15},{16,17},{18,... | collective-permute-start | bytes 3194888 | tf_op jit(solution)/shard_map/ppermute | solution.py:287
  80.1 13.5 %collective-permute-done.7.across_c = f32[4,520,128]{2,1,0:T(8,128)S(1)} collective-permute-done((f32[4,520,128]{2,1,0:T(8,128)S(1)}, f32[4,520,128]{2,1,0:T(8,128)S(1)}, u32[]{:S(2)}, u32[]{:S(2)}) %collective-permute-start.7) | collective-permute-done | bytes 1064992 | tf_op jit(solution)/shard_map/ppermute | solution.py:287
  93.6 13.7 %update.1 = f32[8,4,64,128]{3,2,1,0:T(8,128)S(1)} custom-call(s32[12]{0:T(128)S(1)} %bitcast.16, f32[8,4,64,128]{3,2,1,0:T(8,128)S(1)} %all_to_all.10.state, f32[4,128]{1,0:T(4,128)S(1)} %get-tuple-element.15.centre, f32[2,520,128]{2,1,0:T(8,128)S(1)} %get-tuple-element.16.own, f32[2,520,128]{2,1,0:T(8,128)S(1)} %collective-permute-done.5.odd_z, ...), custom_call_target="tpu_custom_call" | custom-call | tf_op jit(solution)/shard_map/update/pallas_call | solution.py:346
  107.3 32.4 %all_to_all.11 = f32[8,4,64,128]{3,2,1,0:T(8,128)S(1)} all-to-all(f32[8,4,64,128]{3,2,1,0:T(8,128)S(1)} %update.1), channel_id=1, replica_groups=mesh['member'=8,'space'=64] {'member'}, dimensions={0} | all-to-all | bytes 2097152 | tf_op jit(solution)/shard_map/all_to_all | solution.py:291
  139.8 0.6 copy.13
  140.4 1.3 reshape.4
  (19 shorter events, 0.1 us)
Async XLA Ops:
  0.0 7.4 %copy-start.7 = (f32[64,4,1024]{2,1,0:T(4,128)S(1)}, f32[64,4,1024]{2,1,0:T(4,128)}, u32[]{:S(2)}) copy-start(f32[64,4,1024]{2,1,0:T(4,128)} %ensemble_far.1) | copy-start | bytes 3145732
  2.6 13.2 %copy-start = (f32[4,1024]{1,0:T(4,128)S(1)}, f32[4,1024]{1,0:T(4,128)}, u32[]{:S(2)}) copy-start(f32[4,1024]{1,0:T(4,128)} %speed_row.1) | copy-start | bytes 49156
  2.6 13.2 %copy-start.1 = (f32[4,1024]{1,0:T(4,128)S(1)}, f32[4,1024]{1,0:T(4,128)}, u32[]{:S(2)}) copy-start(f32[4,1024]{1,0:T(4,128)} %speed_col.1) | copy-start | bytes 49156
  2.6 13.2 %collective-permute-start = (f32[17,8,1024]{2,1,0:T(8,128)}, f32[17,8,1024]{2,1,0:T(8,128)S(1)}, u32[]{:S(2)}, u32[]{:S(2)}) collective-permute-start(f32[17,8,1024]{2,1,0:T(8,128)} %get-tuple-element.13), channel_id=1, source_target_pairs={{1,2},{3,4},{5,6},{7,8},{9,10},{11,12},{13,14},{15,16},{17,18},{19... | collective-permute-start | bytes 1671176 | tf_op jit(solution)/shard_map/ppermute | solution.py:287
  5.4 10.4 %collective-permute-start.1 = (f32[17,8,1024]{2,1,0:T(8,128)}, f32[17,8,1024]{2,1,0:T(8,128)S(1)}, u32[]{:S(2)}, u32[]{:S(2)}) collective-permute-start(f32[17,8,1024]{2,1,0:T(8,128)} %get-tuple-element.14), channel_id=1, source_target_pairs={{0,1},{2,3},{4,5},{6,7},{8,9},{10,11},{12,13},{14,15},{16,17},{18,... | collective-permute-start | bytes 1671176 | tf_op jit(solution)/shard_map/ppermute | solution.py:287
  17.9 38.3 %copy-start.2 = (s32[1,1,1,2,128]{4,3,2,1,0:T(2,128)S(1)}, s32[1,1,1,2,128]{4,3,2,1,0:T(2,128)}, u32[]{:S(2)}) copy-start(s32[1,1,1,2,128]{4,3,2,1,0:T(2,128)} %param.11) | copy-start | bytes 3076
  17.9 38.3 %copy-start.3 = (f32[1,1,1,2,128]{4,3,2,1,0:T(2,128)S(1)}, f32[1,1,1,2,128]{4,3,2,1,0:T(2,128)}, u32[]{:S(2)}) copy-start(f32[1,1,1,2,128]{4,3,2,1,0:T(2,128)} %param.12) | copy-start | bytes 3076
  17.9 38.3 %copy-start.4 = (f32[1,1,1,2,128]{4,3,2,1,0:T(2,128)S(1)}, f32[1,1,1,2,128]{4,3,2,1,0:T(2,128)}, u32[]{:S(2)}) copy-start(f32[1,1,1,2,128]{4,3,2,1,0:T(2,128)} %param.13) | copy-start | bytes 3076
  17.9 38.3 %copy-start.5 = (s32[1,1,1,2]{3,2,1,0:T(1,128)S(1)}, s32[1,1,1,2]{3,2,1,0:T(1,128)}, u32[]{:S(2)}) copy-start(s32[1,1,1,2]{3,2,1,0:T(1,128)} %param.14) | copy-start | bytes 28
  57.9 35.8 %copy-start.6 = (s32[1,1,1,12]{3,2,1,0:T(1,128)S(1)}, s32[1,1,1,12]{3,2,1,0:T(1,128)}, u32[]{:S(2)}) copy-start(s32[1,1,1,12]{3,2,1,0:T(1,128)} %param.15) | copy-start | bytes 148
  57.9 16.6 %collective-permute-start.5 = (f32[2,520,128]{2,1,0:T(8,128)S(1)}, f32[2,520,128]{2,1,0:T(8,128)S(1)}, u32[]{:S(2)}, u32[]{:S(2)}) collective-permute-start(f32[2,520,128]{2,1,0:T(8,128)S(1)} %get-tuple-element.16.own), channel_id=1, source_target_pairs={{64,128},{192,256},{320,384},{448,0},{128,64},{256,192},{384,320},... | collective-permute-start | bytes 1597448 | tf_op jit(solution)/shard_map/ppermute | solution.py:287
  59.8 15.3 %collective-permute-start.4 = (f32[2,520,128]{2,1,0:T(8,128)S(1)}, f32[2,520,128]{2,1,0:T(8,128)S(1)}, u32[]{:S(2)}, u32[]{:S(2)}) collective-permute-start(f32[2,520,128]{2,1,0:T(8,128)S(1)} %get-tuple-element.16.own), channel_id=1, source_target_pairs={{0,64},{128,192},{256,320},{384,448},{64,0},{192,128},{320,256},{4... | collective-permute-start | bytes 1597448 | tf_op jit(solution)/shard_map/ppermute | solution.py:287
  62.0 13.1 %collective-permute-start.3 = (f32[2,520,128]{2,1,0:T(8,128)S(1)}, f32[2,520,128]{2,1,0:T(8,128)S(1)}, u32[]{:S(2)}, u32[]{:S(2)}) collective-permute-start(f32[2,520,128]{2,1,0:T(8,128)S(1)} %get-tuple-element.16.own), channel_id=1, source_target_pairs={{1,2},{3,4},{5,6},{7,8},{9,10},{11,12},{13,14},{15,16},{17,18},{19... | collective-permute-start | bytes 1597448 | tf_op jit(solution)/shard_map/ppermute | solution.py:287
  64.2 11.0 %collective-permute-start.2 = (f32[2,520,128]{2,1,0:T(8,128)S(1)}, f32[2,520,128]{2,1,0:T(8,128)S(1)}, u32[]{:S(2)}, u32[]{:S(2)}) collective-permute-start(f32[2,520,128]{2,1,0:T(8,128)S(1)} %get-tuple-element.16.own), channel_id=1, source_target_pairs={{0,1},{2,3},{4,5},{6,7},{8,9},{10,11},{12,13},{14,15},{16,17},{18,... | collective-permute-start | bytes 1597448 | tf_op jit(solution)/shard_map/ppermute | solution.py:287
  75.2 18.4 %collective-permute-start.7 = (f32[4,520,128]{2,1,0:T(8,128)S(1)}, f32[4,520,128]{2,1,0:T(8,128)S(1)}, u32[]{:S(2)}, u32[]{:S(2)}) collective-permute-start(f32[4,520,128]{2,1,0:T(8,128)S(1)} %constant_dynamic-update-slice_fusion), channel_id=1, source_target_pairs={{1,2},{3,4},{5,6},{7,8},{9,10},{11,12},{13,14},{15,16},{17,18},{19... | collective-permute-start | bytes 3194888 | tf_op jit(solution)/shard_map/ppermute | solution.py:287
  77.2 16.5 %collective-permute-start.6 = (f32[4,520,128]{2,1,0:T(8,128)S(1)}, f32[4,520,128]{2,1,0:T(8,128)S(1)}, u32[]{:S(2)}, u32[]{:S(2)}) collective-permute-start(f32[4,520,128]{2,1,0:T(8,128)S(1)} %constant_dynamic-update-slice_fusion), channel_id=1, source_target_pairs={{0,1},{2,3},{4,5},{6,7},{8,9},{10,11},{12,13},{14,15},{16,17},{18,... | collective-permute-start | bytes 3194888 | tf_op jit(solution)/shard_map/ppermute | solution.py:287

commit v3 on v2

--- a/solution.py
+++ b/solution.py
@@ -53,25 +53,28 @@
 
 
 def edge_kernel(ensemble_far, row_far, col_far, across, within, ensemble, speed_row, speed_col, done):
-    copies = [
-        pltpu.make_async_copy(far, near, done.at[n])
-        for n, (far, near) in enumerate(
-            ((ensemble_far, ensemble), (row_far, speed_row), (col_far, speed_col))
-        )
-    ]
-    for copy in copies:
-        copy.start()
-    for copy in copies:
-        copy.wait()
     members, rows, width = ensemble.shape
     groups = members // SUB
     odd = parity("space") == 1
 
+    def fetch(far, near, n):
+        return pltpu.make_async_copy(far, near, done.at[n])
+
+    def part(g):
+        at = pl.ds(g * SUB, SUB)
+        return fetch(ensemble_far.at[at], ensemble.at[at], g)
+
+    copies = [part(g) for g in range(groups)]
+    copies += [fetch(row_far, speed_row, groups), fetch(col_far, speed_col, groups + 1)]
+    for copy in copies:
+        copy.start()
+
     def put(at, low, high):
         across[at] = jnp.where(odd, high, low)
         within[at] = jnp.where(odd, low, high)
 
     for g in range(groups):
+        copies[g].wait()
         for n in range(2):
             low = ensemble[g * SUB : (g + 1) * SUB, n, :]
             high = ensemble[g * SUB : (g + 1) * SUB, rows - 2 + n, :]
@@ -79,6 +82,7 @@
     across[2 * groups] = jnp.zeros((SUB, width), jnp.float32)
     within[2 * groups] = jnp.zeros((SUB, width), jnp.float32)
     for n, speed in enumerate((speed_row, speed_col)):
+        copies[groups + n].wait()
         put((2 * groups, slice(n, n + 1)), speed[0:1], speed[rows - 1 : rows])
 
 
@@ -206,10 +210,7 @@
     return lax.while_loop(unsettled, newton, (x, jnp.float32(1.0), jnp.int32(0)))[0]
 
 
-def update_kernel(per_patch, slots, state, centre, lines, corners, out, z, inv):
-    parts, rows, members, cols = state.shape
-    total = parts * members
-    half = total // 2
+def fill(z, slots, per_patch, tiles):
     odd_row, odd_col = parity("space"), parity("member")
     mask = jnp.int32(0)
     for n in range(slots.shape[0]):
@@ -218,30 +219,47 @@
         r = r + odd_row * (2 - 2 * r)
         s = s + odd_col * (2 - 2 * s)
         mask = mask | lax.shift_left(jnp.int32(1), (r * 3 + s) * per_patch + t)
-    place = jnp.int32(0)
-    for q in range(9 * per_patch):
-        o, t = q // per_patch, q % per_patch
-        r, s = o // 3 - 1, o % 3 - 1
-        taper = 1.0 / (1.0 + r * r + s * s)
-        chosen = lax.shift_right_logical(mask, q) & 1
-        ref = corners[r, s][0] if r and s else lines[r, s]
-        row = t + (corners[r, s][1] if r and s else 0)
-
-        @pl.when(chosen == 1)
-        def _():
+    for n, (r, s, ref, first) in enumerate(tiles):
+        for t in range(per_patch):
+            bit = ((r + 1) * 3 + s + 1) * per_patch + t
+            chosen = (lax.shift_right_logical(mask, bit) & 1).astype(jnp.float32)
+            root = (1.0 / (1.0 + r * r + s * s)) ** 0.5
             obs = ref.shape[2]
-            z[:, pl.ds(pl.multiple_of(place * obs, obs), obs)] = ref[row] * (taper**0.5)
-
-        place = place + chosen
+            at = (n * per_patch + t) * obs
+            z[:, at : at + obs] = ref[first + t] * (chosen * root)
+
+
+def gram_blocks(z, total):
+    half = total // 2
     z1, z2 = split2(z[0:half, :]), split2(z[half:total, :])
     zd = split2(z[total:, :])
     top = [jnp.concatenate([p, q], axis=0) for p, q in zip(z1, zd)]
-    gram1 = product(top, z1, NT)
-    gram2 = product(top, z2, NT)
+    return product(top, z1, NT), product(top, z2, NT), product(z2, z2, NT)
+
+
+def near_kernel(per_patch, slots, own, odd_z, even_z, within, across, gram1, gram2, gram3, z):
+    tiles = ((0, 0, own, 0), (0, -1, odd_z, 0), (0, 1, even_z, 0), (-1, 0, across, 0), (1, 0, within, 0))
+    fill(z, slots, per_patch, tiles)
+    gram1[...], gram2[...], gram3[...] = gram_blocks(z, 2 * gram3.shape[0])
+
+
+def update_kernel(per_patch, slots, state, centre, near1, near2, near3, within, across, out, z, inv):
+    parts, rows, members, cols = state.shape
+    total = parts * members
+    half = total // 2
+    tiles = (
+        (-1, 1, across, 0),
+        (-1, -1, across, per_patch),
+        (1, 1, within, 0),
+        (1, -1, within, per_patch),
+    )
+    fill(z, slots, per_patch, tiles)
+    gram1, gram2, gram3 = gram_blocks(z, total)
+    gram1, gram2 = gram1 + near1[...], gram2 + near2[...]
     drive = jnp.concatenate([gram1[half:], gram2[half:]], axis=1)
     s11 = gram1[:half] + eye(half)
     s12 = gram2[:half]
-    s22 = product(z2, z2, NT) + eye(half)
+    s22 = gram3 + near3[...] + eye(half)
     inv11 = spd_inverse(s11)
     w = jnp.dot(inv11, s12, precision=HI)
     schur = s22 - lax.dot_general(s12, w, (((0,), (0,)), ((), ())), precision=HI)
@@ -261,17 +279,6 @@
             out[p, i] = result[p * members : (p + 1) * members, i * cols : (i + 1) * cols]
 
 
-def update(per_patch, slots, state, centre, own, odd_z, even_z, across, within, within_c, across_c, *rest):
-    lines = {(0, 0): own, (0, 1): even_z, (0, -1): odd_z, (-1, 0): across, (1, 0): within}
-    corners = {
-        (-1, 1): (across_c, 0),
-        (-1, -1): (across_c, per_patch),
-        (1, 1): (within_c, 0),
-        (1, -1): (within_c, per_patch),
-    }
-    update_kernel(per_patch, slots, state, centre, lines, corners, *rest)
-
-
 VMEM = pl.BlockSpec(memory_space=pltpu.VMEM)
 SMEM = pl.BlockSpec(memory_space=pltpu.SMEM)
 PARAMS = pltpu.CompilerParams(vmem_limit_bytes=28 * 1024 * 1024)
@@ -309,7 +316,7 @@
             pltpu.VMEM(ensemble.shape, jnp.float32),
             pltpu.VMEM(speed_row.shape, jnp.float32),
             pltpu.VMEM(speed_col.shape, jnp.float32),
-            pltpu.SemaphoreType.DMA((3,)),
+            pltpu.SemaphoreType.DMA((groups + 2,)),
         ],
         compiler_params=pltpu.CompilerParams(vmem_limit_bytes=62 * 1024 * 1024),
         name="edges",
@@ -338,23 +345,36 @@
     across = paired(tiles, "space", 1)
     even_z = paired(tiles, "member", 0)
     odd_z = paired(tiles, "member", 1)
-    within, across, even_z, odd_z = lax.optimization_barrier((within, across, even_z, odd_z))
     both_z = jnp.concatenate([even_z, odd_z])
     within_c = paired(both_z, "space", 0)
     across_c = paired(both_z, "space", 1)
     slots = loc_slots[0, 0, 0]
+    half = total // 2
+    depth = per_patch * obs
+    near = pl.pallas_call(
+        functools.partial(near_kernel, per_patch),
+        out_shape=(f32(half + SUB, half), f32(half + SUB, half), f32(half, half)),
+        in_specs=[SMEM] + [VMEM] * 5,
+        out_specs=(VMEM, VMEM, VMEM),
+        scratch_shapes=[pltpu.VMEM((total + SUB, 5 * depth), jnp.float32)],
+        compiler_params=PARAMS,
+        cost_estimate=pl.CostEstimate(
+            flops=240 * total * total * depth, bytes_accessed=12 * (total + SUB) * depth * 4, transcendentals=0
+        ),
+        name="near_gram",
+    )(slots, tiles, odd_z, even_z, within, across)
     state = pl.pallas_call(
-        functools.partial(update, per_patch),
+        functools.partial(update_kernel, per_patch),
         out_shape=f32(parts, rows, members, cols),
-        in_specs=[SMEM] + [VMEM] * 9,
+        in_specs=[SMEM] + [VMEM] * 7,
         out_specs=VMEM,
         scratch_shapes=[
-            pltpu.VMEM((total + SUB, slots.shape[0] * obs), jnp.float32),
+            pltpu.VMEM((total + SUB, 4 * depth), jnp.float32),
             pltpu.VMEM((total, total), jnp.float32),
         ],
         compiler_params=PARAMS,
         name="update",
-    )(slots, state, centre, tiles, odd_z, even_z, across, within, within_c, across_c)
+    )(slots, state, centre, *near, within_c, across_c)
     state = swap(state)
     return state.transpose(2, 1, 0, 3).reshape(members, rows, width)
 

time: 142 us -> 141 us (level)
  the two profiles are of different devices: /device:TPU:55 before, /device:TPU:15 now
where the time goes in v3:
time: 141 us; the launch traced here: 140 us
  blocking collectives  68.8 us (49%)
  waiting for transfers between devices  27.9 us (20%)
  Pallas kernels  21.3 us (15%)
  starting transfers between devices  19.4 us (14%)
  local copies, waits for them, and re-layouts  2.65 us (2%)
    all_to_all x2, blocking collectives, swap(): return lax.all_to_all(x, 'member', split_axis=0, concat_axis=0, tiled=True)  68.8 us
    ppermute x8, waiting for transfers between devices, paired(): return lax.ppermute(x, axis, pairs + [(j, i) for i, j in pairs])  27.9 us
    ppermute x8, starting transfers between devices, paired(): return lax.ppermute(x, axis, pairs + [(j, i) for i, j in pairs])  19.4 us
    pallas_call x1, Pallas kernels, on_device(): pl.pallas_call(functools.partial(update_kernel, per_patch), out_shape=f32...  12.6 us
  transfers between devices with their start and end apart: 8, of which 4 were waited for; matrix products, arithmetic and copies ran while one was open for 0% of the time, Pallas kernels for 2%

profile of v3, /device:TPU:15, one launch (start us, length us, event | category | flops | bytes accessed | tf_op | source)
XLA Modules:
  0.0 140.3 jit_solution(8354429169302278329)
XLA Ops:
  0.0 2.5 %edges.1 = (f32[17,8,1024]{2,1,0:T(8,128)}, f32[17,8,1024]{2,1,0:T(8,128)}) custom-call(f32[64,4,1024]{2,1,0:T(4,128)} %ensemble_far.1, f32[4,1024]{1,0:T(4,128)} %speed_row.1, f32[4,1024]{1,0:T(4,128)} %speed_col.1), custom_call_target="tpu_custom_call" | custom-call | tf_op jit(solution)/shard_map/edges/pallas_call | solution.py:310
  2.5 0.0 copy-start.1
  2.5 3.7 %collective-permute-start = (f32[17,8,1024]{2,1,0:T(8,128)}, f32[17,8,1024]{2,1,0:T(8,128)S(1)}, u32[]{:S(2)}, u32[]{:S(2)}) collective-permute-start(f32[17,8,1024]{2,1,0:T(8,128)} %get-tuple-element.12), channel_id=1, source_target_pairs={{1,2},{3,4},{5,6},{7,8},{9,10},{11,12},{13,14},{15,16},{17,18},{19... | collective-permute-start | bytes 1671176 | tf_op jit(solution)/shard_map/ppermute | solution.py:294
  6.2 1.9 %collective-permute-start.1 = (f32[17,8,1024]{2,1,0:T(8,128)}, f32[17,8,1024]{2,1,0:T(8,128)S(1)}, u32[]{:S(2)}, u32[]{:S(2)}) collective-permute-start(f32[17,8,1024]{2,1,0:T(8,128)} %get-tuple-element.13), channel_id=1, source_target_pairs={{0,1},{2,3},{4,5},{6,7},{8,9},{10,11},{12,13},{14,15},{16,17},{18,... | collective-permute-start | bytes 1671176 | tf_op jit(solution)/shard_map/ppermute | solution.py:294
  8.1 0.6 copy.16
  8.8 6.9 %collective-permute-done.across = f32[17,8,1024]{2,1,0:T(8,128)S(1)} collective-permute-done((f32[17,8,1024]{2,1,0:T(8,128)}, f32[17,8,1024]{2,1,0:T(8,128)S(1)}, u32[]{:S(2)}, u32[]{:S(2)}) %collective-permute-start) | collective-permute-done | bytes 557088 | tf_op jit(solution)/shard_map/ppermute | solution.py:294
  15.7 2.1 %advect.1 = f32[8,4,64,128]{3,2,1,0:T(8,128)S(1)} custom-call(f32[4,64,1024]{2,1,0:T(8,128)S(1)} %bitcast.11, f32[17,8,1024]{2,1,0:T(8,128)S(1)} %collective-permute-done.across, f32[17,8,1024]{2,1,0:T(8,128)S(1)} %collective-permute-done.1.within, f32[4,1024]{1,0:T(4,128)S(1)} %copy-done, f32[4,1024]{1,0:T(4,128)S(1)} %copy-done.1), custom_call_target="tpu_custom_call" | custom-call | tf_op jit(solution)/shard_map/advect/pallas_call | solution.py:326
  17.8 0.0 copy-start.2
  17.8 38.3 %all_to_all.10.state = f32[8,4,64,128]{3,2,1,0:T(8,128)S(1)} all-to-all(f32[8,4,64,128]{3,2,1,0:T(8,128)S(1)} %advect.1), channel_id=1, replica_groups=mesh['member'=8,'space'=64] {'member'}, dimensions={0} | all-to-all | bytes 2097152 | tf_op jit(solution)/shard_map/all_to_all | solution.py:298
  56.1 1.7 %tiles.1 = (f32[2,520,128]{2,1,0:T(8,128)S(1)}, f32[4,128]{1,0:T(4,128)S(1)}) custom-call(s32[2]{0:T(128)S(1)} %bitcast.15, f32[8,4,64,128]{3,2,1,0:T(8,128)S(1)} %all_to_all.10.state, s32[2,128]{1,0:T(2,128)S(1)} %bitcast.12, f32[2,128]{1,0:T(2,128)S(1)} %bitcast.13, f32[2,128]{1,0:T(2,128)S(1)} %bitcast.14), custom_call_target="tpu_custom_call" | custom-call | tf_op jit(solution)/shard_map/tiles/pallas_call | solution.py:336
  57.8 2.2 %collective-permute-start.3 = (f32[2,520,128]{2,1,0:T(8,128)S(1)}, f32[2,520,128]{2,1,0:T(8,128)S(1)}, u32[]{:S(2)}, u32[]{:S(2)}) collective-permute-start(f32[2,520,128]{2,1,0:T(8,128)S(1)} %get-tuple-element.15.own), channel_id=1, source_target_pairs={{0,64},{128,192},{256,320},{384,448},{64,0},{192,128},{320,256},{4... | collective-permute-start | bytes 1597448 | tf_op jit(solution)/shard_map/ppermute | solution.py:294
  60.0 1.9 %collective-permute-start.2 = (f32[2,520,128]{2,1,0:T(8,128)S(1)}, f32[2,520,128]{2,1,0:T(8,128)S(1)}, u32[]{:S(2)}, u32[]{:S(2)}) collective-permute-start(f32[2,520,128]{2,1,0:T(8,128)S(1)} %get-tuple-element.15.own), channel_id=1, source_target_pairs={{64,128},{192,256},{320,384},{448,0},{128,64},{256,192},{384,320},... | collective-permute-start | bytes 1597448 | tf_op jit(solution)/shard_map/ppermute | solution.py:294
  61.9 3.2 %collective-permute-start.5 = (f32[2,520,128]{2,1,0:T(8,128)S(1)}, f32[2,520,128]{2,1,0:T(8,128)S(1)}, u32[]{:S(2)}, u32[]{:S(2)}) collective-permute-start(f32[2,520,128]{2,1,0:T(8,128)S(1)} %get-tuple-element.15.own), channel_id=1, source_target_pairs={{1,2},{3,4},{5,6},{7,8},{9,10},{11,12},{13,14},{15,16},{17,18},{19... | collective-permute-start | bytes 1597448 | tf_op jit(solution)/shard_map/ppermute | solution.py:294
  65.2 1.9 %collective-permute-start.4 = (f32[2,520,128]{2,1,0:T(8,128)S(1)}, f32[2,520,128]{2,1,0:T(8,128)S(1)}, u32[]{:S(2)}, u32[]{:S(2)}) collective-permute-start(f32[2,520,128]{2,1,0:T(8,128)S(1)} %get-tuple-element.15.own), channel_id=1, source_target_pairs={{0,1},{2,3},{4,5},{6,7},{8,9},{10,11},{12,13},{14,15},{16,17},{18,... | collective-permute-start | bytes 1597448 | tf_op jit(solution)/shard_map/ppermute | solution.py:294
  67.1 6.1 %collective-permute-done.3.even_z = f32[2,520,128]{2,1,0:T(8,128)S(1)} collective-permute-done((f32[2,520,128]{2,1,0:T(8,128)S(1)}, f32[2,520,128]{2,1,0:T(8,128)S(1)}, u32[]{:S(2)}, u32[]{:S(2)}) %collective-permute-start.3) | collective-permute-done | bytes 532512 | tf_op jit(solution)/shard_map/ppermute | solution.py:294
  73.2 3.7 %collective-permute-done.2.odd_z = f32[2,520,128]{2,1,0:T(8,128)S(1)} collective-permute-done((f32[2,520,128]{2,1,0:T(8,128)S(1)}, f32[2,520,128]{2,1,0:T(8,128)S(1)}, u32[]{:S(2)}, u32[]{:S(2)}) %collective-permute-start.2) | collective-permute-done | bytes 532512 | tf_op jit(solution)/shard_map/ppermute | solution.py:294
  76.9 1.9 %collective-permute-start.7 = (f32[4,520,128]{2,1,0:T(8,128)S(1)}, f32[4,520,128]{2,1,0:T(8,128)S(1)}, u32[]{:S(2)}, u32[]{:S(2)}) collective-permute-start(f32[4,520,128]{2,1,0:T(8,128)S(1)} %constant_dynamic-update-slice_fusion), channel_id=1, source_target_pairs={{1,2},{3,4},{5,6},{7,8},{9,10},{11,12},{13,14},{15,16},{17,18},{19... | collective-permute-start | bytes 3194888 | tf_op jit(solution)/shard_map/ppermute | solution.py:294
  78.8 2.7 %collective-permute-start.6 = (f32[4,520,128]{2,1,0:T(8,128)S(1)}, f32[4,520,128]{2,1,0:T(8,128)S(1)}, u32[]{:S(2)}, u32[]{:S(2)}) collective-permute-start(f32[4,520,128]{2,1,0:T(8,128)S(1)} %constant_dynamic-update-slice_fusion), channel_id=1, source_target_pairs={{0,1},{2,3},{4,5},{6,7},{8,9},{10,11},{12,13},{14,15},{16,17},{18,... | collective-permute-start | bytes 3194888 | tf_op jit(solution)/shard_map/ppermute | solution.py:294
  81.5 2.5 %near_gram.1 = (f32[264,256]{1,0:T(8,128)S(1)}, f32[264,256]{1,0:T(8,128)S(1)}, f32[256,256]{1,0:T(8,128)S(1)}) custom-call(s32[12]{0:T(128)S(1)} %bitcast.16, f32[2,520,128]{2,1,0:T(8,128)S(1)} %get-tuple-element.15.own, f32[2,520,128]{2,1,0:T(8,128)S(1)} %collective-permute-done.2.odd_z, f32[2,520,128]{2,1,0:T(8,128)S(1)} %collective-permute-done.3.even_z, ...), custom_call_target="tpu_custom_call" | custom-call | flops 16106127360 | bytes 6389760 | tf_op jit(solution)/shard_map/near_gram/pallas_call | solution.py:354
  84.0 11.3 %collective-permute-done.7.across = f32[4,520,128]{2,1,0:T(8,128)S(1)} collective-permute-done((f32[4,520,128]{2,1,0:T(8,128)S(1)}, f32[4,520,128]{2,1,0:T(8,128)S(1)}, u32[]{:S(2)}, u32[]{:S(2)}) %collective-permute-start.7) | collective-permute-done | bytes 1064992 | tf_op jit(solution)/shard_map/ppermute | solution.py:294
  95.3 12.6 %update.1 = f32[8,4,64,128]{3,2,1,0:T(8,128)S(1)} custom-call(s32[12]{0:T(128)S(1)} %bitcast.17, f32[8,4,64,128]{3,2,1,0:T(8,128)S(1)} %all_to_all.10.state, f32[4,128]{1,0:T(4,128)S(1)} %get-tuple-element.14.centre, f32[264,256]{1,0:T(8,128)S(1)} %get-tuple-element.16.near1, f32[264,256]{1,0:T(8,128)S(1)} %get-tuple-element.17.near2, ...), custom_call_target="tpu_custom_call" | custom-call | tf_op jit(solution)/shard_map/update/pallas_call | solution.py:366
  107.9 30.5 %all_to_all.11 = f32[8,4,64,128]{3,2,1,0:T(8,128)S(1)} all-to-all(f32[8,4,64,128]{3,2,1,0:T(8,128)S(1)} %update.1), channel_id=1, replica_groups=mesh['member'=8,'space'=64] {'member'}, dimensions={0} | all-to-all | bytes 2097152 | tf_op jit(solution)/shard_map/all_to_all | solution.py:298
  138.4 0.6 copy.13
  139.0 1.3 reshape.4
  (20 shorter events, 0.1 us)
Async XLA Ops:
  0.0 8.1 %copy-start.7 = (f32[64,4,1024]{2,1,0:T(4,128)S(1)}, f32[64,4,1024]{2,1,0:T(4,128)}, u32[]{:S(2)}) copy-start(f32[64,4,1024]{2,1,0:T(4,128)} %ensemble_far.1) | copy-start | bytes 3145732
  2.5 13.2 %copy-start = (f32[4,1024]{1,0:T(4,128)S(1)}, f32[4,1024]{1,0:T(4,128)}, u32[]{:S(2)}) copy-start(f32[4,1024]{1,0:T(4,128)} %speed_row.1) | copy-start | bytes 49156
  2.5 13.2 %copy-start.1 = (f32[4,1024]{1,0:T(4,128)S(1)}, f32[4,1024]{1,0:T(4,128)}, u32[]{:S(2)}) copy-start(f32[4,1024]{1,0:T(4,128)} %speed_col.1) | copy-start | bytes 49156
  2.5 13.2 %collective-permute-start = (f32[17,8,1024]{2,1,0:T(8,128)}, f32[17,8,1024]{2,1,0:T(8,128)S(1)}, u32[]{:S(2)}, u32[]{:S(2)}) collective-permute-start(f32[17,8,1024]{2,1,0:T(8,128)} %get-tuple-element.12), channel_id=1, source_target_pairs={{1,2},{3,4},{5,6},{7,8},{9,10},{11,12},{13,14},{15,16},{17,18},{19... | collective-permute-start | bytes 1671176 | tf_op jit(solution)/shard_map/ppermute | solution.py:294
  6.2 9.5 %collective-permute-start.1 = (f32[17,8,1024]{2,1,0:T(8,128)}, f32[17,8,1024]{2,1,0:T(8,128)S(1)}, u32[]{:S(2)}, u32[]{:S(2)}) collective-permute-start(f32[17,8,1024]{2,1,0:T(8,128)} %get-tuple-element.13), channel_id=1, source_target_pairs={{0,1},{2,3},{4,5},{6,7},{8,9},{10,11},{12,13},{14,15},{16,17},{18,... | collective-permute-start | bytes 1671176 | tf_op jit(solution)/shard_map/ppermute | solution.py:294
  17.8 38.3 %copy-start.2 = (s32[1,1,1,2,128]{4,3,2,1,0:T(2,128)S(1)}, s32[1,1,1,2,128]{4,3,2,1,0:T(2,128)}, u32[]{:S(2)}) copy-start(s32[1,1,1,2,128]{4,3,2,1,0:T(2,128)} %param.11) | copy-start | bytes 3076
  17.8 38.3 %copy-start.3 = (f32[1,1,1,2,128]{4,3,2,1,0:T(2,128)S(1)}, f32[1,1,1,2,128]{4,3,2,1,0:T(2,128)}, u32[]{:S(2)}) copy-start(f32[1,1,1,2,128]{4,3,2,1,0:T(2,128)} %param.12) | copy-start | bytes 3076
  17.8 38.3 %copy-start.4 = (f32[1,1,1,2,128]{4,3,2,1,0:T(2,128)S(1)}, f32[1,1,1,2,128]{4,3,2,1,0:T(2,128)}, u32[]{:S(2)}) copy-start(f32[1,1,1,2,128]{4,3,2,1,0:T(2,128)} %param.13) | copy-start | bytes 3076
  17.8 38.3 %copy-start.5 = (s32[1,1,1,2]{3,2,1,0:T(1,128)S(1)}, s32[1,1,1,2]{3,2,1,0:T(1,128)}, u32[]{:S(2)}) copy-start(s32[1,1,1,2]{3,2,1,0:T(1,128)} %param.14) | copy-start | bytes 28
  57.8 23.7 %copy-start.6 = (s32[1,1,1,12]{3,2,1,0:T(1,128)S(1)}, s32[1,1,1,12]{3,2,1,0:T(1,128)}, u32[]{:S(2)}) copy-start(s32[1,1,1,12]{3,2,1,0:T(1,128)} %param.15) | copy-start | bytes 148
  57.8 15.3 %collective-permute-start.3 = (f32[2,520,128]{2,1,0:T(8,128)S(1)}, f32[2,520,128]{2,1,0:T(8,128)S(1)}, u32[]{:S(2)}, u32[]{:S(2)}) collective-permute-start(f32[2,520,128]{2,1,0:T(8,128)S(1)} %get-tuple-element.15.own), channel_id=1, source_target_pairs={{0,64},{128,192},{256,320},{384,448},{64,0},{192,128},{320,256},{4... | collective-permute-start | bytes 1597448 | tf_op jit(solution)/shard_map/ppermute | solution.py:294
  60.0 16.9 %collective-permute-start.2 = (f32[2,520,128]{2,1,0:T(8,128)S(1)}, f32[2,520,128]{2,1,0:T(8,128)S(1)}, u32[]{:S(2)}, u32[]{:S(2)}) collective-permute-start(f32[2,520,128]{2,1,0:T(8,128)S(1)} %get-tuple-element.15.own), channel_id=1, source_target_pairs={{64,128},{192,256},{320,384},{448,0},{128,64},{256,192},{384,320},... | collective-permute-start | bytes 1597448 | tf_op jit(solution)/shard_map/ppermute | solution.py:294
  61.9 19.6 %collective-permute-start.5 = (f32[2,520,128]{2,1,0:T(8,128)S(1)}, f32[2,520,128]{2,1,0:T(8,128)S(1)}, u32[]{:S(2)}, u32[]{:S(2)}) collective-permute-start(f32[2,520,128]{2,1,0:T(8,128)S(1)} %get-tuple-element.15.own), channel_id=1, source_target_pairs={{1,2},{3,4},{5,6},{7,8},{9,10},{11,12},{13,14},{15,16},{17,18},{19... | collective-permute-start | bytes 1597448 | tf_op jit(solution)/shard_map/ppermute | solution.py:294
  65.2 16.3 %collective-permute-start.4 = (f32[2,520,128]{2,1,0:T(8,128)S(1)}, f32[2,520,128]{2,1,0:T(8,128)S(1)}, u32[]{:S(2)}, u32[]{:S(2)}) collective-permute-start(f32[2,520,128]{2,1,0:T(8,128)S(1)} %get-tuple-element.15.own), channel_id=1, source_target_pairs={{0,1},{2,3},{4,5},{6,7},{8,9},{10,11},{12,13},{14,15},{16,17},{18,... | collective-permute-start | bytes 1597448 | tf_op jit(solution)/shard_map/ppermute | solution.py:294
  76.9 18.4 %collective-permute-start.7 = (f32[4,520,128]{2,1,0:T(8,128)S(1)}, f32[4,520,128]{2,1,0:T(8,128)S(1)}, u32[]{:S(2)}, u32[]{:S(2)}) collective-permute-start(f32[4,520,128]{2,1,0:T(8,128)S(1)} %constant_dynamic-update-slice_fusion), channel_id=1, source_target_pairs={{1,2},{3,4},{5,6},{7,8},{9,10},{11,12},{13,14},{15,16},{17,18},{19... | collective-permute-start | bytes 3194888 | tf_op jit(solution)/shard_map/ppermute | solution.py:294
  78.8 16.5 %collective-permute-start.6 = (f32[4,520,128]{2,1,0:T(8,128)S(1)}, f32[4,520,128]{2,1,0:T(8,128)S(1)}, u32[]{:S(2)}, u32[]{:S(2)}) collective-permute-start(f32[4,520,128]{2,1,0:T(8,128)S(1)} %constant_dynamic-update-slice_fusion), channel_id=1, source_target_pairs={{0,1},{2,3},{4,5},{6,7},{8,9},{10,11},{12,13},{14,15},{16,17},{18,... | collective-permute-start | bytes 3194888 | tf_op jit(solution)/shard_map/ppermute | solution.py:294

commit v4 on v3

--- a/solution.py
+++ b/solution.py
@@ -145,28 +145,33 @@
     )
 
 
-def tile_kernel(count, state, cell, value, variance, tiles, centre):
-    parts, rows, members, cols = state.shape
+def gather_kernel(state, cell, raw):
+    blocks, rows, members, cols = state.shape
+    per_patch, obs = cell.shape[1:]
+    row = lax.broadcasted_iota(jnp.int32, (rows * cols, obs), 0)
+    for b in range(blocks):
+        x = jnp.concatenate([state[b, i] for i in range(rows)], axis=1)
+        x = jnp.concatenate(split3(x)[::-1], axis=0)
+        pick = [jnp.where(row == cell[b, t : t + 1, :], 1.0, 0.0) for t in range(per_patch)]
+        pick = jnp.concatenate(pick, axis=1).astype(jnp.bfloat16)
+        y = jnp.dot(x, pick, preferred_element_type=jnp.float32)
+        y = y[:members] + y[members : 2 * members] + y[2 * members :]
+        for t in range(per_patch):
+            raw[b, t] = y[:, t * obs : (t + 1) * obs]
+
+
+def tile_kernel(count, raw, value, variance, tiles):
+    parts, per_patch, members, obs = raw.shape
     total = parts * members
-    cells = rows * cols
-    per_patch, obs = cell.shape
-    x = patch_matrix(state)
-    mean = jnp.sum(x, axis=0, keepdims=True) * (1.0 / total)
-    for i in range(rows):
-        centre[i : i + 1, :] = mean[:, i * cols : (i + 1) * cols]
-    anomaly = jnp.concatenate([x - mean, jnp.broadcast_to(mean, (SUB, cells))], axis=0)
-    parts3 = split3(anomaly)
-    row = lax.broadcasted_iota(jnp.int32, (cells, obs), 0)
     lane = lax.broadcasted_iota(jnp.int32, (1, obs), 1)
     below = lax.broadcasted_iota(jnp.int32, (SUB, obs), 0)
     for t in range(per_patch):
-        pick = jnp.where(row == cell[t : t + 1, :], 1.0, 0.0).astype(jnp.bfloat16)
-        y = sum(jnp.dot(p, pick, preferred_element_type=jnp.float32) for p in parts3[::-1])
-        live = lane < count[t]
-        weight = jnp.where(live, 1.0 / variance[t : t + 1, :], 0.0)
+        y = raw[:, t].reshape(total, obs)
+        mean = jnp.sum(y, axis=0, keepdims=True) * (1.0 / total)
+        weight = jnp.where(lane < count[t], 1.0 / variance[t : t + 1, :], 0.0)
         scale = jnp.sqrt(weight * (1.0 / (total - 1.0)))
-        tiles[t, 0:total, :] = y[:total] * scale
-        innovation = (value[t : t + 1, :] - y[total:]) * scale
+        tiles[t, 0:total, :] = (y - mean) * scale
+        innovation = (value[t : t + 1, :] - mean) * scale
         tiles[t, total : total + SUB, :] = jnp.where(below == 0, innovation, 0.0)
 
 
@@ -243,10 +248,9 @@
     gram1[...], gram2[...], gram3[...] = gram_blocks(z, 2 * gram3.shape[0])
 
 
-def update_kernel(per_patch, slots, state, centre, near1, near2, near3, within, across, out, z, inv):
-    parts, rows, members, cols = state.shape
-    total = parts * members
-    half = total // 2
+def weight_kernel(per_patch, slots, near1, near2, near3, within, across, out, z):
+    half = near3.shape[0]
+    total = 2 * half
     tiles = (
         (-1, 1, across, 0),
         (-1, -1, across, per_patch),
@@ -265,15 +269,22 @@
     schur = s22 - lax.dot_general(s12, w, (((0,), (0,)), ((), ())), precision=HI)
     inv22 = spd_inverse(0.5 * (schur + schur.T))
     low = jnp.dot(w, inv22, precision=HI)
-    inv[0:half, 0:half] = inv11 + lax.dot_general(low, w, NT, precision=HI)
-    inv[0:half, half:] = -low
-    inv[half:, 0:half] = -low.T
-    inv[half:, half:] = inv22
-    shift = jnp.dot(drive, inv[...], precision=HI)[0:1]
-    mean = jnp.concatenate([centre[i : i + 1, :] for i in range(rows)], axis=1)
-    anomaly = patch_matrix(state) - mean
-    result = product3(0.5 * inv[...] + shift, anomaly)
-    result = result + (mean + 0.5 * anomaly)
+    inv = jnp.concatenate(
+        [
+            jnp.concatenate([inv11 + lax.dot_general(low, w, NT, precision=HI), -low], axis=1),
+            jnp.concatenate([-low.T, inv22], axis=1),
+        ],
+        axis=0,
+    )
+    out[...] = 0.5 * inv + full(drive, inv)[0:1]
+
+
+def update_kernel(weight, state, out):
+    parts, rows, members, cols = state.shape
+    x = patch_matrix(state)
+    mean = jnp.sum(x, axis=0, keepdims=True) * (1.0 / (parts * members))
+    anomaly = x - mean
+    result = product3(weight[...], anomaly) + (mean + 0.5 * anomaly)
     for p in range(parts):
         for i in range(rows):
             out[p, i] = result[p * members : (p + 1) * members, i * cols : (i + 1) * cols]
@@ -281,7 +292,7 @@
 
 VMEM = pl.BlockSpec(memory_space=pltpu.VMEM)
 SMEM = pl.BlockSpec(memory_space=pltpu.SMEM)
-PARAMS = pltpu.CompilerParams(vmem_limit_bytes=28 * 1024 * 1024)
+PARAMS = pltpu.CompilerParams(vmem_limit_bytes=20 * 1024 * 1024)
 
 
 def f32(*shape):
@@ -332,20 +343,30 @@
         compiler_params=PARAMS,
         name="advect",
     )(planes, across, within, speed_row, speed_col)
-    state = swap(state)
-    tiles, centre = pl.pallas_call(
+    cell = swap(jnp.broadcast_to(obs_cell[0, 0], (parts, per_patch, obs)))
+    raw = pl.pallas_call(
+        gather_kernel,
+        out_shape=f32(parts, per_patch, members, obs),
+        in_specs=[VMEM] * 2,
+        out_specs=VMEM,
+        compiler_params=PARAMS,
+        name="gather",
+    )(state, cell)
+    raw = swap(raw)
+    tiles = pl.pallas_call(
         tile_kernel,
-        out_shape=(f32(per_patch, total + SUB, obs), f32(rows, cols)),
-        in_specs=[SMEM] + [VMEM] * 4,
-        out_specs=(VMEM, VMEM),
+        out_shape=f32(per_patch, total + SUB, obs),
+        in_specs=[SMEM] + [VMEM] * 3,
+        out_specs=VMEM,
         compiler_params=PARAMS,
         name="tiles",
-    )(obs_count[0, 0, 0], state, obs_cell[0, 0, 0], obs_value[0, 0, 0], obs_var[0, 0, 0])
+    )(obs_count[0, 0, 0], raw, obs_value[0, 0, 0], obs_var[0, 0, 0])
     within = paired(tiles, "space", 0)
     across = paired(tiles, "space", 1)
     even_z = paired(tiles, "member", 0)
     odd_z = paired(tiles, "member", 1)
     both_z = jnp.concatenate([even_z, odd_z])
+    state = swap(state)
     within_c = paired(both_z, "space", 0)
     across_c = paired(both_z, "space", 1)
     slots = loc_slots[0, 0, 0]
@@ -363,18 +384,26 @@
         ),
         name="near_gram",
     )(slots, tiles, odd_z, even_z, within, across)
+    weight = pl.pallas_call(
+        functools.partial(weight_kernel, per_patch),
+        out_shape=f32(total, total),
+        in_specs=[SMEM] + [VMEM] * 5,
+        out_specs=VMEM,
+        scratch_shapes=[pltpu.VMEM((total + SUB, 4 * depth), jnp.float32)],
+        compiler_params=PARAMS,
+        cost_estimate=pl.CostEstimate(
+            flops=120 * total * total * depth, bytes_accessed=12 * total * total, transcendentals=0
+        ),
+        name="weights",
+    )(slots, *near, within_c, across_c)
     state = pl.pallas_call(
-        functools.partial(update_kernel, per_patch),
+        update_kernel,
         out_shape=f32(parts, rows, members, cols),
-        in_specs=[SMEM] + [VMEM] * 7,
+        in_specs=[VMEM] * 2,
         out_specs=VMEM,
-        scratch_shapes=[
-            pltpu.VMEM((total + SUB, 4 * depth), jnp.float32),
-            pltpu.VMEM((total, total), jnp.float32),
-        ],
         compiler_params=PARAMS,
         name="update",
-    )(slots, state, centre, *near, within_c, across_c)
+    )(weight, state)
     state = swap(state)
     return state.transpose(2, 1, 0, 3).reshape(members, rows, width)
 

time: 141 us -> 135 us (0.957)
  the two profiles are of different devices: /device:TPU:15 before, /device:TPU:63 now
where the time goes in v4:
time: 135 us; the launch traced here: 134 us
  blocking collectives  53.3 us (39%)
  starting transfers between devices  36.8 us (27%)
  Pallas kernels  24.6 us (18%)
  waiting for transfers between devices  16.2 us (12%)
  local copies, waits for them, and re-layouts  3.23 us (2%)
    all_to_all x2, blocking collectives, swap(): return lax.all_to_all(x, 'member', split_axis=0, concat_axis=0, tiled=True)  53.3 us
    ppermute x8, starting transfers between devices, paired(): return lax.ppermute(x, axis, pairs + [(j, i) for i, j in pairs])  26.9 us
    ppermute x8, waiting for transfers between devices, paired(): return lax.ppermute(x, axis, pairs + [(j, i) for i, j in pairs])  13.3 us
    pallas_call x1, Pallas kernels, on_device(): pl.pallas_call(functools.partial(weight_kernel, per_patch), out_shape=f32...  12.4 us
    all_to_all x2, starting transfers between devices, swap(): return lax.all_to_all(x, 'member', split_axis=0, concat_axis=0, tiled=True)  9.87 us
    pallas_call x1, Pallas kernels, on_device(): pl.pallas_call(advect_kernel, out_shape=f32(parts, rows, members, cols),...  3.05 us
    pallas_call x1, Pallas kernels, on_device(): pl.pallas_call(functools.partial(near_kernel, per_patch), out_shape=(f32(...  2.99 us
    all_to_all x2, waiting for transfers between devices, swap(): return lax.all_to_all(x, 'member', split_axis=0, concat_axis=0, tiled=True)  2.86 us
  transfers between devices with their start and end apart: 10, of which 3 were waited for; matrix products, arithmetic and copies ran while one was open for 1% of the time, Pallas kernels for 14%

profile of v4, /device:TPU:63, one launch (start us, length us, event | category | flops | bytes accessed | tf_op | source)
XLA Modules:
  0.0 134.4 jit_solution(8344555630185126082)
XLA Ops:
  0.0 2.5 %edges.1 = (f32[17,8,1024]{2,1,0:T(8,128)}, f32[17,8,1024]{2,1,0:T(8,128)}) custom-call(f32[64,4,1024]{2,1,0:T(4,128)} %ensemble_far.1, f32[4,1024]{1,0:T(4,128)} %speed_row.1, f32[4,1024]{1,0:T(4,128)} %speed_col.1), custom_call_target="tpu_custom_call" | custom-call | tf_op jit(solution)/shard_map/edges/pallas_call | solution.py:321
  2.5 7.2 %collective-permute-start = (f32[17,8,1024]{2,1,0:T(8,128)}, f32[17,8,1024]{2,1,0:T(8,128)S(1)}, u32[]{:S(2)}, u32[]{:S(2)}) collective-permute-start(f32[17,8,1024]{2,1,0:T(8,128)} %get-tuple-element.10), channel_id=1, source_target_pairs={{1,2},{3,4},{5,6},{7,8},{9,10},{11,12},{13,14},{15,16},{17,18},{19... | collective-permute-start | bytes 1671176 | tf_op jit(solution)/shard_map/ppermute | solution.py:305
  9.8 1.9 %collective-permute-start.1 = (f32[17,8,1024]{2,1,0:T(8,128)}, f32[17,8,1024]{2,1,0:T(8,128)S(1)}, u32[]{:S(2)}, u32[]{:S(2)}) collective-permute-start(f32[17,8,1024]{2,1,0:T(8,128)} %get-tuple-element.11), channel_id=1, source_target_pairs={{0,1},{2,3},{4,5},{6,7},{8,9},{10,11},{12,13},{14,15},{16,17},{18,... | collective-permute-start | bytes 1671176 | tf_op jit(solution)/shard_map/ppermute | solution.py:305
  12.3 5.6 %all-to-all-start = ((s32[8,2,128]{2,1,0:T(2,128)}), s32[8,2,128]{2,1,0:T(2,128)S(1)}, u32[]{:S(2)}, u32[]{:S(2)}) async-start(s32[8,2,128]{2,1,0:T(2,128)} %broadcast_in_dim.8), calls=%async_computation | async-start | bytes 16384 | tf_op jit(solution)/shard_map/all_to_all | solution.py:309
  18.0 0.6 copy.16
  18.6 3.0 %advect.1.state = f32[8,4,64,128]{3,2,1,0:T(8,128)} custom-call(f32[4,64,1024]{2,1,0:T(8,128)S(1)} %bitcast.11, f32[17,8,1024]{2,1,0:T(8,128)S(1)} %collective-permute-done.across, f32[17,8,1024]{2,1,0:T(8,128)S(1)} %collective-permute-done.1.within, f32[4,1024]{1,0:T(4,128)S(1)} %copy-done, f32[4,1024]{1,0:T(4,128)S(1)} %copy-done.1), custom_call_target="tpu_custom_call" | custom-call | tf_op jit(solution)/shard_map/advect/pallas_call | solution.py:337
  21.7 2.9 %all-to-all-done.cell = s32[8,2,128]{2,1,0:T(2,128)S(1)} async-done(((s32[8,2,128]{2,1,0:T(2,128)}), s32[8,2,128]{2,1,0:T(2,128)S(1)}, u32[]{:S(2)}, u32[]{:S(2)}) %all-to-all-start) | async-done | bytes 8224 | tf_op jit(solution)/shard_map/all_to_all | solution.py:309
  24.5 1.9 %gather.1 = f32[8,2,64,128]{3,2,1,0:T(8,128)S(1)} custom-call(f32[8,4,64,128]{3,2,1,0:T(8,128)} %advect.1.state, s32[8,2,128]{2,1,0:T(2,128)S(1)} %all-to-all-done.cell), custom_call_target="tpu_custom_call" | custom-call | tf_op jit(solution)/shard_map/gather/pallas_call | solution.py:347
  26.4 22.7 %all_to_all.20.raw = f32[8,2,64,128]{3,2,1,0:T(8,128)S(1)} all-to-all(f32[8,2,64,128]{3,2,1,0:T(8,128)S(1)} %gather.1), channel_id=1, replica_groups=mesh['member'=8,'space'=64] {'member'}, dimensions={0} | all-to-all | bytes 1048576 | tf_op jit(solution)/shard_map/all_to_all | solution.py:309
  49.2 0.7 tiles.1.own
  49.9 2.2 %collective-permute-start.3 = (f32[2,520,128]{2,1,0:T(8,128)S(1)}, f32[2,520,128]{2,1,0:T(8,128)S(1)}, u32[]{:S(2)}, u32[]{:S(2)}) collective-permute-start(f32[2,520,128]{2,1,0:T(8,128)S(1)} %tiles.1.own), channel_id=1, source_target_pairs={{0,64},{128,192},{256,320},{384,448},{64,0},{192,128},{320,256},{4... | collective-permute-start | bytes 1597448 | tf_op jit(solution)/shard_map/ppermute | solution.py:305
  52.0 1.9 %collective-permute-start.2 = (f32[2,520,128]{2,1,0:T(8,128)S(1)}, f32[2,520,128]{2,1,0:T(8,128)S(1)}, u32[]{:S(2)}, u32[]{:S(2)}) collective-permute-start(f32[2,520,128]{2,1,0:T(8,128)S(1)} %tiles.1.own), channel_id=1, source_target_pairs={{64,128},{192,256},{320,384},{448,0},{128,64},{256,192},{384,320},... | collective-permute-start | bytes 1597448 | tf_op jit(solution)/shard_map/ppermute | solution.py:305
  54.0 6.0 %collective-permute-start.5 = (f32[2,520,128]{2,1,0:T(8,128)S(1)}, f32[2,520,128]{2,1,0:T(8,128)S(1)}, u32[]{:S(2)}, u32[]{:S(2)}) collective-permute-start(f32[2,520,128]{2,1,0:T(8,128)S(1)} %tiles.1.own), channel_id=1, source_target_pairs={{1,2},{3,4},{5,6},{7,8},{9,10},{11,12},{13,14},{15,16},{17,18},{19... | collective-permute-start | bytes 1597448 | tf_op jit(solution)/shard_map/ppermute | solution.py:305
  60.0 1.9 %collective-permute-start.4 = (f32[2,520,128]{2,1,0:T(8,128)S(1)}, f32[2,520,128]{2,1,0:T(8,128)}, u32[]{:S(2)}, u32[]{:S(2)}) collective-permute-start(f32[2,520,128]{2,1,0:T(8,128)S(1)} %tiles.1.own), channel_id=1, source_target_pairs={{0,1},{2,3},{4,5},{6,7},{8,9},{10,11},{12,13},{14,15},{16,17},{18,... | collective-permute-start | bytes 1597448 | tf_op jit(solution)/shard_map/ppermute | solution.py:305
  61.9 4.2 %all-to-all-start.2 = ((f32[8,4,64,128]{3,2,1,0:T(8,128)}), f32[8,4,64,128]{3,2,1,0:T(8,128)S(1)}, u32[]{:S(2)}, u32[]{:S(2)}) async-start(f32[8,4,64,128]{3,2,1,0:T(8,128)} %advect.1.state), calls=%async_computation.2 | async-start | bytes 2097152 | tf_op jit(solution)/shard_map/all_to_all | solution.py:309
  66.2 2.5 %collective-permute-done.2.odd_z = f32[2,520,128]{2,1,0:T(8,128)S(1)} collective-permute-done((f32[2,520,128]{2,1,0:T(8,128)S(1)}, f32[2,520,128]{2,1,0:T(8,128)S(1)}, u32[]{:S(2)}, u32[]{:S(2)}) %collective-permute-start.2) | collective-permute-done | bytes 532512 | tf_op jit(solution)/shard_map/ppermute | solution.py:305
  68.7 3.8 %collective-permute-start.7 = (f32[4,520,128]{2,1,0:T(8,128)S(1)}, f32[4,520,128]{2,1,0:T(8,128)S(1)}, u32[]{:S(2)}, u32[]{:S(2)}) collective-permute-start(f32[4,520,128]{2,1,0:T(8,128)S(1)} %constant_dynamic-update-slice_fusion), channel_id=1, source_target_pairs={{1,2},{3,4},{5,6},{7,8},{9,10},{11,12},{13,14},{15,16},{17,18},{19... | collective-permute-start | bytes 3194888 | tf_op jit(solution)/shard_map/ppermute | solution.py:305
  72.6 1.9 %collective-permute-start.6 = (f32[4,520,128]{2,1,0:T(8,128)S(1)}, f32[4,520,128]{2,1,0:T(8,128)S(1)}, u32[]{:S(2)}, u32[]{:S(2)}) collective-permute-start(f32[4,520,128]{2,1,0:T(8,128)S(1)} %constant_dynamic-update-slice_fusion), channel_id=1, source_target_pairs={{0,1},{2,3},{4,5},{6,7},{8,9},{10,11},{12,13},{14,15},{16,17},{18,... | collective-permute-start | bytes 3194888 | tf_op jit(solution)/shard_map/ppermute | solution.py:305
  74.5 3.0 %near_gram.1 = (f32[264,256]{1,0:T(8,128)S(1)}, f32[264,256]{1,0:T(8,128)S(1)}, f32[256,256]{1,0:T(8,128)S(1)}) custom-call(s32[12]{0:T(128)S(1)} %bitcast.15, f32[2,520,128]{2,1,0:T(8,128)S(1)} %tiles.1.own, f32[2,520,128]{2,1,0:T(8,128)S(1)} %collective-permute-done.2.odd_z, f32[2,520,128]{2,1,0:T(8,128)S(1)} %collective-permute-done.3.even_z, ...), custom_call_target="tpu_custom_call" | custom-call | flops 16106127360 | bytes 6389760 | tf_op jit(solution)/shard_map/near_gram/pallas_call | solution.py:375
  77.5 10.8 %collective-permute-done.7.across = f32[4,520,128]{2,1,0:T(8,128)S(1)} collective-permute-done((f32[4,520,128]{2,1,0:T(8,128)S(1)}, f32[4,520,128]{2,1,0:T(8,128)S(1)}, u32[]{:S(2)}, u32[]{:S(2)}) %collective-permute-start.7) | collective-permute-done | bytes 1064992 | tf_op jit(solution)/shard_map/ppermute | solution.py:305
  88.3 12.4 %weights.1.weight = f32[512,512]{1,0:T(8,128)S(1)} custom-call(s32[12]{0:T(128)S(1)} %bitcast.16, f32[264,256]{1,0:T(8,128)S(1)} %get-tuple-element.12.near1, f32[264,256]{1,0:T(8,128)S(1)} %get-tuple-element.13.near2, f32[256,256]{1,0:T(8,128)S(1)} %get-tuple-element.14.near3, f32[4,520,128]{2,1,0:T(8,128)S(1)} %collective-permute-done.6.within, ...), custom_call_target="tpu_custom_call" | custom-call | flops 8053063680 | bytes 3145728 | tf_op jit(solution)/shard_map/weights/pallas_call | solution.py:387
  100.8 1.1 update.1
  101.9 30.6 %all_to_all.21 = f32[8,4,64,128]{3,2,1,0:T(8,128)S(1)} all-to-all(f32[8,4,64,128]{3,2,1,0:T(8,128)S(1)} %update.1), channel_id=1, replica_groups=mesh['member'=8,'space'=64] {'member'}, dimensions={0} | all-to-all | bytes 2097152 | tf_op jit(solution)/shard_map/all_to_all | solution.py:309
  133.1 1.3 reshape.5
  (27 shorter events, 1.3 us)
Async XLA Ops:
  0.0 17.9 %copy-start.6 = (f32[64,4,1024]{2,1,0:T(4,128)S(1)}, f32[64,4,1024]{2,1,0:T(4,128)}, u32[]{:S(2)}) copy-start(f32[64,4,1024]{2,1,0:T(4,128)} %ensemble_far.1) | copy-start | bytes 3145732
  0.0 11.7 %copy-start.7 = (s32[1,1,1,2,128]{4,3,2,1,0:T(2,128)S(1)}, s32[1,1,1,2,128]{4,3,2,1,0:T(2,128)}, u32[]{:S(2)}) copy-start(s32[1,1,1,2,128]{4,3,2,1,0:T(2,128)} %param.11) | copy-start | bytes 3076
  2.5 16.1 %copy-start = (f32[4,1024]{1,0:T(4,128)S(1)}, f32[4,1024]{1,0:T(4,128)}, u32[]{:S(2)}) copy-start(f32[4,1024]{1,0:T(4,128)} %speed_row.1) | copy-start | bytes 49156
  2.5 16.1 %copy-start.1 = (f32[4,1024]{1,0:T(4,128)S(1)}, f32[4,1024]{1,0:T(4,128)}, u32[]{:S(2)}) copy-start(f32[4,1024]{1,0:T(4,128)} %speed_col.1) | copy-start | bytes 49156
  2.5 16.0 %collective-permute-start = (f32[17,8,1024]{2,1,0:T(8,128)}, f32[17,8,1024]{2,1,0:T(8,128)S(1)}, u32[]{:S(2)}, u32[]{:S(2)}) collective-permute-start(f32[17,8,1024]{2,1,0:T(8,128)} %get-tuple-element.10), channel_id=1, source_target_pairs={{1,2},{3,4},{5,6},{7,8},{9,10},{11,12},{13,14},{15,16},{17,18},{19... | collective-permute-start | bytes 1671176 | tf_op jit(solution)/shard_map/ppermute | solution.py:305
  9.8 8.8 %collective-permute-start.1 = (f32[17,8,1024]{2,1,0:T(8,128)}, f32[17,8,1024]{2,1,0:T(8,128)S(1)}, u32[]{:S(2)}, u32[]{:S(2)}) collective-permute-start(f32[17,8,1024]{2,1,0:T(8,128)} %get-tuple-element.11), channel_id=1, source_target_pairs={{0,1},{2,3},{4,5},{6,7},{8,9},{10,11},{12,13},{14,15},{16,17},{18,... | collective-permute-start | bytes 1671176 | tf_op jit(solution)/shard_map/ppermute | solution.py:305
  12.3 12.2 %all-to-all-start = ((s32[8,2,128]{2,1,0:T(2,128)}), s32[8,2,128]{2,1,0:T(2,128)S(1)}, u32[]{:S(2)}, u32[]{:S(2)}) async-start(s32[8,2,128]{2,1,0:T(2,128)} %broadcast_in_dim.8), calls=%async_computation | async-start | bytes 16384 | tf_op jit(solution)/shard_map/all_to_all | solution.py:309
  21.7 27.5 %copy-start.2 = (f32[1,1,1,2,128]{4,3,2,1,0:T(2,128)S(1)}, f32[1,1,1,2,128]{4,3,2,1,0:T(2,128)}, u32[]{:S(2)}) copy-start(f32[1,1,1,2,128]{4,3,2,1,0:T(2,128)} %param.12) | copy-start | bytes 3076
  21.7 27.5 %copy-start.3 = (f32[1,1,1,2,128]{4,3,2,1,0:T(2,128)S(1)}, f32[1,1,1,2,128]{4,3,2,1,0:T(2,128)}, u32[]{:S(2)}) copy-start(f32[1,1,1,2,128]{4,3,2,1,0:T(2,128)} %param.13) | copy-start | bytes 3076
  21.7 27.5 %copy-start.4 = (s32[1,1,1,2]{3,2,1,0:T(1,128)S(1)}, s32[1,1,1,2]{3,2,1,0:T(1,128)}, u32[]{:S(2)}) copy-start(s32[1,1,1,2]{3,2,1,0:T(1,128)} %param.14) | copy-start | bytes 28
  49.9 16.3 %collective-permute-start.3 = (f32[2,520,128]{2,1,0:T(8,128)S(1)}, f32[2,520,128]{2,1,0:T(8,128)S(1)}, u32[]{:S(2)}, u32[]{:S(2)}) collective-permute-start(f32[2,520,128]{2,1,0:T(8,128)S(1)} %tiles.1.own), channel_id=1, source_target_pairs={{0,64},{128,192},{256,320},{384,448},{64,0},{192,128},{320,256},{4... | collective-permute-start | bytes 1597448 | tf_op jit(solution)/shard_map/ppermute | solution.py:305
  52.0 16.7 %collective-permute-start.2 = (f32[2,520,128]{2,1,0:T(8,128)S(1)}, f32[2,520,128]{2,1,0:T(8,128)S(1)}, u32[]{:S(2)}, u32[]{:S(2)}) collective-permute-start(f32[2,520,128]{2,1,0:T(8,128)S(1)} %tiles.1.own), channel_id=1, source_target_pairs={{64,128},{192,256},{320,384},{448,0},{128,64},{256,192},{384,320},... | collective-permute-start | bytes 1597448 | tf_op jit(solution)/shard_map/ppermute | solution.py:305
  54.0 20.5 %collective-permute-start.5 = (f32[2,520,128]{2,1,0:T(8,128)S(1)}, f32[2,520,128]{2,1,0:T(8,128)S(1)}, u32[]{:S(2)}, u32[]{:S(2)}) collective-permute-start(f32[2,520,128]{2,1,0:T(8,128)S(1)} %tiles.1.own), channel_id=1, source_target_pairs={{1,2},{3,4},{5,6},{7,8},{9,10},{11,12},{13,14},{15,16},{17,18},{19... | collective-permute-start | bytes 1597448 | tf_op jit(solution)/shard_map/ppermute | solution.py:305
  60.0 14.5 %collective-permute-start.4 = (f32[2,520,128]{2,1,0:T(8,128)S(1)}, f32[2,520,128]{2,1,0:T(8,128)}, u32[]{:S(2)}, u32[]{:S(2)}) collective-permute-start(f32[2,520,128]{2,1,0:T(8,128)S(1)} %tiles.1.own), channel_id=1, source_target_pairs={{0,1},{2,3},{4,5},{6,7},{8,9},{10,11},{12,13},{14,15},{16,17},{18,... | collective-permute-start | bytes 1597448 | tf_op jit(solution)/shard_map/ppermute | solution.py:305
  61.9 38.9 %all-to-all-start.2 = ((f32[8,4,64,128]{3,2,1,0:T(8,128)}), f32[8,4,64,128]{3,2,1,0:T(8,128)S(1)}, u32[]{:S(2)}, u32[]{:S(2)}) async-start(f32[8,4,64,128]{3,2,1,0:T(8,128)} %advect.1.state), calls=%async_computation.2 | async-start | bytes 2097152 | tf_op jit(solution)/shard_map/all_to_all | solution.py:309
  66.1 8.4 %copy-start.5 = (s32[1,1,1,12]{3,2,1,0:T(1,128)S(1)}, s32[1,1,1,12]{3,2,1,0:T(1,128)}, u32[]{:S(2)}) copy-start(s32[1,1,1,12]{3,2,1,0:T(1,128)} %param.15) | copy-start | bytes 148
  68.7 19.6 %collective-permute-start.7 = (f32[4,520,128]{2,1,0:T(8,128)S(1)}, f32[4,520,128]{2,1,0:T(8,128)S(1)}, u32[]{:S(2)}, u32[]{:S(2)}) collective-permute-start(f32[4,520,128]{2,1,0:T(8,128)S(1)} %constant_dynamic-update-slice_fusion), channel_id=1, source_target_pairs={{1,2},{3,4},{5,6},{7,8},{9,10},{11,12},{13,14},{15,16},{17,18},{19... | collective-permute-start | bytes 3194888 | tf_op jit(solution)/shard_map/ppermute | solution.py:305
  72.6 15.8 %collective-permute-start.6 = (f32[4,520,128]{2,1,0:T(8,128)S(1)}, f32[4,520,128]{2,1,0:T(8,128)S(1)}, u32[]{:S(2)}, u32[]{:S(2)}) collective-permute-start(f32[4,520,128]{2,1,0:T(8,128)S(1)} %constant_dynamic-update-slice_fusion), channel_id=1, source_target_pairs={{0,1},{2,3},{4,5},{6,7},{8,9},{10,11},{12,13},{14,15},{16,17},{18,... | collective-permute-start | bytes 3194888 | tf_op jit(solution)/shard_map/ppermute | solution.py:305

commit v5 on v4

--- a/solution.py
+++ b/solution.py
@@ -86,7 +86,7 @@
         put((2 * groups, slice(n, n + 1)), speed[0:1], speed[rows - 1 : rows])
 
 
-def advect_kernel(planes, across, within, speed_row, speed_col, out, coef):
+def advect_kernel(planes, across, within, speed_row, speed_col, out, far, coef, done):
     rows, members, width = planes.shape
     blocks = out.shape[0]
     cols = out.shape[3]
@@ -133,9 +133,16 @@
         for i in range(rows):
             for b in range(blocks):
                 out[b, i, at, :] = field[i][:, b * cols : (b + 1) * cols]
+        store(g).start()
         return carry
 
+    def store(g):
+        at = pl.ds(pl.multiple_of(g * SUB, SUB), SUB)
+        return pltpu.make_async_copy(out.at[:, :, at, :], far.at[:, :, at, :], done.at[g])
+
     lax.fori_loop(0, groups, body, 0)
+    for g in range(groups):
+        store(g).wait()
 
 
 def patch_matrix(state):
@@ -186,13 +193,20 @@
     e = unit - scale * s
     rho = (bound - 1.0) / (bound + 1.0)
 
-    def square(multiply, carry):
+    def quick_pair(x, e):
+        e = split2(e)
+        return product(split2(x), e), product(e, e)
+
+    def full_pair(x, e):
+        return full(x, e), full(e, e)
+
+    def square(pair, carry):
         x, e, rho = carry
-        both = multiply(jnp.concatenate([x, e], axis=0), e)
+        x_more, e_more = pair(x, e)
         square_rho = rho * rho
         scale = 2.0 / (2.0 - square_rho)
-        x = scale * (x + both[:n])
-        e = scale * both[n:] + (1.0 - scale) * unit
+        x = scale * (x + x_more)
+        e = scale * e_more + (1.0 - scale) * unit
         return x, e, square_rho / (2.0 - square_rho)
 
     def quick(carry):
@@ -201,8 +215,8 @@
     def careful(carry):
         return carry[2] > 1e-3
 
-    carry = lax.while_loop(quick, functools.partial(square, product3), (x, e, rho))
-    x = lax.while_loop(careful, functools.partial(square, full), carry)[0]
+    carry = lax.while_loop(quick, functools.partial(square, quick_pair), (x, e, rho))
+    x = lax.while_loop(careful, functools.partial(square, full_pair), carry)[0]
 
     def unsettled(carry):
         return (carry[1] > 1e-5) & (carry[2] < 8)
@@ -290,7 +304,23 @@
             out[p, i] = result[p * members : (p + 1) * members, i * cols : (i + 1) * cols]
 
 
+def output_kernel(state, out, near, done):
+    blocks, rows, members, cols = state.shape
+    step = members // done.shape[0]
+    copies = []
+    for g in range(done.shape[0]):
+        at = pl.ds(g * step, step)
+        for b in range(blocks):
+            for i in range(rows):
+                near[at, i, b * cols : (b + 1) * cols] = state[b, i, at]
+        copies.append(pltpu.make_async_copy(near.at[at], out.at[at], done.at[g]))
+        copies[-1].start()
+    for copy in copies:
+        copy.wait()
+
+
 VMEM = pl.BlockSpec(memory_space=pltpu.VMEM)
+HBM = pl.BlockSpec(memory_space=pltpu.HBM)
 SMEM = pl.BlockSpec(memory_space=pltpu.SMEM)
 PARAMS = pltpu.CompilerParams(vmem_limit_bytes=20 * 1024 * 1024)
 
@@ -321,7 +351,7 @@
     across, within = pl.pallas_call(
         edge_kernel,
         out_shape=(f32(2 * groups + 1, SUB, width), f32(2 * groups + 1, SUB, width)),
-        in_specs=[pl.BlockSpec(memory_space=pltpu.HBM)] * 3,
+        in_specs=[HBM] * 3,
         out_specs=(VMEM, VMEM),
         scratch_shapes=[
             pltpu.VMEM(ensemble.shape, jnp.float32),
@@ -334,12 +364,15 @@
     )(ensemble, speed_row, speed_col)
     across = paired(across, "space", 1)
     within = paired(within, "space", 0)
-    state = pl.pallas_call(
+    fresh, state = pl.pallas_call(
         advect_kernel,
-        out_shape=f32(parts, rows, members, cols),
+        out_shape=(f32(parts, rows, members, cols), f32(parts, rows, members, cols)),
         in_specs=[VMEM] * 5,
-        out_specs=VMEM,
-        scratch_shapes=[pltpu.VMEM((rows + 2, 4, SUB, width), jnp.float32)],
+        out_specs=(VMEM, HBM),
+        scratch_shapes=[
+            pltpu.VMEM((rows + 2, 4, SUB, width), jnp.float32),
+            pltpu.SemaphoreType.DMA((groups,)),
+        ],
         compiler_params=PARAMS,
         name="advect",
     )(planes, across, within, speed_row, speed_col)
@@ -351,7 +384,7 @@
         out_specs=VMEM,
         compiler_params=PARAMS,
         name="gather",
-    )(state, cell)
+    )(fresh, cell)
     raw = swap(raw)
     tiles = pl.pallas_call(
         tile_kernel,
@@ -405,7 +438,18 @@
         name="update",
     )(weight, state)
     state = swap(state)
-    return state.transpose(2, 1, 0, 3).reshape(members, rows, width)
+    return pl.pallas_call(
+        output_kernel,
+        out_shape=f32(members, rows, width),
+        in_specs=[VMEM],
+        out_specs=HBM,
+        scratch_shapes=[
+            pltpu.VMEM((members, rows, width), jnp.float32),
+            pltpu.SemaphoreType.DMA((4,)),
+        ],
+        compiler_params=PARAMS,
+        name="output",
+    )(state)
 
 
 def solution(mesh):

time: 135 us -> 133 us (0.985)
  local copies, waits for them, and re-layouts: 3.23 us -> 1.32 us
    reshape x2 -> x0, local copies, waits for them, and re-layouts: 1.92 us -> none  [on_device(): return state.transpose(2, 1, 0, 3).reshape(members, rows, width)]
    pallas_call x1 -> x2, Pallas kernels: 3.05 us -> 4.34 us  [the longest x1 2.81 us: on_device(): pl.pallas_call(advect_kernel, out_shape=(f32(parts, rows, members, cols),...]
  transfers between devices with their start and end apart: 10 -> 10, of which waited for: 3 -> 3; matrix products, arithmetic and copies ran while one was open for 1% -> 1% of each run, Pallas kernels for 14% -> 13%
where the time goes in v5:
time: 133 us
  blocking collectives  54 us (41%)
  starting transfers between devices  36.8 us (28%)
  Pallas kernels  23.9 us (18%)
  waiting for transfers between devices  16.4 us (12%)
    all_to_all x2, blocking collectives, swap(): return lax.all_to_all(x, 'member', split_axis=0, concat_axis=0, tiled=True)  54 us
    ppermute x8, starting transfers between devices, paired(): return lax.ppermute(x, axis, pairs + [(j, i) for i, j in pairs])  26.9 us
    ppermute x8, waiting for transfers between devices, paired(): return lax.ppermute(x, axis, pairs + [(j, i) for i, j in pairs])  13.3 us
    pallas_call x1, Pallas kernels, on_device(): pl.pallas_call(functools.partial(weight_kernel, per_patch), out_shape=f32...  11.6 us
    all_to_all x2, starting transfers between devices, swap(): return lax.all_to_all(x, 'member', split_axis=0, concat_axis=0, tiled=True)  9.86 us
    all_to_all x2, waiting for transfers between devices, swap(): return lax.all_to_all(x, 'member', split_axis=0, concat_axis=0, tiled=True)  3.09 us
    pallas_call x1, Pallas kernels, on_device(): pl.pallas_call(functools.partial(near_kernel, per_patch), out_shape=(f32(...  3 us
    pallas_call x1, Pallas kernels, on_device(): pl.pallas_call(advect_kernel, out_shape=(f32(parts, rows, members, cols),...  2.81 us
  transfers between devices with their start and end apart: 10, of which 3 were waited for; matrix products, arithmetic and copies ran while one was open for 1% of the time, Pallas kernels for 13%

profile of v5, /device:TPU:63, one launch (start us, length us, event | category | flops | bytes accessed | tf_op | source)
XLA Modules:
  0.0 132.8 jit_solution(15625722262525197428)
XLA Ops:
  0.0 2.5 %edges.1 = (f32[17,8,1024]{2,1,0:T(8,128)}, f32[17,8,1024]{2,1,0:T(8,128)}) custom-call(f32[64,4,1024]{2,1,0:T(4,128)} %ensemble_far.1, f32[4,1024]{1,0:T(4,128)} %speed_row.1, f32[4,1024]{1,0:T(4,128)} %speed_col.1), custom_call_target="tpu_custom_call" | custom-call | tf_op jit(solution)/shard_map/edges/pallas_call | solution.py:351
  2.5 7.2 %collective-permute-start = (f32[17,8,1024]{2,1,0:T(8,128)}, f32[17,8,1024]{2,1,0:T(8,128)S(1)}, u32[]{:S(2)}, u32[]{:S(2)}) collective-permute-start(f32[17,8,1024]{2,1,0:T(8,128)} %get-tuple-element.12), channel_id=1, source_target_pairs={{1,2},{3,4},{5,6},{7,8},{9,10},{11,12},{13,14},{15,16},{17,18},{19... | collective-permute-start | bytes 1671176 | tf_op jit(solution)/shard_map/ppermute | solution.py:335
  9.8 1.9 %collective-permute-start.1 = (f32[17,8,1024]{2,1,0:T(8,128)}, f32[17,8,1024]{2,1,0:T(8,128)S(1)}, u32[]{:S(2)}, u32[]{:S(2)}) collective-permute-start(f32[17,8,1024]{2,1,0:T(8,128)} %get-tuple-element.13), channel_id=1, source_target_pairs={{0,1},{2,3},{4,5},{6,7},{8,9},{10,11},{12,13},{14,15},{16,17},{18,... | collective-permute-start | bytes 1671176 | tf_op jit(solution)/shard_map/ppermute | solution.py:335
  12.3 5.6 %all-to-all-start = ((s32[8,2,128]{2,1,0:T(2,128)}), s32[8,2,128]{2,1,0:T(2,128)S(1)}, u32[]{:S(2)}, u32[]{:S(2)}) async-start(s32[8,2,128]{2,1,0:T(2,128)} %broadcast_in_dim.8), calls=%async_computation | async-start | bytes 16384 | tf_op jit(solution)/shard_map/all_to_all | solution.py:339
  18.0 0.6 copy.11
  18.6 2.8 %advect.1 = (f32[8,4,64,128]{3,2,1,0:T(8,128)S(1)}, f32[8,4,64,128]{3,2,1,0:T(8,128)}) custom-call(f32[4,64,1024]{2,1,0:T(8,128)S(1)} %bitcast.8, f32[17,8,1024]{2,1,0:T(8,128)S(1)} %collective-permute-done.across, f32[17,8,1024]{2,1,0:T(8,128)S(1)} %collective-permute-done.1.within, f32[4,1024]{1,0:T(4,128)S(1)} %copy-done, f32[4,1024]{1,0:T(4,128)S(1)} %copy-done.1), custom_call_target="tpu_custom_call" | custom-call | tf_op jit(solution)/shard_map/advect/pallas_call | solution.py:367
  21.4 3.1 %all-to-all-done.cell = s32[8,2,128]{2,1,0:T(2,128)S(1)} async-done(((s32[8,2,128]{2,1,0:T(2,128)}), s32[8,2,128]{2,1,0:T(2,128)S(1)}, u32[]{:S(2)}, u32[]{:S(2)}) %all-to-all-start) | async-done | bytes 8224 | tf_op jit(solution)/shard_map/all_to_all | solution.py:339
  24.5 0.7 gather.1
  25.3 22.5 %all_to_all.20.raw = f32[8,2,64,128]{3,2,1,0:T(8,128)S(1)} all-to-all(f32[8,2,64,128]{3,2,1,0:T(8,128)S(1)} %gather.1), channel_id=1, replica_groups=mesh['member'=8,'space'=64] {'member'}, dimensions={0} | all-to-all | bytes 1048576 | tf_op jit(solution)/shard_map/all_to_all | solution.py:339
  47.8 0.7 tiles.1.own
  48.5 2.1 %collective-permute-start.3 = (f32[2,520,128]{2,1,0:T(8,128)S(1)}, f32[2,520,128]{2,1,0:T(8,128)S(1)}, u32[]{:S(2)}, u32[]{:S(2)}) collective-permute-start(f32[2,520,128]{2,1,0:T(8,128)S(1)} %tiles.1.own), channel_id=1, source_target_pairs={{0,64},{128,192},{256,320},{384,448},{64,0},{192,128},{320,256},{4... | collective-permute-start | bytes 1597448 | tf_op jit(solution)/shard_map/ppermute | solution.py:335
  50.6 1.9 %collective-permute-start.2 = (f32[2,520,128]{2,1,0:T(8,128)S(1)}, f32[2,520,128]{2,1,0:T(8,128)S(1)}, u32[]{:S(2)}, u32[]{:S(2)}) collective-permute-start(f32[2,520,128]{2,1,0:T(8,128)S(1)} %tiles.1.own), channel_id=1, source_target_pairs={{64,128},{192,256},{320,384},{448,0},{128,64},{256,192},{384,320},... | collective-permute-start | bytes 1597448 | tf_op jit(solution)/shard_map/ppermute | solution.py:335
  52.5 6.0 %collective-permute-start.5 = (f32[2,520,128]{2,1,0:T(8,128)S(1)}, f32[2,520,128]{2,1,0:T(8,128)S(1)}, u32[]{:S(2)}, u32[]{:S(2)}) collective-permute-start(f32[2,520,128]{2,1,0:T(8,128)S(1)} %tiles.1.own), channel_id=1, source_target_pairs={{1,2},{3,4},{5,6},{7,8},{9,10},{11,12},{13,14},{15,16},{17,18},{19... | collective-permute-start | bytes 1597448 | tf_op jit(solution)/shard_map/ppermute | solution.py:335
  58.5 1.9 %collective-permute-start.4 = (f32[2,520,128]{2,1,0:T(8,128)S(1)}, f32[2,520,128]{2,1,0:T(8,128)}, u32[]{:S(2)}, u32[]{:S(2)}) collective-permute-start(f32[2,520,128]{2,1,0:T(8,128)S(1)} %tiles.1.own), channel_id=1, source_target_pairs={{0,1},{2,3},{4,5},{6,7},{8,9},{10,11},{12,13},{14,15},{16,17},{18,... | collective-permute-start | bytes 1597448 | tf_op jit(solution)/shard_map/ppermute | solution.py:335
  60.5 4.2 %all-to-all-start.2 = ((f32[8,4,64,128]{3,2,1,0:T(8,128)}), f32[8,4,64,128]{3,2,1,0:T(8,128)S(1)}, u32[]{:S(2)}, u32[]{:S(2)}) async-start(f32[8,4,64,128]{3,2,1,0:T(8,128)} %get-tuple-element.18), calls=%async_computation.2 | async-start | bytes 2097152 | tf_op jit(solution)/shard_map/all_to_all | solution.py:339
  64.8 2.5 %collective-permute-done.2.odd_z = f32[2,520,128]{2,1,0:T(8,128)S(1)} collective-permute-done((f32[2,520,128]{2,1,0:T(8,128)S(1)}, f32[2,520,128]{2,1,0:T(8,128)S(1)}, u32[]{:S(2)}, u32[]{:S(2)}) %collective-permute-start.2) | collective-permute-done | bytes 532512 | tf_op jit(solution)/shard_map/ppermute | solution.py:335
  67.3 3.9 %collective-permute-start.7 = (f32[4,520,128]{2,1,0:T(8,128)S(1)}, f32[4,520,128]{2,1,0:T(8,128)S(1)}, u32[]{:S(2)}, u32[]{:S(2)}) collective-permute-start(f32[4,520,128]{2,1,0:T(8,128)S(1)} %constant_dynamic-update-slice_fusion), channel_id=1, source_target_pairs={{1,2},{3,4},{5,6},{7,8},{9,10},{11,12},{13,14},{15,16},{17,18},{19... | collective-permute-start | bytes 3194888 | tf_op jit(solution)/shard_map/ppermute | solution.py:335
  71.1 1.9 %collective-permute-start.6 = (f32[4,520,128]{2,1,0:T(8,128)S(1)}, f32[4,520,128]{2,1,0:T(8,128)S(1)}, u32[]{:S(2)}, u32[]{:S(2)}) collective-permute-start(f32[4,520,128]{2,1,0:T(8,128)S(1)} %constant_dynamic-update-slice_fusion), channel_id=1, source_target_pairs={{0,1},{2,3},{4,5},{6,7},{8,9},{10,11},{12,13},{14,15},{16,17},{18,... | collective-permute-start | bytes 3194888 | tf_op jit(solution)/shard_map/ppermute | solution.py:335
  73.1 3.0 %near_gram.1 = (f32[264,256]{1,0:T(8,128)S(1)}, f32[264,256]{1,0:T(8,128)S(1)}, f32[256,256]{1,0:T(8,128)S(1)}) custom-call(s32[12]{0:T(128)S(1)} %bitcast.12, f32[2,520,128]{2,1,0:T(8,128)S(1)} %tiles.1.own, f32[2,520,128]{2,1,0:T(8,128)S(1)} %collective-permute-done.2.odd_z, f32[2,520,128]{2,1,0:T(8,128)S(1)} %collective-permute-done.3.even_z, ...), custom_call_target="tpu_custom_call" | custom-call | flops 16106127360 | bytes 6389760 | tf_op jit(solution)/shard_map/near_gram/pallas_call | solution.py:408
  76.1 10.8 %collective-permute-done.7.across = f32[4,520,128]{2,1,0:T(8,128)S(1)} collective-permute-done((f32[4,520,128]{2,1,0:T(8,128)S(1)}, f32[4,520,128]{2,1,0:T(8,128)S(1)}, u32[]{:S(2)}, u32[]{:S(2)}) %collective-permute-start.7) | collective-permute-done | bytes 1064992 | tf_op jit(solution)/shard_map/ppermute | solution.py:335
  86.9 11.6 %weights.1.weight = f32[512,512]{1,0:T(8,128)S(1)} custom-call(s32[12]{0:T(128)S(1)} %bitcast.13, f32[264,256]{1,0:T(8,128)S(1)} %get-tuple-element.15.near1, f32[264,256]{1,0:T(8,128)S(1)} %get-tuple-element.16.near2, f32[256,256]{1,0:T(8,128)S(1)} %get-tuple-element.17.near3, f32[4,520,128]{2,1,0:T(8,128)S(1)} %collective-permute-done.6.within, ...), custom_call_target="tpu_custom_call" | custom-call | flops 8053063680 | bytes 3145728 | tf_op jit(solution)/shard_map/weights/pallas_call | solution.py:420
  98.5 1.1 update.1
  99.6 31.5 %all_to_all.21.state = f32[8,4,64,128]{3,2,1,0:T(8,128)S(1)} all-to-all(f32[8,4,64,128]{3,2,1,0:T(8,128)S(1)} %update.1), channel_id=1, replica_groups=mesh['member'=8,'space'=64] {'member'}, dimensions={0} | all-to-all | bytes 2097152 | tf_op jit(solution)/shard_map/all_to_all | solution.py:339
  131.1 1.5 %output.1 = f32[64,4,1024]{2,1,0:T(4,128)} custom-call(f32[8,4,64,128]{3,2,1,0:T(8,128)S(1)} %all_to_all.21.state), custom_call_target="tpu_custom_call" | custom-call | tf_op jit(solution)/shard_map/output/pallas_call | solution.py:441
  (26 shorter events, 0.7 us)
Async XLA Ops:
  0.0 18.0 %copy-start.6 = (f32[64,4,1024]{2,1,0:T(4,128)S(1)}, f32[64,4,1024]{2,1,0:T(4,128)}, u32[]{:S(2)}) copy-start(f32[64,4,1024]{2,1,0:T(4,128)} %ensemble_far.1) | copy-start | bytes 3145732
  0.0 11.7 %copy-start.7 = (s32[1,1,1,2,128]{4,3,2,1,0:T(2,128)S(1)}, s32[1,1,1,2,128]{4,3,2,1,0:T(2,128)}, u32[]{:S(2)}) copy-start(s32[1,1,1,2,128]{4,3,2,1,0:T(2,128)} %param.11) | copy-start | bytes 3076
  2.5 16.1 %copy-start = (f32[4,1024]{1,0:T(4,128)S(1)}, f32[4,1024]{1,0:T(4,128)}, u32[]{:S(2)}) copy-start(f32[4,1024]{1,0:T(4,128)} %speed_row.1) | copy-start | bytes 49156
  2.5 16.1 %copy-start.1 = (f32[4,1024]{1,0:T(4,128)S(1)}, f32[4,1024]{1,0:T(4,128)}, u32[]{:S(2)}) copy-start(f32[4,1024]{1,0:T(4,128)} %speed_col.1) | copy-start | bytes 49156
  2.5 16.0 %collective-permute-start = (f32[17,8,1024]{2,1,0:T(8,128)}, f32[17,8,1024]{2,1,0:T(8,128)S(1)}, u32[]{:S(2)}, u32[]{:S(2)}) collective-permute-start(f32[17,8,1024]{2,1,0:T(8,128)} %get-tuple-element.12), channel_id=1, source_target_pairs={{1,2},{3,4},{5,6},{7,8},{9,10},{11,12},{13,14},{15,16},{17,18},{19... | collective-permute-start | bytes 1671176 | tf_op jit(solution)/shard_map/ppermute | solution.py:335
  9.8 8.8 %collective-permute-start.1 = (f32[17,8,1024]{2,1,0:T(8,128)}, f32[17,8,1024]{2,1,0:T(8,128)S(1)}, u32[]{:S(2)}, u32[]{:S(2)}) collective-permute-start(f32[17,8,1024]{2,1,0:T(8,128)} %get-tuple-element.13), channel_id=1, source_target_pairs={{0,1},{2,3},{4,5},{6,7},{8,9},{10,11},{12,13},{14,15},{16,17},{18,... | collective-permute-start | bytes 1671176 | tf_op jit(solution)/shard_map/ppermute | solution.py:335
  12.3 12.2 %all-to-all-start = ((s32[8,2,128]{2,1,0:T(2,128)}), s32[8,2,128]{2,1,0:T(2,128)S(1)}, u32[]{:S(2)}, u32[]{:S(2)}) async-start(s32[8,2,128]{2,1,0:T(2,128)} %broadcast_in_dim.8), calls=%async_computation | async-start | bytes 16384 | tf_op jit(solution)/shard_map/all_to_all | solution.py:339
  24.5 23.2 %copy-start.2 = (f32[1,1,1,2,128]{4,3,2,1,0:T(2,128)S(1)}, f32[1,1,1,2,128]{4,3,2,1,0:T(2,128)}, u32[]{:S(2)}) copy-start(f32[1,1,1,2,128]{4,3,2,1,0:T(2,128)} %param.12) | copy-start | bytes 3076
  24.5 23.2 %copy-start.3 = (f32[1,1,1,2,128]{4,3,2,1,0:T(2,128)S(1)}, f32[1,1,1,2,128]{4,3,2,1,0:T(2,128)}, u32[]{:S(2)}) copy-start(f32[1,1,1,2,128]{4,3,2,1,0:T(2,128)} %param.13) | copy-start | bytes 3076
  24.5 23.2 %copy-start.4 = (s32[1,1,1,2]{3,2,1,0:T(1,128)S(1)}, s32[1,1,1,2]{3,2,1,0:T(1,128)}, u32[]{:S(2)}) copy-start(s32[1,1,1,2]{3,2,1,0:T(1,128)} %param.14) | copy-start | bytes 28
  48.5 16.2 %collective-permute-start.3 = (f32[2,520,128]{2,1,0:T(8,128)S(1)}, f32[2,520,128]{2,1,0:T(8,128)S(1)}, u32[]{:S(2)}, u32[]{:S(2)}) collective-permute-start(f32[2,520,128]{2,1,0:T(8,128)S(1)} %tiles.1.own), channel_id=1, source_target_pairs={{0,64},{128,192},{256,320},{384,448},{64,0},{192,128},{320,256},{4... | collective-permute-start | bytes 1597448 | tf_op jit(solution)/shard_map/ppermute | solution.py:335
  50.6 16.6 %collective-permute-start.2 = (f32[2,520,128]{2,1,0:T(8,128)S(1)}, f32[2,520,128]{2,1,0:T(8,128)S(1)}, u32[]{:S(2)}, u32[]{:S(2)}) collective-permute-start(f32[2,520,128]{2,1,0:T(8,128)S(1)} %tiles.1.own), channel_id=1, source_target_pairs={{64,128},{192,256},{320,384},{448,0},{128,64},{256,192},{384,320},... | collective-permute-start | bytes 1597448 | tf_op jit(solution)/shard_map/ppermute | solution.py:335
  52.5 20.5 %collective-permute-start.5 = (f32[2,520,128]{2,1,0:T(8,128)S(1)}, f32[2,520,128]{2,1,0:T(8,128)S(1)}, u32[]{:S(2)}, u32[]{:S(2)}) collective-permute-start(f32[2,520,128]{2,1,0:T(8,128)S(1)} %tiles.1.own), channel_id=1, source_target_pairs={{1,2},{3,4},{5,6},{7,8},{9,10},{11,12},{13,14},{15,16},{17,18},{19... | collective-permute-start | bytes 1597448 | tf_op jit(solution)/shard_map/ppermute | solution.py:335
  58.5 14.5 %collective-permute-start.4 = (f32[2,520,128]{2,1,0:T(8,128)S(1)}, f32[2,520,128]{2,1,0:T(8,128)}, u32[]{:S(2)}, u32[]{:S(2)}) collective-permute-start(f32[2,520,128]{2,1,0:T(8,128)S(1)} %tiles.1.own), channel_id=1, source_target_pairs={{0,1},{2,3},{4,5},{6,7},{8,9},{10,11},{12,13},{14,15},{16,17},{18,... | collective-permute-start | bytes 1597448 | tf_op jit(solution)/shard_map/ppermute | solution.py:335
  60.5 38.1 %all-to-all-start.2 = ((f32[8,4,64,128]{3,2,1,0:T(8,128)}), f32[8,4,64,128]{3,2,1,0:T(8,128)S(1)}, u32[]{:S(2)}, u32[]{:S(2)}) async-start(f32[8,4,64,128]{3,2,1,0:T(8,128)} %get-tuple-element.18), calls=%async_computation.2 | async-start | bytes 2097152 | tf_op jit(solution)/shard_map/all_to_all | solution.py:339
  64.7 8.4 %copy-start.5 = (s32[1,1,1,12]{3,2,1,0:T(1,128)S(1)}, s32[1,1,1,12]{3,2,1,0:T(1,128)}, u32[]{:S(2)}) copy-start(s32[1,1,1,12]{3,2,1,0:T(1,128)} %param.15) | copy-start | bytes 148
  67.3 19.6 %collective-permute-start.7 = (f32[4,520,128]{2,1,0:T(8,128)S(1)}, f32[4,520,128]{2,1,0:T(8,128)S(1)}, u32[]{:S(2)}, u32[]{:S(2)}) collective-permute-start(f32[4,520,128]{2,1,0:T(8,128)S(1)} %constant_dynamic-update-slice_fusion), channel_id=1, source_target_pairs={{1,2},{3,4},{5,6},{7,8},{9,10},{11,12},{13,14},{15,16},{17,18},{19... | collective-permute-start | bytes 3194888 | tf_op jit(solution)/shard_map/ppermute | solution.py:335
  71.1 15.8 %collective-permute-start.6 = (f32[4,520,128]{2,1,0:T(8,128)S(1)}, f32[4,520,128]{2,1,0:T(8,128)S(1)}, u32[]{:S(2)}, u32[]{:S(2)}) collective-permute-start(f32[4,520,128]{2,1,0:T(8,128)S(1)} %constant_dynamic-update-slice_fusion), channel_id=1, source_target_pairs={{0,1},{2,3},{4,5},{6,7},{8,9},{10,11},{12,13},{14,15},{16,17},{18,... | collective-permute-start | bytes 3194888 | tf_op jit(solution)/shard_map/ppermute | solution.py:335

commit v6 on v5

--- a/solution.py
+++ b/solution.py
@@ -210,10 +210,10 @@
         return x, e, square_rho / (2.0 - square_rho)
 
     def quick(carry):
-        return (carry[2] > 1e-3) & (bound < 1000.0)
+        return (carry[2] > 2e-4) & (bound < 1000.0)
 
     def careful(carry):
-        return carry[2] > 1e-3
+        return carry[2] > 2e-4
 
     carry = lax.while_loop(quick, functools.partial(square, quick_pair), (x, e, rho))
     x = lax.while_loop(careful, functools.partial(square, full_pair), carry)[0]
@@ -256,20 +256,26 @@
     return product(top, z1, NT), product(top, z2, NT), product(z2, z2, NT)
 
 
-def near_kernel(per_patch, slots, own, odd_z, even_z, within, across, gram1, gram2, gram3, z):
+def near_kernel(per_patch, slots, own, odd_z, even_z, across, within, gram1, gram2, gram3, z):
     tiles = ((0, 0, own, 0), (0, -1, odd_z, 0), (0, 1, even_z, 0), (-1, 0, across, 0), (1, 0, within, 0))
     fill(z, slots, per_patch, tiles)
     gram1[...], gram2[...], gram3[...] = gram_blocks(z, 2 * gram3.shape[0])
 
 
-def weight_kernel(per_patch, slots, near1, near2, near3, within, across, out, z):
+def corner_kernel(per_patch, slots, near1, near2, near3, within, gram1, gram2, gram3, z):
+    fill(z, slots, per_patch, ((1, 1, within, 0), (1, -1, within, per_patch)))
+    more1, more2, more3 = gram_blocks(z, 2 * near3.shape[0])
+    gram1[...] = near1[...] + more1
+    gram2[...] = near2[...] + more2
+    gram3[...] = near3[...] + more3
+
+
+def weight_kernel(per_patch, slots, near1, near2, near3, across, out, z):
     half = near3.shape[0]
     total = 2 * half
     tiles = (
         (-1, 1, across, 0),
         (-1, -1, across, per_patch),
-        (1, 1, within, 0),
-        (1, -1, within, per_patch),
     )
     fill(z, slots, per_patch, tiles)
     gram1, gram2, gram3 = gram_blocks(z, total)
@@ -400,7 +406,8 @@
     odd_z = paired(tiles, "member", 1)
     both_z = jnp.concatenate([even_z, odd_z])
     state = swap(state)
-    within_c = paired(both_z, "space", 0)
+    late_z, across, within = lax.optimization_barrier((both_z, across, within))
+    within_c = paired(late_z, "space", 0)
     across_c = paired(both_z, "space", 1)
     slots = loc_slots[0, 0, 0]
     half = total // 2
@@ -416,19 +423,31 @@
             flops=240 * total * total * depth, bytes_accessed=12 * (total + SUB) * depth * 4, transcendentals=0
         ),
         name="near_gram",
-    )(slots, tiles, odd_z, even_z, within, across)
+    )(slots, tiles, odd_z, even_z, across, within)
+    near = pl.pallas_call(
+        functools.partial(corner_kernel, per_patch),
+        out_shape=(f32(half + SUB, half), f32(half + SUB, half), f32(half, half)),
+        in_specs=[SMEM] + [VMEM] * 4,
+        out_specs=(VMEM, VMEM, VMEM),
+        scratch_shapes=[pltpu.VMEM((total + SUB, 2 * depth), jnp.float32)],
+        compiler_params=PARAMS,
+        cost_estimate=pl.CostEstimate(
+            flops=6 * total * total * depth, bytes_accessed=12 * total * total, transcendentals=0
+        ),
+        name="corner_gram",
+    )(slots, *near, within_c)
     weight = pl.pallas_call(
         functools.partial(weight_kernel, per_patch),
         out_shape=f32(total, total),
-        in_specs=[SMEM] + [VMEM] * 5,
+        in_specs=[SMEM] + [VMEM] * 4,
         out_specs=VMEM,
-        scratch_shapes=[pltpu.VMEM((total + SUB, 4 * depth), jnp.float32)],
+        scratch_shapes=[pltpu.VMEM((total + SUB, 2 * depth), jnp.float32)],
         compiler_params=PARAMS,
         cost_estimate=pl.CostEstimate(
             flops=120 * total * total * depth, bytes_accessed=12 * total * total, transcendentals=0
         ),
         name="weights",
-    )(slots, *near, within_c, across_c)
+    )(slots, *near, across_c)
     state = pl.pallas_call(
         update_kernel,
         out_shape=f32(parts, rows, members, cols),

time: 133 us -> 133 us (level)
  waiting for transfers between devices: 16.4 us -> 14.8 us
    pallas_call x0 -> x1, Pallas kernels: none -> 1.53 us  [on_device(): pl.pallas_call(functools.partial(corner_kernel, per_patch), out_shape=(f3...]
    ppermute x8, waiting for transfers between devices: 13.3 us -> 11.8 us  [paired(): return lax.ppermute(x, axis, pairs + [(j, i) for i, j in pairs])]
  transfers between devices with their start and end apart: 10 -> 10, of which waited for: 3 -> 3; matrix products, arithmetic and copies ran while one was open for 1% -> 1% of each run, Pallas kernels for 13% -> 14%
where the time goes in v6:
time: 133 us; the launch traced here: 132 us
  blocking collectives  53.9 us (41%)
  starting transfers between devices  36.8 us (28%)
  Pallas kernels  24.8 us (19%)
  waiting for transfers between devices  14.8 us (11%)
    all_to_all x2, blocking collectives, swap(): return lax.all_to_all(x, 'member', split_axis=0, concat_axis=0, tiled=True)  53.9 us
    ppermute x8, starting transfers between devices, paired(): return lax.ppermute(x, axis, pairs + [(j, i) for i, j in pairs])  26.9 us
    ppermute x8, waiting for transfers between devices, paired(): return lax.ppermute(x, axis, pairs + [(j, i) for i, j in pairs])  11.8 us
    pallas_call x1, Pallas kernels, on_device(): pl.pallas_call(functools.partial(weight_kernel, per_patch), out_shape=f32...  11 us
    all_to_all x2, starting transfers between devices, swap(): return lax.all_to_all(x, 'member', split_axis=0, concat_axis=0, tiled=True)  9.86 us
    all_to_all x2, waiting for transfers between devices, swap(): return lax.all_to_all(x, 'member', split_axis=0, concat_axis=0, tiled=True)  3.09 us
    pallas_call x1, Pallas kernels, on_device(): pl.pallas_call(functools.partial(near_kernel, per_patch), out_shape=(f32(...  3 us
    pallas_call x1, Pallas kernels, on_device(): pl.pallas_call(advect_kernel, out_shape=(f32(parts, rows, members, cols),...  2.81 us
  transfers between devices with their start and end apart: 10, of which 3 were waited for; matrix products, arithmetic and copies ran while one was open for 1% of the time, Pallas kernels for 14%

profile of v6, /device:TPU:63, one launch (start us, length us, event | category | flops | bytes accessed | tf_op | source)
XLA Modules:
  0.0 132.2 jit_solution(15901487633627154084)
XLA Ops:
  0.0 2.5 %edges.1 = (f32[17,8,1024]{2,1,0:T(8,128)}, f32[17,8,1024]{2,1,0:T(8,128)}) custom-call(f32[64,4,1024]{2,1,0:T(4,128)} %ensemble_far.1, f32[4,1024]{1,0:T(4,128)} %speed_row.1, f32[4,1024]{1,0:T(4,128)} %speed_col.1), custom_call_target="tpu_custom_call" | custom-call | tf_op jit(solution)/shard_map/edges/pallas_call | solution.py:357
  2.5 7.2 %collective-permute-start = (f32[17,8,1024]{2,1,0:T(8,128)}, f32[17,8,1024]{2,1,0:T(8,128)S(1)}, u32[]{:S(2)}, u32[]{:S(2)}) collective-permute-start(f32[17,8,1024]{2,1,0:T(8,128)} %get-tuple-element.18), channel_id=1, source_target_pairs={{1,2},{3,4},{5,6},{7,8},{9,10},{11,12},{13,14},{15,16},{17,18},{19... | collective-permute-start | bytes 1671176 | tf_op jit(solution)/shard_map/ppermute | solution.py:341
  9.8 1.9 %collective-permute-start.1 = (f32[17,8,1024]{2,1,0:T(8,128)}, f32[17,8,1024]{2,1,0:T(8,128)S(1)}, u32[]{:S(2)}, u32[]{:S(2)}) collective-permute-start(f32[17,8,1024]{2,1,0:T(8,128)} %get-tuple-element.19), channel_id=1, source_target_pairs={{0,1},{2,3},{4,5},{6,7},{8,9},{10,11},{12,13},{14,15},{16,17},{18,... | collective-permute-start | bytes 1671176 | tf_op jit(solution)/shard_map/ppermute | solution.py:341
  12.3 5.6 %all-to-all-start = ((s32[8,2,128]{2,1,0:T(2,128)}), s32[8,2,128]{2,1,0:T(2,128)S(1)}, u32[]{:S(2)}, u32[]{:S(2)}) async-start(s32[8,2,128]{2,1,0:T(2,128)} %broadcast_in_dim.8), calls=%async_computation | async-start | bytes 16384 | tf_op jit(solution)/shard_map/all_to_all | solution.py:345
  18.6 2.8 %advect.1 = (f32[8,4,64,128]{3,2,1,0:T(8,128)S(1)}, f32[8,4,64,128]{3,2,1,0:T(8,128)}) custom-call(f32[4,64,1024]{2,1,0:T(8,128)S(1)} %bitcast.8, f32[17,8,1024]{2,1,0:T(8,128)S(1)} %collective-permute-done.across, f32[17,8,1024]{2,1,0:T(8,128)S(1)} %collective-permute-done.1.within, f32[4,1024]{1,0:T(4,128)S(1)} %copy-done, f32[4,1024]{1,0:T(4,128)S(1)} %copy-done.1), custom_call_target="tpu_custom_call" | custom-call | tf_op jit(solution)/shard_map/advect/pallas_call | solution.py:373
  21.4 3.1 %all-to-all-done.cell = s32[8,2,128]{2,1,0:T(2,128)S(1)} async-done(((s32[8,2,128]{2,1,0:T(2,128)}), s32[8,2,128]{2,1,0:T(2,128)S(1)}, u32[]{:S(2)}, u32[]{:S(2)}) %all-to-all-start) | async-done | bytes 8224 | tf_op jit(solution)/shard_map/all_to_all | solution.py:345
  24.5 0.7 gather.1
  25.3 22.5 %all_to_all.20.raw = f32[8,2,64,128]{3,2,1,0:T(8,128)S(1)} all-to-all(f32[8,2,64,128]{3,2,1,0:T(8,128)S(1)} %gather.1), channel_id=1, replica_groups=mesh['member'=8,'space'=64] {'member'}, dimensions={0} | all-to-all | bytes 1048576 | tf_op jit(solution)/shard_map/all_to_all | solution.py:345
  47.8 0.7 tiles.1.own
  48.4 2.2 %collective-permute-start.3 = (f32[2,520,128]{2,1,0:T(8,128)S(1)}, f32[2,520,128]{2,1,0:T(8,128)S(1)}, u32[]{:S(2)}, u32[]{:S(2)}) collective-permute-start(f32[2,520,128]{2,1,0:T(8,128)S(1)} %tiles.1.own), channel_id=1, source_target_pairs={{0,64},{128,192},{256,320},{384,448},{64,0},{192,128},{320,256},{4... | collective-permute-start | bytes 1597448 | tf_op jit(solution)/shard_map/ppermute | solution.py:341
  50.6 1.9 %collective-permute-start.2 = (f32[2,520,128]{2,1,0:T(8,128)S(1)}, f32[2,520,128]{2,1,0:T(8,128)S(1)}, u32[]{:S(2)}, u32[]{:S(2)}) collective-permute-start(f32[2,520,128]{2,1,0:T(8,128)S(1)} %tiles.1.own), channel_id=1, source_target_pairs={{64,128},{192,256},{320,384},{448,0},{128,64},{256,192},{384,320},... | collective-permute-start | bytes 1597448 | tf_op jit(solution)/shard_map/ppermute | solution.py:341
  52.5 6.0 %collective-permute-start.4 = (f32[2,520,128]{2,1,0:T(8,128)S(1)}, f32[2,520,128]{2,1,0:T(8,128)S(1)}, u32[]{:S(2)}, u32[]{:S(2)}) collective-permute-start(f32[2,520,128]{2,1,0:T(8,128)S(1)} %tiles.1.own), channel_id=1, source_target_pairs={{1,2},{3,4},{5,6},{7,8},{9,10},{11,12},{13,14},{15,16},{17,18},{19... | collective-permute-start | bytes 1597448 | tf_op jit(solution)/shard_map/ppermute | solution.py:341
  58.5 1.9 %collective-permute-start.5 = (f32[2,520,128]{2,1,0:T(8,128)S(1)}, f32[2,520,128]{2,1,0:T(8,128)}, u32[]{:S(2)}, u32[]{:S(2)}) collective-permute-start(f32[2,520,128]{2,1,0:T(8,128)S(1)} %tiles.1.own), channel_id=1, source_target_pairs={{0,1},{2,3},{4,5},{6,7},{8,9},{10,11},{12,13},{14,15},{16,17},{18,... | collective-permute-start | bytes 1597448 | tf_op jit(solution)/shard_map/ppermute | solution.py:341
  60.5 4.2 %all-to-all-start.2 = ((f32[8,4,64,128]{3,2,1,0:T(8,128)}), f32[8,4,64,128]{3,2,1,0:T(8,128)S(1)}, u32[]{:S(2)}, u32[]{:S(2)}) async-start(f32[8,4,64,128]{3,2,1,0:T(8,128)} %get-tuple-element.30), calls=%async_computation.2 | async-start | bytes 2097152 | tf_op jit(solution)/shard_map/all_to_all | solution.py:345
  64.8 2.5 %collective-permute-done.2.odd_z = f32[2,520,128]{2,1,0:T(8,128)S(1)} collective-permute-done((f32[2,520,128]{2,1,0:T(8,128)S(1)}, f32[2,520,128]{2,1,0:T(8,128)S(1)}, u32[]{:S(2)}, u32[]{:S(2)}) %collective-permute-start.2) | collective-permute-done | bytes 532512 | tf_op jit(solution)/shard_map/ppermute | solution.py:341
  67.3 3.8 %collective-permute-start.7 = (f32[4,520,128]{2,1,0:T(8,128)S(1)}, f32[4,520,128]{2,1,0:T(8,128)S(1)}, u32[]{:S(2)}, u32[]{:S(2)}) collective-permute-start(f32[4,520,128]{2,1,0:T(8,128)S(1)} %constant_dynamic-update-slice_fusion), channel_id=1, source_target_pairs={{1,2},{3,4},{5,6},{7,8},{9,10},{11,12},{13,14},{15,16},{17,18},{19... | collective-permute-start | bytes 3194888 | tf_op jit(solution)/shard_map/ppermute | solution.py:341
  71.2 1.9 %collective-permute-start.6 = (f32[4,520,128]{2,1,0:T(8,128)S(1)}, f32[4,520,128]{2,1,0:T(8,128)S(1)}, u32[]{:S(2)}, u32[]{:S(2)}) collective-permute-start(f32[4,520,128]{2,1,0:T(8,128)S(1)} %constant_dynamic-update-slice_fusion), channel_id=1, source_target_pairs={{0,1},{2,3},{4,5},{6,7},{8,9},{10,11},{12,13},{14,15},{16,17},{18,... | collective-permute-start | bytes 3194888 | tf_op jit(solution)/shard_map/ppermute | solution.py:341
  73.1 3.0 %near_gram.1 = (f32[264,256]{1,0:T(8,128)S(1)}, f32[264,256]{1,0:T(8,128)S(1)}, f32[256,256]{1,0:T(8,128)S(1)}) custom-call(s32[12]{0:T(128)S(1)} %bitcast.12, f32[2,520,128]{2,1,0:T(8,128)S(1)} %tiles.1.own, f32[2,520,128]{2,1,0:T(8,128)S(1)} %collective-permute-done.2.odd_z, f32[2,520,128]{2,1,0:T(8,128)S(1)} %collective-permute-done.3.even_z, ...), custom_call_target="tpu_custom_call" | custom-call | flops 16106127360 | bytes 6389760 | tf_op jit(solution)/shard_map/near_gram/pallas_call | solution.py:415
  76.1 1.5 %corner_gram.1 = (f32[264,256]{1,0:T(8,128)S(1)}, f32[264,256]{1,0:T(8,128)S(1)}, f32[256,256]{1,0:T(8,128)S(1)}) custom-call(s32[12]{0:T(128)S(1)} %bitcast.13, f32[264,256]{1,0:T(8,128)S(1)} %get-tuple-element.23.near1, f32[264,256]{1,0:T(8,128)S(1)} %get-tuple-element.24.near2, f32[256,256]{1,0:T(8,128)S(1)} %get-tuple-element.25.near3, ...), custom_call_target="tpu_custom_call" | custom-call | flops 402653184 | bytes 3145728 | tf_op jit(solution)/shard_map/corner_gram/pallas_call | solution.py:427
  77.6 9.3 %collective-permute-done.7.across = f32[4,520,128]{2,1,0:T(8,128)S(1)} collective-permute-done((f32[4,520,128]{2,1,0:T(8,128)S(1)}, f32[4,520,128]{2,1,0:T(8,128)S(1)}, u32[]{:S(2)}, u32[]{:S(2)}) %collective-permute-start.7) | collective-permute-done | bytes 1064992 | tf_op jit(solution)/shard_map/ppermute | solution.py:341
  86.9 11.0 %weights.1.weight = f32[512,512]{1,0:T(8,128)S(1)} custom-call(s32[12]{0:T(128)S(1)} %bitcast.14, f32[264,256]{1,0:T(8,128)S(1)} %get-tuple-element.27.near1, f32[264,256]{1,0:T(8,128)S(1)} %get-tuple-element.28.near2, f32[256,256]{1,0:T(8,128)S(1)} %get-tuple-element.29.near3, f32[4,520,128]{2,1,0:T(8,128)S(1)} %collective-permute-done.7.across), custom_call_target="tpu_custom_call" | custom-call | flops 8053063680 | bytes 3145728 | tf_op jit(solution)/shard_map/weights/pallas_call | solution.py:439
  97.9 1.1 update.1
  99.0 31.4 %all_to_all.21.state = f32[8,4,64,128]{3,2,1,0:T(8,128)S(1)} all-to-all(f32[8,4,64,128]{3,2,1,0:T(8,128)S(1)} %update.1), channel_id=1, replica_groups=mesh['member'=8,'space'=64] {'member'}, dimensions={0} | all-to-all | bytes 2097152 | tf_op jit(solution)/shard_map/all_to_all | solution.py:345
  130.5 1.5 %output.1 = f32[64,4,1024]{2,1,0:T(4,128)} custom-call(f32[8,4,64,128]{3,2,1,0:T(8,128)S(1)} %all_to_all.21.state), custom_call_target="tpu_custom_call" | custom-call | tf_op jit(solution)/shard_map/output/pallas_call | solution.py:460
  (27 shorter events, 1.3 us)
Async XLA Ops:
  0.0 18.0 %copy-start.6 = (f32[64,4,1024]{2,1,0:T(4,128)S(1)}, f32[64,4,1024]{2,1,0:T(4,128)}, u32[]{:S(2)}) copy-start(f32[64,4,1024]{2,1,0:T(4,128)} %ensemble_far.1) | copy-start | bytes 3145732
  0.0 11.7 %copy-start.7 = (s32[1,1,1,2,128]{4,3,2,1,0:T(2,128)S(1)}, s32[1,1,1,2,128]{4,3,2,1,0:T(2,128)}, u32[]{:S(2)}) copy-start(s32[1,1,1,2,128]{4,3,2,1,0:T(2,128)} %param.11) | copy-start | bytes 3076
  2.5 16.1 %copy-start = (f32[4,1024]{1,0:T(4,128)S(1)}, f32[4,1024]{1,0:T(4,128)}, u32[]{:S(2)}) copy-start(f32[4,1024]{1,0:T(4,128)} %speed_row.1) | copy-start | bytes 49156
  2.5 16.1 %copy-start.1 = (f32[4,1024]{1,0:T(4,128)S(1)}, f32[4,1024]{1,0:T(4,128)}, u32[]{:S(2)}) copy-start(f32[4,1024]{1,0:T(4,128)} %speed_col.1) | copy-start | bytes 49156
  2.5 16.0 %collective-permute-start = (f32[17,8,1024]{2,1,0:T(8,128)}, f32[17,8,1024]{2,1,0:T(8,128)S(1)}, u32[]{:S(2)}, u32[]{:S(2)}) collective-permute-start(f32[17,8,1024]{2,1,0:T(8,128)} %get-tuple-element.18), channel_id=1, source_target_pairs={{1,2},{3,4},{5,6},{7,8},{9,10},{11,12},{13,14},{15,16},{17,18},{19... | collective-permute-start | bytes 1671176 | tf_op jit(solution)/shard_map/ppermute | solution.py:341
  9.8 8.8 %collective-permute-start.1 = (f32[17,8,1024]{2,1,0:T(8,128)}, f32[17,8,1024]{2,1,0:T(8,128)S(1)}, u32[]{:S(2)}, u32[]{:S(2)}) collective-permute-start(f32[17,8,1024]{2,1,0:T(8,128)} %get-tuple-element.19), channel_id=1, source_target_pairs={{0,1},{2,3},{4,5},{6,7},{8,9},{10,11},{12,13},{14,15},{16,17},{18,... | collective-permute-start | bytes 1671176 | tf_op jit(solution)/shard_map/ppermute | solution.py:341
  12.3 12.2 %all-to-all-start = ((s32[8,2,128]{2,1,0:T(2,128)}), s32[8,2,128]{2,1,0:T(2,128)S(1)}, u32[]{:S(2)}, u32[]{:S(2)}) async-start(s32[8,2,128]{2,1,0:T(2,128)} %broadcast_in_dim.8), calls=%async_computation | async-start | bytes 16384 | tf_op jit(solution)/shard_map/all_to_all | solution.py:345
  24.5 23.2 %copy-start.2 = (f32[1,1,1,2,128]{4,3,2,1,0:T(2,128)S(1)}, f32[1,1,1,2,128]{4,3,2,1,0:T(2,128)}, u32[]{:S(2)}) copy-start(f32[1,1,1,2,128]{4,3,2,1,0:T(2,128)} %param.12) | copy-start | bytes 3076
  24.5 23.2 %copy-start.3 = (f32[1,1,1,2,128]{4,3,2,1,0:T(2,128)S(1)}, f32[1,1,1,2,128]{4,3,2,1,0:T(2,128)}, u32[]{:S(2)}) copy-start(f32[1,1,1,2,128]{4,3,2,1,0:T(2,128)} %param.13) | copy-start | bytes 3076
  24.5 23.2 %copy-start.4 = (s32[1,1,1,2]{3,2,1,0:T(1,128)S(1)}, s32[1,1,1,2]{3,2,1,0:T(1,128)}, u32[]{:S(2)}) copy-start(s32[1,1,1,2]{3,2,1,0:T(1,128)} %param.14) | copy-start | bytes 28
  48.4 16.3 %collective-permute-start.3 = (f32[2,520,128]{2,1,0:T(8,128)S(1)}, f32[2,520,128]{2,1,0:T(8,128)S(1)}, u32[]{:S(2)}, u32[]{:S(2)}) collective-permute-start(f32[2,520,128]{2,1,0:T(8,128)S(1)} %tiles.1.own), channel_id=1, source_target_pairs={{0,64},{128,192},{256,320},{384,448},{64,0},{192,128},{320,256},{4... | collective-permute-start | bytes 1597448 | tf_op jit(solution)/shard_map/ppermute | solution.py:341
  50.6 16.7 %collective-permute-start.2 = (f32[2,520,128]{2,1,0:T(8,128)S(1)}, f32[2,520,128]{2,1,0:T(8,128)S(1)}, u32[]{:S(2)}, u32[]{:S(2)}) collective-permute-start(f32[2,520,128]{2,1,0:T(8,128)S(1)} %tiles.1.own), channel_id=1, source_target_pairs={{64,128},{192,256},{320,384},{448,0},{128,64},{256,192},{384,320},... | collective-permute-start | bytes 1597448 | tf_op jit(solution)/shard_map/ppermute | solution.py:341
  52.5 18.6 %collective-permute-start.4 = (f32[2,520,128]{2,1,0:T(8,128)S(1)}, f32[2,520,128]{2,1,0:T(8,128)S(1)}, u32[]{:S(2)}, u32[]{:S(2)}) collective-permute-start(f32[2,520,128]{2,1,0:T(8,128)S(1)} %tiles.1.own), channel_id=1, source_target_pairs={{1,2},{3,4},{5,6},{7,8},{9,10},{11,12},{13,14},{15,16},{17,18},{19... | collective-permute-start | bytes 1597448 | tf_op jit(solution)/shard_map/ppermute | solution.py:341
  58.5 12.6 %collective-permute-start.5 = (f32[2,520,128]{2,1,0:T(8,128)S(1)}, f32[2,520,128]{2,1,0:T(8,128)}, u32[]{:S(2)}, u32[]{:S(2)}) collective-permute-start(f32[2,520,128]{2,1,0:T(8,128)S(1)} %tiles.1.own), channel_id=1, source_target_pairs={{0,1},{2,3},{4,5},{6,7},{8,9},{10,11},{12,13},{14,15},{16,17},{18,... | collective-permute-start | bytes 1597448 | tf_op jit(solution)/shard_map/ppermute | solution.py:341
  60.5 37.4 %all-to-all-start.2 = ((f32[8,4,64,128]{3,2,1,0:T(8,128)}), f32[8,4,64,128]{3,2,1,0:T(8,128)S(1)}, u32[]{:S(2)}, u32[]{:S(2)}) async-start(f32[8,4,64,128]{3,2,1,0:T(8,128)} %get-tuple-element.30), calls=%async_computation.2 | async-start | bytes 2097152 | tf_op jit(solution)/shard_map/all_to_all | solution.py:345
  64.7 8.4 %copy-start.5 = (s32[1,1,1,12]{3,2,1,0:T(1,128)S(1)}, s32[1,1,1,12]{3,2,1,0:T(1,128)}, u32[]{:S(2)}) copy-start(s32[1,1,1,12]{3,2,1,0:T(1,128)} %param.15) | copy-start | bytes 148
  67.3 19.6 %collective-permute-start.7 = (f32[4,520,128]{2,1,0:T(8,128)S(1)}, f32[4,520,128]{2,1,0:T(8,128)S(1)}, u32[]{:S(2)}, u32[]{:S(2)}) collective-permute-start(f32[4,520,128]{2,1,0:T(8,128)S(1)} %constant_dynamic-update-slice_fusion), channel_id=1, source_target_pairs={{1,2},{3,4},{5,6},{7,8},{9,10},{11,12},{13,14},{15,16},{17,18},{19... | collective-permute-start | bytes 3194888 | tf_op jit(solution)/shard_map/ppermute | solution.py:341
  71.2 4.9 %collective-permute-start.6 = (f32[4,520,128]{2,1,0:T(8,128)S(1)}, f32[4,520,128]{2,1,0:T(8,128)S(1)}, u32[]{:S(2)}, u32[]{:S(2)}) collective-permute-start(f32[4,520,128]{2,1,0:T(8,128)S(1)} %constant_dynamic-update-slice_fusion), channel_id=1, source_target_pairs={{0,1},{2,3},{4,5},{6,7},{8,9},{10,11},{12,13},{14,15},{16,17},{18,... | collective-permute-start | bytes 3194888 | tf_op jit(solution)/shard_map/ppermute | solution.py:341

commit v7 on v6

--- a/solution.py
+++ b/solution.py
@@ -52,7 +52,9 @@
     return lax.rem(lax.axis_index(axis), 2)
 
 
-def edge_kernel(ensemble_far, row_far, col_far, across, within, ensemble, speed_row, speed_col, done):
+def edge_kernel(
+    ensemble_far, row_far, col_far, cell_far, across, within, cells, ensemble, speed_row, speed_col, cell, done
+):
     members, rows, width = ensemble.shape
     groups = members // SUB
     odd = parity("space") == 1
@@ -66,6 +68,7 @@
 
     copies = [part(g) for g in range(groups)]
     copies += [fetch(row_far, speed_row, groups), fetch(col_far, speed_col, groups + 1)]
+    copies += [fetch(cell_far, cell, groups + 2)]
     for copy in copies:
         copy.start()
 
@@ -84,6 +87,9 @@
     for n, speed in enumerate((speed_row, speed_col)):
         copies[groups + n].wait()
         put((2 * groups, slice(n, n + 1)), speed[0:1], speed[rows - 1 : rows])
+    copies[groups + 2].wait()
+    for b in range(cells.shape[0]):
+        cells[b] = cell[...]
 
 
 def advect_kernel(planes, across, within, speed_row, speed_col, out, far, coef, done):
@@ -354,20 +360,26 @@
     total = parts * members
 
     planes = ensemble.transpose(1, 0, 2)
-    across, within = pl.pallas_call(
+    own_cell = obs_cell[0, 0, 0]
+    across, within, cells = pl.pallas_call(
         edge_kernel,
-        out_shape=(f32(2 * groups + 1, SUB, width), f32(2 * groups + 1, SUB, width)),
-        in_specs=[HBM] * 3,
-        out_specs=(VMEM, VMEM),
+        out_shape=(
+            f32(2 * groups + 1, SUB, width),
+            f32(2 * groups + 1, SUB, width),
+            jax.ShapeDtypeStruct((parts, per_patch, obs), jnp.int32),
+        ),
+        in_specs=[HBM] * 4,
+        out_specs=(VMEM, VMEM, VMEM),
         scratch_shapes=[
             pltpu.VMEM(ensemble.shape, jnp.float32),
             pltpu.VMEM(speed_row.shape, jnp.float32),
             pltpu.VMEM(speed_col.shape, jnp.float32),
-            pltpu.SemaphoreType.DMA((groups + 2,)),
+            pltpu.VMEM((per_patch, obs), jnp.int32),
+            pltpu.SemaphoreType.DMA((groups + 3,)),
         ],
         compiler_params=pltpu.CompilerParams(vmem_limit_bytes=62 * 1024 * 1024),
         name="edges",
-    )(ensemble, speed_row, speed_col)
+    )(ensemble, speed_row, speed_col, own_cell)
     across = paired(across, "space", 1)
     within = paired(within, "space", 0)
     fresh, state = pl.pallas_call(
@@ -382,7 +394,7 @@
         compiler_params=PARAMS,
         name="advect",
     )(planes, across, within, speed_row, speed_col)
-    cell = swap(jnp.broadcast_to(obs_cell[0, 0], (parts, per_patch, obs)))
+    cell = swap(cells)
     raw = pl.pallas_call(
         gather_kernel,
         out_shape=f32(parts, per_patch, members, obs),

time: 133 us -> 132 us (level)
  the two profiles are of different devices: /device:TPU:63 before, /device:TPU:31 now
where the time goes in v7:
time: 132 us
  blocking collectives  53.3 us (40%)
  starting transfers between devices  41.8 us (32%)
  Pallas kernels  24.8 us (19%)
  waiting for transfers between devices  10.7 us (8%)
    all_to_all x2, blocking collectives, swap(): return lax.all_to_all(x, 'member', split_axis=0, concat_axis=0, tiled=True)  53.3 us
    ppermute x8, starting transfers between devices, paired(): return lax.ppermute(x, axis, pairs + [(j, i) for i, j in pairs])  27.3 us
    all_to_all x2, starting transfers between devices, swap(): return lax.all_to_all(x, 'member', split_axis=0, concat_axis=0, tiled=True)  14.5 us
    pallas_call x1, Pallas kernels, on_device(): pl.pallas_call(functools.partial(weight_kernel, per_patch), out_shape=f32...  11 us
    ppermute x8, waiting for transfers between devices, paired(): return lax.ppermute(x, axis, pairs + [(j, i) for i, j in pairs])  7.62 us
    all_to_all x2, waiting for transfers between devices, swap(): return lax.all_to_all(x, 'member', split_axis=0, concat_axis=0, tiled=True)  3.09 us
    pallas_call x1, Pallas kernels, on_device(): pl.pallas_call(functools.partial(near_kernel, per_patch), out_shape=(f32(...  3 us
    pallas_call x1, Pallas kernels, on_device(): pl.pallas_call(advect_kernel, out_shape=(f32(parts, rows, members, cols),...  2.81 us
  transfers between devices with their start and end apart: 10, of which 2 were waited for; matrix products, arithmetic and copies ran while one was open for 1% of the time, Pallas kernels for 14%

profile of v7, /device:TPU:31, one launch (start us, length us, event | category | flops | bytes accessed | tf_op | source)
XLA Modules:
  0.0 131.8 jit_solution(7230979749149759284)
XLA Ops:
  0.0 2.5 %edges.1 = (f32[17,8,1024]{2,1,0:T(8,128)}, f32[17,8,1024]{2,1,0:T(8,128)}, s32[8,2,128]{2,1,0:T(2,128)}) custom-call(f32[64,4,1024]{2,1,0:T(4,128)} %ensemble_far.1, f32[4,1024]{1,0:T(4,128)} %speed_row.1, f32[4,1024]{1,0:T(4,128)} %speed_col.1, s32[2,128]{1,0:T(2,128)} %bitcast.15), custom_call_target="tpu_custom_call" | custom-call | tf_op jit(solution)/shard_map/edges/pallas_call | solution.py:364
  2.5 4.9 %collective-permute-start = (f32[17,8,1024]{2,1,0:T(8,128)}, f32[17,8,1024]{2,1,0:T(8,128)S(1)}, u32[]{:S(2)}, u32[]{:S(2)}) collective-permute-start(f32[17,8,1024]{2,1,0:T(8,128)} %get-tuple-element.19), channel_id=1, source_target_pairs={{1,2},{3,4},{5,6},{7,8},{9,10},{11,12},{13,14},{15,16},{17,18},{19... | collective-permute-start | bytes 1671176 | tf_op jit(solution)/shard_map/ppermute | solution.py:347
  7.4 1.9 %collective-permute-start.1 = (f32[17,8,1024]{2,1,0:T(8,128)}, f32[17,8,1024]{2,1,0:T(8,128)S(1)}, u32[]{:S(2)}, u32[]{:S(2)}) collective-permute-start(f32[17,8,1024]{2,1,0:T(8,128)} %get-tuple-element.20), channel_id=1, source_target_pairs={{0,1},{2,3},{4,5},{6,7},{8,9},{10,11},{12,13},{14,15},{16,17},{18,... | collective-permute-start | bytes 1671176 | tf_op jit(solution)/shard_map/ppermute | solution.py:347
  9.3 10.0 %all-to-all-start = ((s32[8,2,128]{2,1,0:T(2,128)}), s32[8,2,128]{2,1,0:T(2,128)S(1)}, u32[]{:S(2)}, u32[]{:S(2)}) async-start(s32[8,2,128]{2,1,0:T(2,128)} %get-tuple-element.22), calls=%async_computation | async-start | bytes 16384 | tf_op jit(solution)/shard_map/all_to_all | solution.py:351
  19.4 0.6 copy.11
  20.1 2.8 %advect.1 = (f32[8,4,64,128]{3,2,1,0:T(8,128)S(1)}, f32[8,4,64,128]{3,2,1,0:T(8,128)}) custom-call(f32[4,64,1024]{2,1,0:T(8,128)S(1)} %bitcast.8, f32[17,8,1024]{2,1,0:T(8,128)S(1)} %collective-permute-done.across, f32[17,8,1024]{2,1,0:T(8,128)S(1)} %collective-permute-done.1.within, f32[4,1024]{1,0:T(4,128)S(1)} %copy-done, f32[4,1024]{1,0:T(4,128)S(1)} %copy-done.1), custom_call_target="tpu_custom_call" | custom-call | tf_op jit(solution)/shard_map/advect/pallas_call | solution.py:385
  22.9 3.1 %all-to-all-done.cell = s32[8,2,128]{2,1,0:T(2,128)S(1)} async-done(((s32[8,2,128]{2,1,0:T(2,128)}), s32[8,2,128]{2,1,0:T(2,128)S(1)}, u32[]{:S(2)}, u32[]{:S(2)}) %all-to-all-start) | async-done | bytes 8224 | tf_op jit(solution)/shard_map/all_to_all | solution.py:351
  26.0 0.7 gather.1
  26.7 19.4 %all_to_all.20.raw = f32[8,2,64,128]{3,2,1,0:T(8,128)S(1)} all-to-all(f32[8,2,64,128]{3,2,1,0:T(8,128)S(1)} %gather.1), channel_id=1, replica_groups=mesh['member'=8,'space'=64] {'member'}, dimensions={0} | all-to-all | bytes 1048576 | tf_op jit(solution)/shard_map/all_to_all | solution.py:351
  46.1 0.7 tiles.1.own
  46.8 1.9 %collective-permute-start.3 = (f32[2,520,128]{2,1,0:T(8,128)S(1)}, f32[2,520,128]{2,1,0:T(8,128)S(1)}, u32[]{:S(2)}, u32[]{:S(2)}) collective-permute-start(f32[2,520,128]{2,1,0:T(8,128)S(1)} %tiles.1.own), channel_id=1, source_target_pairs={{0,64},{128,192},{256,320},{384,448},{64,0},{192,128},{320,256},{4... | collective-permute-start | bytes 1597448 | tf_op jit(solution)/shard_map/ppermute | solution.py:347
  48.7 3.8 %collective-permute-start.2 = (f32[2,520,128]{2,1,0:T(8,128)S(1)}, f32[2,520,128]{2,1,0:T(8,128)S(1)}, u32[]{:S(2)}, u32[]{:S(2)}) collective-permute-start(f32[2,520,128]{2,1,0:T(8,128)S(1)} %tiles.1.own), channel_id=1, source_target_pairs={{64,128},{192,256},{320,384},{448,0},{128,64},{256,192},{384,320},... | collective-permute-start | bytes 1597448 | tf_op jit(solution)/shard_map/ppermute | solution.py:347
  52.5 5.5 %collective-permute-start.4 = (f32[2,520,128]{2,1,0:T(8,128)S(1)}, f32[2,520,128]{2,1,0:T(8,128)S(1)}, u32[]{:S(2)}, u32[]{:S(2)}) collective-permute-start(f32[2,520,128]{2,1,0:T(8,128)S(1)} %tiles.1.own), channel_id=1, source_target_pairs={{1,2},{3,4},{5,6},{7,8},{9,10},{11,12},{13,14},{15,16},{17,18},{19... | collective-permute-start | bytes 1597448 | tf_op jit(solution)/shard_map/ppermute | solution.py:347
  58.0 1.9 %collective-permute-start.5 = (f32[2,520,128]{2,1,0:T(8,128)S(1)}, f32[2,520,128]{2,1,0:T(8,128)}, u32[]{:S(2)}, u32[]{:S(2)}) collective-permute-start(f32[2,520,128]{2,1,0:T(8,128)S(1)} %tiles.1.own), channel_id=1, source_target_pairs={{0,1},{2,3},{4,5},{6,7},{8,9},{10,11},{12,13},{14,15},{16,17},{18,... | collective-permute-start | bytes 1597448 | tf_op jit(solution)/shard_map/ppermute | solution.py:347
  59.9 4.4 %all-to-all-start.2 = ((f32[8,4,64,128]{3,2,1,0:T(8,128)}), f32[8,4,64,128]{3,2,1,0:T(8,128)S(1)}, u32[]{:S(2)}, u32[]{:S(2)}) async-start(f32[8,4,64,128]{3,2,1,0:T(8,128)} %get-tuple-element.32), calls=%async_computation.2 | async-start | bytes 2097152 | tf_op jit(solution)/shard_map/all_to_all | solution.py:351
  64.4 5.5 %collective-permute-start.7 = (f32[4,520,128]{2,1,0:T(8,128)S(1)}, f32[4,520,128]{2,1,0:T(8,128)S(1)}, u32[]{:S(2)}, u32[]{:S(2)}) collective-permute-start(f32[4,520,128]{2,1,0:T(8,128)S(1)} %constant_dynamic-update-slice_fusion), channel_id=1, source_target_pairs={{1,2},{3,4},{5,6},{7,8},{9,10},{11,12},{13,14},{15,16},{17,18},{19... | collective-permute-start | bytes 3194888 | tf_op jit(solution)/shard_map/ppermute | solution.py:347
  70.0 1.9 %collective-permute-start.6 = (f32[4,520,128]{2,1,0:T(8,128)S(1)}, f32[4,520,128]{2,1,0:T(8,128)S(1)}, u32[]{:S(2)}, u32[]{:S(2)}) collective-permute-start(f32[4,520,128]{2,1,0:T(8,128)S(1)} %constant_dynamic-update-slice_fusion), channel_id=1, source_target_pairs={{0,1},{2,3},{4,5},{6,7},{8,9},{10,11},{12,13},{14,15},{16,17},{18,... | collective-permute-start | bytes 3194888 | tf_op jit(solution)/shard_map/ppermute | solution.py:347
  71.9 3.0 %near_gram.1 = (f32[264,256]{1,0:T(8,128)S(1)}, f32[264,256]{1,0:T(8,128)S(1)}, f32[256,256]{1,0:T(8,128)S(1)}) custom-call(s32[12]{0:T(128)S(1)} %bitcast.12, f32[2,520,128]{2,1,0:T(8,128)S(1)} %tiles.1.own, f32[2,520,128]{2,1,0:T(8,128)S(1)} %collective-permute-done.2.odd_z, f32[2,520,128]{2,1,0:T(8,128)S(1)} %collective-permute-done.3.even_z, ...), custom_call_target="tpu_custom_call" | custom-call | flops 16106127360 | bytes 6389760 | tf_op jit(solution)/shard_map/near_gram/pallas_call | solution.py:427
  74.9 1.5 %corner_gram.1 = (f32[264,256]{1,0:T(8,128)S(1)}, f32[264,256]{1,0:T(8,128)S(1)}, f32[256,256]{1,0:T(8,128)S(1)}) custom-call(s32[12]{0:T(128)S(1)} %bitcast.13, f32[264,256]{1,0:T(8,128)S(1)} %get-tuple-element.25.near1, f32[264,256]{1,0:T(8,128)S(1)} %get-tuple-element.26.near2, f32[256,256]{1,0:T(8,128)S(1)} %get-tuple-element.27.near3, ...), custom_call_target="tpu_custom_call" | custom-call | flops 402653184 | bytes 3145728 | tf_op jit(solution)/shard_map/corner_gram/pallas_call | solution.py:439
  76.5 7.6 %collective-permute-done.7.across = f32[4,520,128]{2,1,0:T(8,128)S(1)} collective-permute-done((f32[4,520,128]{2,1,0:T(8,128)S(1)}, f32[4,520,128]{2,1,0:T(8,128)S(1)}, u32[]{:S(2)}, u32[]{:S(2)}) %collective-permute-start.7) | collective-permute-done | bytes 1064992 | tf_op jit(solution)/shard_map/ppermute | solution.py:347
  84.1 11.0 %weights.1.weight = f32[512,512]{1,0:T(8,128)S(1)} custom-call(s32[12]{0:T(128)S(1)} %bitcast.14, f32[264,256]{1,0:T(8,128)S(1)} %get-tuple-element.29.near1, f32[264,256]{1,0:T(8,128)S(1)} %get-tuple-element.30.near2, f32[256,256]{1,0:T(8,128)S(1)} %get-tuple-element.31.near3, f32[4,520,128]{2,1,0:T(8,128)S(1)} %collective-permute-done.7.across), custom_call_target="tpu_custom_call" | custom-call | flops 8053063680 | bytes 3145728 | tf_op jit(solution)/shard_map/weights/pallas_call | solution.py:451
  95.1 1.1 update.1
  96.2 33.9 %all_to_all.21.state = f32[8,4,64,128]{3,2,1,0:T(8,128)S(1)} all-to-all(f32[8,4,64,128]{3,2,1,0:T(8,128)S(1)} %update.1), channel_id=1, replica_groups=mesh['member'=8,'space'=64] {'member'}, dimensions={0} | all-to-all | bytes 2097152 | tf_op jit(solution)/shard_map/all_to_all | solution.py:351
  130.1 1.5 %output.1 = f32[64,4,1024]{2,1,0:T(4,128)} custom-call(f32[8,4,64,128]{3,2,1,0:T(8,128)S(1)} %all_to_all.21.state), custom_call_target="tpu_custom_call" | custom-call | tf_op jit(solution)/shard_map/output/pallas_call | solution.py:472
  (24 shorter events, 0.1 us)
Async XLA Ops:
  0.0 19.4 %copy-start.6 = (f32[64,4,1024]{2,1,0:T(4,128)S(1)}, f32[64,4,1024]{2,1,0:T(4,128)}, u32[]{:S(2)}) copy-start(f32[64,4,1024]{2,1,0:T(4,128)} %ensemble_far.1) | copy-start | bytes 3145732
  2.5 17.5 %copy-start = (f32[4,1024]{1,0:T(4,128)S(1)}, f32[4,1024]{1,0:T(4,128)}, u32[]{:S(2)}) copy-start(f32[4,1024]{1,0:T(4,128)} %speed_row.1) | copy-start | bytes 49156
  2.5 17.5 %copy-start.1 = (f32[4,1024]{1,0:T(4,128)S(1)}, f32[4,1024]{1,0:T(4,128)}, u32[]{:S(2)}) copy-start(f32[4,1024]{1,0:T(4,128)} %speed_col.1) | copy-start | bytes 49156
  2.5 17.5 %collective-permute-start = (f32[17,8,1024]{2,1,0:T(8,128)}, f32[17,8,1024]{2,1,0:T(8,128)S(1)}, u32[]{:S(2)}, u32[]{:S(2)}) collective-permute-start(f32[17,8,1024]{2,1,0:T(8,128)} %get-tuple-element.19), channel_id=1, source_target_pairs={{1,2},{3,4},{5,6},{7,8},{9,10},{11,12},{13,14},{15,16},{17,18},{19... | collective-permute-start | bytes 1671176 | tf_op jit(solution)/shard_map/ppermute | solution.py:347
  7.4 12.6 %collective-permute-start.1 = (f32[17,8,1024]{2,1,0:T(8,128)}, f32[17,8,1024]{2,1,0:T(8,128)S(1)}, u32[]{:S(2)}, u32[]{:S(2)}) collective-permute-start(f32[17,8,1024]{2,1,0:T(8,128)} %get-tuple-element.20), channel_id=1, source_target_pairs={{0,1},{2,3},{4,5},{6,7},{8,9},{10,11},{12,13},{14,15},{16,17},{18,... | collective-permute-start | bytes 1671176 | tf_op jit(solution)/shard_map/ppermute | solution.py:347
  9.3 16.6 %all-to-all-start = ((s32[8,2,128]{2,1,0:T(2,128)}), s32[8,2,128]{2,1,0:T(2,128)S(1)}, u32[]{:S(2)}, u32[]{:S(2)}) async-start(s32[8,2,128]{2,1,0:T(2,128)} %get-tuple-element.22), calls=%async_computation | async-start | bytes 16384 | tf_op jit(solution)/shard_map/all_to_all | solution.py:351
  26.0 20.1 %copy-start.2 = (f32[1,1,1,2,128]{4,3,2,1,0:T(2,128)S(1)}, f32[1,1,1,2,128]{4,3,2,1,0:T(2,128)}, u32[]{:S(2)}) copy-start(f32[1,1,1,2,128]{4,3,2,1,0:T(2,128)} %param.12) | copy-start | bytes 3076
  26.0 20.1 %copy-start.3 = (f32[1,1,1,2,128]{4,3,2,1,0:T(2,128)S(1)}, f32[1,1,1,2,128]{4,3,2,1,0:T(2,128)}, u32[]{:S(2)}) copy-start(f32[1,1,1,2,128]{4,3,2,1,0:T(2,128)} %param.13) | copy-start | bytes 3076
  26.0 20.1 %copy-start.4 = (s32[1,1,1,2]{3,2,1,0:T(1,128)S(1)}, s32[1,1,1,2]{3,2,1,0:T(1,128)}, u32[]{:S(2)}) copy-start(s32[1,1,1,2]{3,2,1,0:T(1,128)} %param.14) | copy-start | bytes 28
  46.8 17.5 %collective-permute-start.3 = (f32[2,520,128]{2,1,0:T(8,128)S(1)}, f32[2,520,128]{2,1,0:T(8,128)S(1)}, u32[]{:S(2)}, u32[]{:S(2)}) collective-permute-start(f32[2,520,128]{2,1,0:T(8,128)S(1)} %tiles.1.own), channel_id=1, source_target_pairs={{0,64},{128,192},{256,320},{384,448},{64,0},{192,128},{320,256},{4... | collective-permute-start | bytes 1597448 | tf_op jit(solution)/shard_map/ppermute | solution.py:347
  48.7 15.7 %collective-permute-start.2 = (f32[2,520,128]{2,1,0:T(8,128)S(1)}, f32[2,520,128]{2,1,0:T(8,128)S(1)}, u32[]{:S(2)}, u32[]{:S(2)}) collective-permute-start(f32[2,520,128]{2,1,0:T(8,128)S(1)} %tiles.1.own), channel_id=1, source_target_pairs={{64,128},{192,256},{320,384},{448,0},{128,64},{256,192},{384,320},... | collective-permute-start | bytes 1597448 | tf_op jit(solution)/shard_map/ppermute | solution.py:347
  52.5 17.4 %collective-permute-start.4 = (f32[2,520,128]{2,1,0:T(8,128)S(1)}, f32[2,520,128]{2,1,0:T(8,128)S(1)}, u32[]{:S(2)}, u32[]{:S(2)}) collective-permute-start(f32[2,520,128]{2,1,0:T(8,128)S(1)} %tiles.1.own), channel_id=1, source_target_pairs={{1,2},{3,4},{5,6},{7,8},{9,10},{11,12},{13,14},{15,16},{17,18},{19... | collective-permute-start | bytes 1597448 | tf_op jit(solution)/shard_map/ppermute | solution.py:347
  58.0 12.0 %collective-permute-start.5 = (f32[2,520,128]{2,1,0:T(8,128)S(1)}, f32[2,520,128]{2,1,0:T(8,128)}, u32[]{:S(2)}, u32[]{:S(2)}) collective-permute-start(f32[2,520,128]{2,1,0:T(8,128)S(1)} %tiles.1.own), channel_id=1, source_target_pairs={{0,1},{2,3},{4,5},{6,7},{8,9},{10,11},{12,13},{14,15},{16,17},{18,... | collective-permute-start | bytes 1597448 | tf_op jit(solution)/shard_map/ppermute | solution.py:347
  59.9 35.2 %all-to-all-start.2 = ((f32[8,4,64,128]{3,2,1,0:T(8,128)}), f32[8,4,64,128]{3,2,1,0:T(8,128)S(1)}, u32[]{:S(2)}, u32[]{:S(2)}) async-start(f32[8,4,64,128]{3,2,1,0:T(8,128)} %get-tuple-element.32), calls=%async_computation.2 | async-start | bytes 2097152 | tf_op jit(solution)/shard_map/all_to_all | solution.py:351
  64.3 7.6 %copy-start.5 = (s32[1,1,1,12]{3,2,1,0:T(1,128)S(1)}, s32[1,1,1,12]{3,2,1,0:T(1,128)}, u32[]{:S(2)}) copy-start(s32[1,1,1,12]{3,2,1,0:T(1,128)} %param.15) | copy-start | bytes 148
  64.4 19.6 %collective-permute-start.7 = (f32[4,520,128]{2,1,0:T(8,128)S(1)}, f32[4,520,128]{2,1,0:T(8,128)S(1)}, u32[]{:S(2)}, u32[]{:S(2)}) collective-permute-start(f32[4,520,128]{2,1,0:T(8,128)S(1)} %constant_dynamic-update-slice_fusion), channel_id=1, source_target_pairs={{1,2},{3,4},{5,6},{7,8},{9,10},{11,12},{13,14},{15,16},{17,18},{19... | collective-permute-start | bytes 3194888 | tf_op jit(solution)/shard_map/ppermute | solution.py:347
  70.0 5.0 %collective-permute-start.6 = (f32[4,520,128]{2,1,0:T(8,128)S(1)}, f32[4,520,128]{2,1,0:T(8,128)S(1)}, u32[]{:S(2)}, u32[]{:S(2)}) collective-permute-start(f32[4,520,128]{2,1,0:T(8,128)S(1)} %constant_dynamic-update-slice_fusion), channel_id=1, source_target_pairs={{0,1},{2,3},{4,5},{6,7},{8,9},{10,11},{12,13},{14,15},{16,17},{18,... | collective-permute-start | bytes 3194888 | tf_op jit(solution)/shard_map/ppermute | solution.py:347
